TPU v7x, 32 devices: a whole 2x2x4 slice. The times are simulated.
32 devices in a mesh: dp: 4 (over y, x), seq: 8 (over z, core).
Axes of the slice: x: 2, y: 2, z: 4, core: 2. Of those that a mesh axis runs over, the one named last changes fastest.
Arguments:
- queries: bfloat16 [4, 1024, 4096], P('dp', 'seq'), may hold values from -6 to 6
- keys: bfloat16 [4, 1024, 512], P('dp', 'seq'), may hold values from -6 to 6
- values: bfloat16 [4, 1024, 512], P('dp', 'seq'), may hold values from -6 to 6
- grad_out: bfloat16 [4, 1024, 4096], P('dp', 'seq'), may hold values from -15 to 15
- layer_input: bfloat16 [4, 1024, 4096], P('dp', 'seq'), may hold values from -6 to 6
- basis_store: bfloat16 [4, 1024, 256], P('dp'), may hold values from -0.1875 to 0.1875
- owner: int32 [8], replicated, may hold values from 0 to 3
- layout: int32 [32, 8, 4], replicated, may hold values from -1 to 7, as said below
Outputs:
- grad_query: bfloat16 [4, 1024, 4096], P('dp', 'seq')
- lowrank_grad: float32 [4096, 256], P('seq')
Inputs may be any that keep to these rules, and one draw needn't show every extreme that they name: layout[h, i] lists, in rising order, distinct key blocks from 0 to i, among them i itself, and then -1 in its unused slots; some list fills all 4 slots.
All inputs are finite; a program needn't handle non-finite values.
Results may differ from a plain program's by a relative error of at most 0.0088.
Values may be sent and summed in bfloat16 or wider, within the bound.
No kernel may reach another device: no remote copies, remote signals or barrier semaphores. Data moves between devices by JAX's collectives and lax.ppermute only.
A program may use at most 64 MiB of HBM per device.

v0:
```python
from functools import partial

import jax
import jax.numpy as jnp
from jax import lax
from jax.sharding import PartitionSpec as P

HEADS = 32
KV_HEADS = 4
HEAD_DIM = 128
BLOCK = 128


masked_score = -1e30


def spread_2(x, axis, root):
    mine = lax.axis_index(axis) == root
    return lax.psum(jnp.where(mine, x, jnp.zeros_like(x)), axis)


def causal_pattern(width):
    rows = lax.broadcasted_iota(jnp.int32, (width, width), 0)
    columns = lax.broadcasted_iota(jnp.int32, (width, width), 1)
    return columns <= rows


def padded_block(carry, inputs, lists, key_blocks, value_blocks, scale):
    key_grad, value_grad = carry
    query_block, query_rows, grad_rows = inputs
    width = query_rows.shape[0]
    head_dim = query_rows.shape[2]
    listed = lax.dynamic_index_in_dim(lists, query_block, 1, keepdims=False)
    valid = listed >= 0
    safe = jnp.maximum(listed, 0)
    key_sel = jnp.take(key_blocks, safe, axis=0)
    value_sel = jnp.take(value_blocks, safe, axis=0)
    scores = (
        jnp.einsum("qhd,hskd->hqsk", query_rows, key_sel, preferred_element_type=jnp.float32)
        * scale
    )
    earlier = (safe < query_block)[:, None, :, None]
    same = (safe == query_block)[:, None, :, None]
    visible = valid[:, None, :, None] & (earlier | same & causal_pattern(width)[None, :, None, :])
    scores = jnp.where(visible, scores, masked_score)
    top = jnp.max(scores, axis=(2, 3), keepdims=True)
    raw = jnp.exp(scores - top)
    weights = raw / jnp.sum(raw, axis=(2, 3), keepdims=True)
    weights_low = weights.astype(jnp.bfloat16)
    attended = jnp.einsum(
        "hqsk,hskd->qhd", weights_low, value_sel, preferred_element_type=jnp.float32
    )
    delta = jnp.sum(grad_rows.astype(jnp.float32) * attended, axis=2)
    dweights = jnp.einsum(
        "qhd,hskd->hqsk", grad_rows, value_sel, preferred_element_type=jnp.float32
    )
    dscores_low = (weights * (dweights - jnp.transpose(delta)[:, :, None, None])).astype(
        jnp.bfloat16
    )
    query_grad = (
        jnp.einsum("hqsk,hskd->qhd", dscores_low, key_sel, preferred_element_type=jnp.float32)
        * scale
    ).astype(jnp.bfloat16)
    key_terms = (
        jnp.einsum("hqsk,qhd->hskd", dscores_low, query_rows, preferred_element_type=jnp.float32)
        * scale
    )
    value_terms = jnp.einsum(
        "hqsk,qhd->hskd", weights_low, grad_rows, preferred_element_type=jnp.float32
    )
    flat_blocks = safe.reshape(-1)
    key_grad = key_grad.at[flat_blocks].add(key_terms.reshape(-1, width, head_dim))
    value_grad = value_grad.at[flat_blocks].add(value_terms.reshape(-1, width, head_dim))
    return ((key_grad, value_grad), query_grad)


def local(queries, keys, values, grad_out, layer_input, basis_store, owner, layout):
    seq_count = lax.axis_size("seq")
    seq_place = lax.axis_index("seq")
    tok_rows = queries.shape[1]
    seq_len = tok_rows * seq_count
    head_dev = HEADS // seq_count
    blocks = seq_len // BLOCK
    scale = HEAD_DIM ** (-0.5)
    query_heads, grad_heads = (
        lax.all_to_all(queries, "seq", split_axis=2, concat_axis=1, tiled=True),
        lax.all_to_all(grad_out, "seq", split_axis=2, concat_axis=1, tiled=True),
    )
    spread = (1, tok_rows, KV_HEADS, seq_count // KV_HEADS, HEAD_DIM)
    key_copies = jnp.broadcast_to(keys.reshape(1, tok_rows, KV_HEADS, 1, HEAD_DIM), spread).reshape(
        1, tok_rows, seq_count, HEAD_DIM
    )
    value_copies = jnp.broadcast_to(
        values.reshape(1, tok_rows, KV_HEADS, 1, HEAD_DIM), spread
    ).reshape(1, tok_rows, seq_count, HEAD_DIM)
    key_heads, value_heads = (
        lax.all_to_all(key_copies, "seq", split_axis=2, concat_axis=1, tiled=True),
        lax.all_to_all(value_copies, "seq", split_axis=2, concat_axis=1, tiled=True),
    )
    key_blocks = key_heads.reshape(blocks, BLOCK, HEAD_DIM)
    value_blocks = value_heads.reshape(blocks, BLOCK, HEAD_DIM)
    lists = lax.dynamic_slice_in_dim(layout, seq_place * head_dev, head_dev, 0)
    query_blocks = query_heads.reshape(blocks, BLOCK, head_dev, HEAD_DIM)
    grad_blocks = grad_heads.reshape(blocks, BLOCK, head_dev, HEAD_DIM)
    block_step = partial(
        padded_block, lists=lists, key_blocks=key_blocks, value_blocks=value_blocks, scale=scale
    )
    zeros_grad = jnp.zeros((blocks, BLOCK, HEAD_DIM), jnp.float32)
    block_ids = jnp.arange(blocks, dtype=jnp.int32)
    (key_grad, value_grad), query_grad = lax.scan(
        block_step, (zeros_grad, zeros_grad), (block_ids, query_blocks, grad_blocks)
    )
    query_back = query_grad.reshape(1, seq_len, head_dev * HEAD_DIM)
    key_back = key_grad.astype(jnp.bfloat16).reshape(1, seq_len, HEAD_DIM)
    value_back = value_grad.astype(jnp.bfloat16).reshape(1, seq_len, HEAD_DIM)
    grad_query, key_received, value_received = (
        lax.all_to_all(query_back, "seq", split_axis=1, concat_axis=2, tiled=True),
        lax.all_to_all(key_back, "seq", split_axis=1, concat_axis=2, tiled=True),
        lax.all_to_all(value_back, "seq", split_axis=1, concat_axis=2, tiled=True),
    )
    fold_shape = (tok_rows, KV_HEADS, seq_count // KV_HEADS, HEAD_DIM)
    key_sum = jnp.sum(key_received.reshape(fold_shape).astype(jnp.float32), axis=2).reshape(
        tok_rows, KV_HEADS * HEAD_DIM
    )
    value_sum = jnp.sum(value_received.reshape(fold_shape).astype(jnp.float32), axis=2).reshape(
        tok_rows, KV_HEADS * HEAD_DIM
    )
    kv_grad = jnp.concatenate([key_sum, value_sum], axis=1).astype(jnp.bfloat16)
    basis_pieces = []
    for index in range(2 * KV_HEADS):
        local_rows = basis_store[:, index * HEAD_DIM : (index + 1) * HEAD_DIM, :]
        basis_pieces.append(spread_2(local_rows, "dp", owner[index])[0])
    basis = jnp.concatenate(basis_pieces, axis=0)
    projected = jnp.dot(kv_grad, basis, preferred_element_type=jnp.float32).astype(jnp.bfloat16)
    contract_first = (((0,), (0,)), ((), ()))
    inputs_local = layer_input[0]
    partial_rank = lax.psum_scatter(
        lax.dot_general(
            inputs_local, projected, contract_first, preferred_element_type=jnp.float32
        ),
        "seq",
        scatter_dimension=0,
        tiled=True,
    )
    lowrank_grad = lax.psum(partial_rank, "dp") / lax.axis_size("dp")
    return (grad_query, lowrank_grad)


def solution(mesh):
    in_specs = (
        P("dp", "seq", None),
        P("dp", "seq", None),
        P("dp", "seq", None),
        P("dp", "seq", None),
        P("dp", "seq", None),
        P("dp", None, None),
        P(),
        P(),
    )
    out_specs = (P("dp", "seq", None), P("seq", None))
    return jax.shard_map(local, mesh=mesh, in_specs=in_specs, out_specs=out_specs, check_vma=False)
```

profile of v0, /device:TPU:0, one launch (start us, length us, event | category | flops | bytes accessed | tf_op | source)
XLA Modules:
  0.0 518.2 jit_solution(13442966426174149677)
XLA Ops:
  9.0 6.3 %all-to-all-start.1 = ((bf16[1,128,8,128]{3,1,0,2:T(8,128)(2,1)}), bf16[1,128,8,128]{3,1,0,2:T(8,128)(2,1)S(1)}, u32[]{:S(2)}, u32[]{:S(2)}) async-start(bf16[1,128,8,128]{3,1,0,2:T(8,128)(2,1)} %bitcast.23), calls=%async_computation.1 | async-start | bytes 524288 | tf_op jit(solution)/shard_map/all_to_all | solution.py:97
  15.3 5.0 copy.89
  20.9 23.4 %reduce.2 = bf16[4096,128]{1,0:T(8,128)(2,1)} reduce(bf16[4096,1,128]{2,1,0:T(2,128)(2,1)S(1)} %bitcast.199, bf16[]{:T(256)} %broadcast.122), dimensions={1}, to_apply=%bitcast.127.reduce_sub_computation | reduce | bytes 2097154
  46.4 5.1 all-to-all-start
  51.5 5.0 copy.91
  56.6 23.4 %reduce.3 = bf16[4096,128]{1,0:T(8,128)(2,1)} reduce(bf16[4096,1,128]{2,1,0:T(2,128)(2,1)S(1)} %bitcast.201, bf16[]{:T(256)} %broadcast.122), dimensions={1}, to_apply=%bitcast.129.reduce_sub_computation | reduce | bytes 2097154
  82.2 5.2 %all-to-all-start.2 = ((bf16[8,2,32768]{2,1,0:T(2,128)(2,1)}), bf16[8,2,32768]{2,1,0:T(2,128)(2,1)S(1)}, u32[]{:S(2)}, u32[]{:S(2)}) async-start(bf16[8,2,32768]{2,1,0:T(2,128)(2,1)} %reshape.181), calls=%async_computation.2 | async-start | bytes 2097152 | tf_op jit(solution)/shard_map/all_to_all | solution.py:87
  87.5 26.5 %all-to-all-done.2 = bf16[8,2,32768]{2,1,0:T(2,128)(2,1)S(1)} async-done(((bf16[8,2,32768]{2,1,0:T(2,128)(2,1)}), bf16[8,2,32768]{2,1,0:T(2,128)(2,1)S(1)}, u32[]{:S(2)}, u32[]{:S(2)}) %all-to-all-start.2) | async-done | bytes 1048608 | tf_op jit(solution)/shard_map/all_to_all | solution.py:87
  114.7 3.4 all-to-all-start.3
  125.6 5.8 %reshape.180 = bf16[4096,1,128]{2,1,0:T(2,128)(2,1)} reshape(bf16[8,2,32768]{2,1,0:T(2,128)(2,1)} %all-to-all-done) | data formatting | bytes 2097152
  131.4 2.8 copy.120
  134.2 3.5 reshape.182
  137.6 2.7 copy.121
  141.1 215.9 %while.14 = (s32[]{:T(128)}, f32[8,128,128]{2,1,0:T(8,128)S(1)}, f32[8,128,128]{2,1,0:T(8,128)S(1)}, bf16[8,128,4,128]{3,2,1,0:T(4,128)(2,1)}, s32[8]{0:T(128)},...) while((s32[]{:T(128)}, f32[8,128,128]{2,1,0:T(8,128)S(1)}, ...), condition=%wide.region_6.8_spmd, body=%wide.region_0.7_spmd.sunk | while | flops 409026304 | bytes 26009176 | solution.py:110
  150.4 2.4 gather_fusion.1
  177.4 2.4 gather_fusion.1
  204.3 2.4 gather_fusion.1
  231.3 2.4 gather_fusion.1
  258.3 2.4 gather_fusion.1
  339.2 2.4 gather_fusion.1
  360.4 4.8 all-to-all-start.6
  371.3 3.6 all-to-all-done.6
  375.0 3.4 all-to-all-start.5
  379.3 8.7 %all-to-all-done.5 = bf16[8,2,8192]{2,1,0:T(2,128)(2,1)S(1)} async-done(((bf16[8,2,8192]{2,1,0:T(2,128)(2,1)}), bf16[8,2,8192]{2,1,0:T(2,128)(2,1)S(1)}, u32[]{:S(2)}, u32[]{:S(2)}) %all-to-all-start.5) | async-done | bytes 262176 | tf_op jit(solution)/shard_map/all_to_all | solution.py:118
  388.5 3.0 convolution_bitcast_fusion.2
  391.6 5.9 %reshape.178 = bf16[1,1024,512]{2,0,1:T(2,128)(2,1)S(1)} reshape(bf16[8,128,4,128]{3,2,1,0:T(4,128)(2,1)} %get-tuple-element.57) | data formatting | bytes 2097152 | tf_op jit(solution)/shard_map/reshape | solution.py:113
  397.5 8.0 %reduce.4 = bf16[1024,512]{1,0:T(8,128)(2,1)} reduce(bf16[1024,1,512]{2,1,0:T(2,128)(2,1)S(1)} %bitcast.200, bf16[]{:T(256)} %broadcast.122), dimensions={1}, to_apply=%bitcast.131.reduce_sub_computation | reduce | bytes 2097154
  405.5 2.6 reshape.183
  408.1 4.2 all-to-all-start.4
  412.4 44.9 %reduce-scatter.2.cloned.1.call-done = f32[512,256]{0,1:T(8,128)} async-done(((f32[4096,256]{0,1:T(8,128)}), f32[512,256]{0,1:T(8,128)}) %reduce-scatter.2.cloned.1.call-update) | async-done | bytes 524304 | tf_op jit(solution)/shard_map/reduce_scatter | solution.py:137
  457.3 4.3 reshape.184
  465.8 43.8 %all-reduce.4.cloned.1.call-done = f32[512,256]{0,1:T(8,128)} async-done(((f32[512,256]{0,1:T(8,128)}), f32[512,256]{0,1:T(8,128)}) %all-reduce.4.cloned.1.call-update) | async-done | bytes 524304 | tf_op jit(solution)/shard_map/psum | solution.py:145
  (320 shorter events, 213.6 us)
Async XLA Ops:
  7.2 381.4 %copy-start = (bf16[1,128,4096]{2,1,0:T(8,128)(2,1)S(1)}, bf16[1,128,4096]{2,1,0:T(8,128)(2,1)}, u32[]{:S(2)}) copy-start(bf16[1,128,4096]{2,1,0:T(8,128)(2,1)} %param.16) | copy-start | bytes 3145732
  9.0 37.5 %all-to-all-start.1 = ((bf16[1,128,8,128]{3,1,0,2:T(8,128)(2,1)}), bf16[1,128,8,128]{3,1,0,2:T(8,128)(2,1)S(1)}, u32[]{:S(2)}, u32[]{:S(2)}) async-start(bf16[1,128,8,128]{3,1,0,2:T(8,128)(2,1)} %bitcast.23), calls=%async_computation.1 | async-start | bytes 524288 | tf_op jit(solution)/shard_map/all_to_all | solution.py:97
  46.4 35.7 %all-to-all-start = ((bf16[8,2,32768]{2,1,0:T(2,128)(2,1)}), bf16[8,2,32768]{2,1,0:T(2,128)(2,1)}, u32[]{:S(2)}, u32[]{:S(2)}) async-start(bf16[8,2,32768]{2,1,0:T(2,128)(2,1)} %reshape.179), calls=%async_computation | async-start | bytes 2097152 | tf_op jit(solution)/shard_map/all_to_all | solution.py:86
  79.9 7.5 %copy-start.4 = (bf16[1,128,512]{2,1,0:T(8,128)(2,1)S(1)}, bf16[1,128,512]{2,1,0:T(8,128)(2,1)}, u32[]{:S(2)}) copy-start(bf16[1,128,512]{2,1,0:T(8,128)(2,1)} %param.14) | copy-start | bytes 393220
  82.1 36.2 %copy-start.10 = (s32[8]{0:T(128)S(1)}, s32[8]{0:T(128)}, u32[]{:S(2)}) copy-start(s32[8]{0:T(128)} %param.18) | copy-start | bytes 100
  82.1 41.9 %copy-start.3 = (bf16[1,1024,256]{2,1,0:T(8,128)(2,1)S(1)}, bf16[1,1024,256]{2,1,0:T(8,128)(2,1)}, u32[]{:S(2)}) copy-start(bf16[1,1024,256]{2,1,0:T(8,128)(2,1)} %param.17) | copy-start | bytes 1572868
  82.1 42.8 %copy-start.11 = (s32[32,8,4]{0,2,1:T(4,128)S(1)}, s32[32,8,4]{0,2,1:T(4,128)}, u32[]{:S(2)}) copy-start(s32[32,8,4]{0,2,1:T(4,128)} %param.19) | copy-start | bytes 12292
  82.2 31.8 %all-to-all-start.2 = ((bf16[8,2,32768]{2,1,0:T(2,128)(2,1)}), bf16[8,2,32768]{2,1,0:T(2,128)(2,1)S(1)}, u32[]{:S(2)}, u32[]{:S(2)}) async-start(bf16[8,2,32768]{2,1,0:T(2,128)(2,1)} %reshape.181), calls=%async_computation.2 | async-start | bytes 2097152 | tf_op jit(solution)/shard_map/all_to_all | solution.py:87
  114.7 25.6 %all-to-all-start.3 = ((bf16[1,128,8,128]{3,1,0,2:T(8,128)(2,1)}), bf16[1,128,8,128]{3,1,0,2:T(8,128)(2,1)S(1)}, u32[]{:S(2)}, u32[]{:S(2)}) async-start(bf16[1,128,8,128]{3,1,0,2:T(8,128)(2,1)} %bitcast.29), calls=%async_computation.3 | async-start | bytes 524288 | tf_op jit(solution)/shard_map/all_to_all | solution.py:98
  118.1 247.1 %all-reduce.6.cloned.1.call-start = ((), (), s32[]{:S(2)}) async-start(), calls=%async_computation.10 | async-start | bytes 1048576 | tf_op jit(solution)/shard_map/psum | solution.py:19
  140.3 0.7 copy-start.1
  159.8 1.4 copy-start.2
  186.8 1.4 copy-start.2
  213.7 1.4 copy-start.2
  240.7 1.4 copy-start.2
  267.7 1.4 copy-start.2
  294.6 1.4 copy-start.2
  321.6 1.4 copy-start.2
  348.6 1.4 copy-start.2
  360.4 14.5 %all-to-all-start.6 = ((bf16[8,2,8192]{2,1,0:T(2,128)(2,1)}), bf16[8,2,8192]{2,1,0:T(2,128)(2,1)S(1)}, u32[]{:S(2)}, u32[]{:S(2)}) async-start(bf16[8,2,8192]{2,1,0:T(2,128)(2,1)} %reshape.185), calls=%async_computation.6 | async-start | bytes 524288 | tf_op jit(solution)/shard_map/all_to_all | solution.py:119
  365.2 13.4 %copy-start.9 = (bf16[128,256]{1,0:T(8,128)(2,1)S(1)}, bf16[128,256]{1,0:T(8,128)(2,1)}, u32[]{:S(2)}) copy-start(bf16[128,256]{1,0:T(8,128)(2,1)} %get-tuple-element.133) | copy-start | bytes 196612
  365.2 13.4 %copy-start.8 = (bf16[128,256]{1,0:T(8,128)(2,1)S(1)}, bf16[128,256]{1,0:T(8,128)(2,1)}, u32[]{:S(2)}) copy-start(bf16[128,256]{1,0:T(8,128)(2,1)} %get-tuple-element.134) | copy-start | bytes 196612
  365.2 13.4 %copy-start.7 = (bf16[128,256]{1,0:T(8,128)(2,1)S(1)}, bf16[128,256]{1,0:T(8,128)(2,1)}, u32[]{:S(2)}) copy-start(bf16[128,256]{1,0:T(8,128)(2,1)} %get-tuple-element.135) | copy-start | bytes 196612
  365.3 13.5 %copy-start.6 = (bf16[128,256]{1,0:T(8,128)(2,1)S(1)}, bf16[128,256]{1,0:T(8,128)(2,1)}, u32[]{:S(2)}) copy-start(bf16[128,256]{1,0:T(8,128)(2,1)} %get-tuple-element.136) | copy-start | bytes 196612
  366.2 12.6 %copy-start.5 = (bf16[128,256]{1,0:T(8,128)(2,1)S(1)}, bf16[128,256]{1,0:T(8,128)(2,1)}, u32[]{:S(2)}) copy-start(bf16[128,256]{1,0:T(8,128)(2,1)} %get-tuple-element.137) | copy-start | bytes 196612
  375.0 13.1 %all-to-all-start.5 = ((bf16[8,2,8192]{2,1,0:T(2,128)(2,1)}), bf16[8,2,8192]{2,1,0:T(2,128)(2,1)S(1)}, u32[]{:S(2)}, u32[]{:S(2)}) async-start(bf16[8,2,8192]{2,1,0:T(2,128)(2,1)} %reshape.187), calls=%async_computation.5 | async-start | bytes 524288 | tf_op jit(solution)/shard_map/all_to_all | solution.py:118
  378.4 78.9 %reduce-scatter.2.cloned.1.call-start = ((), (), s32[]{:S(2)}) async-start(), calls=%async_computation.8 | async-start | bytes 4718592 | tf_op jit(solution)/shard_map/reduce_scatter | solution.py:137
  408.1 49.2 %all-to-all-start.4 = ((bf16[8,2,32768]{2,1,0:T(2,128)(2,1)}), bf16[8,2,32768]{2,1,0:T(2,128)(2,1)}, u32[]{:S(2)}, u32[]{:S(2)}) async-start(bf16[8,2,32768]{2,1,0:T(2,128)(2,1)} %reshape.183), calls=%async_computation.4 | async-start | bytes 2097152 | tf_op jit(solution)/shard_map/all_to_all | solution.py:117
  412.4 97.2 %all-reduce.4.cloned.1.call-start = ((), (), s32[]{:S(2)}) async-start(), calls=%async_computation.9 | async-start | bytes 1048576 | tf_op jit(solution)/shard_map/psum | solution.py:145
Sparse Core Ops, SparseCore 0:
  125.0 48.3 all-reduce.5
  391.7 65.5 reduce-scatter.1
  460.3 49.2 all-reduce.3
where the time goes:
time: 523 us; the launch traced here: 518 us
  local copies, waits for them, and re-layouts  145 us (28%)
  waiting for transfers between devices  128 us (24%)
  other arithmetic  101 us (19%)
  matrix products  76.4 us (15%)
  starting transfers between devices  33 us (6%)
  between operations  19.1 us (4%)
  loops' own time  15.8 us (3%)
    unnamed x5, other arithmetic  59.1 us
    unnamed x49, local copies, waits for them, and re-layouts  45.2 us
    reduce_scatter x1, waiting for transfers between devices, local(): lax.psum_scatter(lax.dot_general(inputs_local, projected, contract_first,...  44.9 us
    psum x1, waiting for transfers between devices, local(): lowrank_grad = lax.psum(partial_rank, 'dp') / lax.axis_size('dp')  43.8 us
    gather x16, local copies, waits for them, and re-layouts, padded_block(): value_sel = jnp.take(value_blocks, safe, axis=0)  35.5 us
    all_to_all x1, waiting for transfers between devices, local(): lax.all_to_all(grad_out, 'seq', split_axis=2, concat_axis=1, tiled=True)  26.5 us
    dynamic_slice x24, local copies, waits for them, and re-layouts, local(): lax.scan(block_step, (zeros_grad, zeros_grad), (block_ids, query_blocks,...  23.5 us
    another operation x1, loops' own time, local(): lax.scan(block_step, (zeros_grad, zeros_grad), (block_ids, query_blocks,...  15.8 us
  transfers between devices with their start and end apart: 10, of which 5 were waited for; matrix products, arithmetic and copies ran while one was open for 61% of the time, Pallas kernels for 0%

commit v1 on v0

v1 whole, which is shorter than its diff:
```python
import math
from functools import partial

import jax
import jax.numpy as jnp
from jax import lax
from jax.experimental import pallas as pl
from jax.experimental.pallas import tpu as pltpu
from jax.sharding import PartitionSpec as P

HEADS = 32
KV_HEADS = 4
HEAD_DIM = 128
BLOCK = 128
GROUP = HEADS // KV_HEADS
UNROLL = 2
MASKED = -1e30

bf16 = jnp.bfloat16
f32 = jnp.float32
NT = (((1,), (1,)), ((), ()))
NN = (((1,), (0,)), ((), ()))
TN = (((0,), (0,)), ((), ()))


def mm(a, b, dims=NN):
    return lax.dot_general(a, b, dims, preferred_element_type=f32)


def attention_kernel(
    layout_ref, owner_ref, q_ref, do_ref, *refs, chips, dp_count, blocks, slots
):
    count = 2 * chips
    k_refs, refs = refs[:count], refs[count:]
    v_refs, refs = refs[:count], refs[count:]
    bk_refs, refs = refs[:dp_count], refs[dp_count:]
    bv_refs, refs = refs[:dp_count], refs[dp_count:]
    dq_ref, keep_ref, send_ref, kbuf, ktbuf, vbuf, dk_acc, dv_acc, basis, send_acc = refs

    kv_head = pl.program_id(0)
    place = lax.axis_index("seq")
    chip = place // 2
    core = lax.rem(place, 2)
    me = lax.axis_index("dp")
    scale = HEAD_DIM ** (-0.5)
    to_exp2 = scale * math.log2(math.e)

    for index in range(count):
        block = k_refs[index][...]
        kbuf[index] = block
        ktbuf[index] = block.T
        vbuf[index] = v_refs[index][...]
    dk_acc[...] = jnp.zeros_like(dk_acc)
    dv_acc[...] = jnp.zeros_like(dv_acc)

    own_k = lax.rem(me - owner_ref[kv_head] + dp_count, dp_count)
    own_v = lax.rem(me - owner_ref[KV_HEADS + kv_head] + dp_count, dp_count)
    for index in range(dp_count):

        @pl.when(own_k == index)
        def _():
            basis[:HEAD_DIM] = bk_refs[index][...]

        @pl.when(own_v == index)
        def _():
            basis[HEAD_DIM:] = bv_refs[index][...]

    rows = lax.broadcasted_iota(jnp.int32, (BLOCK, BLOCK), 0)
    columns = lax.broadcasted_iota(jnp.int32, (BLOCK, BLOCK), 1)
    causal = rows <= columns

    def heads_step(step, carry):
        lists = []
        for unit in range(UNROLL):
            head = kv_head * GROUP + step * UNROLL + unit
            base = (head * blocks + place) * slots
            listed = [layout_ref[base + slot] for slot in range(slots)]
            length = sum([(entry >= 0).astype(jnp.int32) for entry in listed])
            lists.append((listed, length))
        most = lists[0][1]
        for _, length in lists[1:]:
            most = jnp.maximum(most, length)

        def work(width):
            for unit in range(UNROLL):
                listed, length = lists[unit]
                lane = pl.ds(pl.multiple_of((step * UNROLL + unit) * HEAD_DIM, HEAD_DIM), HEAD_DIM)
                q = q_ref[:, lane]
                do = do_ref[:, lane]
                spots = [0]
                valid = [None]
                for slot in range(1, width):
                    entry = listed[slot - 1]
                    ok = slot < length
                    spot = (chip - entry // 2) + chips * (lax.rem(entry + core, 2))
                    spots.append(jnp.where(ok, spot, 0))
                    valid.append(ok)
                ks = jnp.concatenate([kbuf[spot] for spot in spots], axis=0)
                vs = jnp.concatenate([vbuf[spot] for spot in spots], axis=0)
                scores = mm(ks, q, NT) * to_exp2
                pieces = []
                for slot in range(width):
                    piece = scores[slot * BLOCK : (slot + 1) * BLOCK]
                    if slot == 0:
                        piece = jnp.where(causal, piece, MASKED)
                    else:
                        piece = jnp.where(valid[slot], piece, MASKED)
                    pieces.append(piece)
                scores = jnp.concatenate(pieces, axis=0)
                top = jnp.max(scores, axis=0, keepdims=True)
                raw = jnp.exp2(scores - top)
                weights = raw * (1.0 / jnp.sum(raw, axis=0, keepdims=True))
                low = weights.astype(bf16)
                dweights = mm(vs, do, NT)
                delta = jnp.sum(low.astype(f32) * dweights, axis=0, keepdims=True)
                dscores = (weights * (dweights - delta)).astype(bf16)
                dk = mm(dscores, q)
                dv = mm(low, do)
                kt = jnp.concatenate([ktbuf[spot] for spot in spots], axis=1)
                dq = (mm(kt, dscores) * scale).astype(bf16)
                dq_ref[:, lane] = dq.T
                for slot in range(width):
                    part = slice(slot * BLOCK, (slot + 1) * BLOCK)
                    dk_acc[spots[slot]] += dk[part]
                    dv_acc[spots[slot]] += dv[part]

        for width in range(1, slots + 1):
            pl.when(most == width)(partial(work, width))
        return carry

    lax.fori_loop(0, GROUP // UNROLL, heads_step, 0)

    chosen = basis[...]
    for index in range(count):
        grads = jnp.concatenate(
            [(dk_acc[index] * scale).astype(bf16), dv_acc[index].astype(bf16)], axis=1
        )
        term = mm(grads, chosen)
        target = keep_ref if index < chips else send_acc
        spot = slice((index % chips) * BLOCK, (index % chips + 1) * BLOCK)

        @pl.when(kv_head == 0)
        def _():
            target[spot] = term

        @pl.when(kv_head > 0)
        def _():
            target[spot] += term

    @pl.when(kv_head == KV_HEADS - 1)
    def _():
        send_ref[...] = send_acc[...].astype(bf16)


def attention(layout, owner, queries, grads, kv_parts, bases, blocks, slots):
    count = len(kv_parts)
    chips = count // 2
    rank = bases[0].shape[1]
    width = GROUP * HEAD_DIM
    body = partial(
        attention_kernel, chips=chips, dp_count=len(bases), blocks=blocks, slots=slots
    )
    wide = pl.BlockSpec((BLOCK, width), lambda g, *_: (0, g))
    key_spec = pl.BlockSpec((BLOCK, HEAD_DIM), lambda g, *_: (0, g))
    value_spec = pl.BlockSpec((BLOCK, HEAD_DIM), lambda g, *_: (0, KV_HEADS + g))
    basis_k = pl.BlockSpec((HEAD_DIM, rank), lambda g, *_: (g, 0))
    basis_v = pl.BlockSpec((HEAD_DIM, rank), lambda g, *_: (KV_HEADS + g, 0))
    whole = pl.BlockSpec((chips * BLOCK, rank), lambda g, *_: (0, 0))
    pairs = HEADS * 3
    return pl.pallas_call(
        body,
        grid_spec=pltpu.PrefetchScalarGridSpec(
            num_scalar_prefetch=2,
            grid=(KV_HEADS,),
            in_specs=[wide, wide]
            + [key_spec] * count
            + [value_spec] * count
            + [basis_k] * len(bases)
            + [basis_v] * len(bases),
            out_specs=[wide, whole, whole],
            scratch_shapes=[
                pltpu.VMEM((count, BLOCK, HEAD_DIM), bf16),
                pltpu.VMEM((count, HEAD_DIM, BLOCK), bf16),
                pltpu.VMEM((count, BLOCK, HEAD_DIM), bf16),
                pltpu.VMEM((count, BLOCK, HEAD_DIM), f32),
                pltpu.VMEM((count, BLOCK, HEAD_DIM), f32),
                pltpu.VMEM((2 * HEAD_DIM, rank), bf16),
                pltpu.VMEM((chips * BLOCK, rank), f32),
            ],
        ),
        out_shape=[
            jax.ShapeDtypeStruct((BLOCK, HEADS * HEAD_DIM), bf16),
            jax.ShapeDtypeStruct((chips * BLOCK, rank), f32),
            jax.ShapeDtypeStruct((chips * BLOCK, rank), bf16),
        ],
        compiler_params=pltpu.CompilerParams(vmem_limit_bytes=56 * 1024 * 1024),
        cost_estimate=pl.CostEstimate(
            flops=pairs * 10 * BLOCK**3, bytes_accessed=8 << 20, transcendentals=pairs * BLOCK**2
        ),
        name="attention_backward",
    )(
        layout,
        owner,
        queries,
        grads,
        *kv_parts,
        *kv_parts,
        *bases,
        *bases,
    )


def fold_kernel(keep_ref, came_ref, own_ref, *send_refs):
    own_ref[...] = keep_ref[:BLOCK] + came_ref[:BLOCK].astype(f32)
    for index, send_ref in enumerate(send_refs):
        rows = slice((index + 1) * BLOCK, (index + 2) * BLOCK)
        send_ref[...] = (keep_ref[rows] + came_ref[rows].astype(f32)).astype(bf16)


def fold(keep, came, chips):
    rank = keep.shape[1]
    return pl.pallas_call(
        fold_kernel,
        out_shape=[jax.ShapeDtypeStruct((BLOCK, rank), f32)]
        + [jax.ShapeDtypeStruct((BLOCK, rank), bf16)] * (chips - 1),
        compiler_params=pltpu.CompilerParams(vmem_limit_bytes=32 * 1024 * 1024),
        name="fold_parts",
    )(keep, came)


def outer_kernel(*refs, chips):
    x_refs, refs = refs[:chips], refs[chips:]
    p_refs, refs = refs[:chips], refs[chips:]
    keep_ref, send_ref = refs
    core = lax.rem(lax.axis_index("seq"), 2)
    half = keep_ref.shape[0]

    def product(which):
        columns = pl.ds(pl.multiple_of(which * half, half), half)
        inputs = jnp.concatenate([ref[:, columns] for ref in x_refs], axis=0)
        projected = jnp.concatenate([ref[...] for ref in p_refs], axis=0)
        return mm(inputs, projected, TN)

    send_ref[...] = product(1 - core).astype(bf16)
    keep_ref[...] = product(core)


def outer(x_parts, p_parts):
    chips = len(x_parts)
    features = x_parts[0].shape[1]
    rank = p_parts[0].shape[1]
    return pl.pallas_call(
        partial(outer_kernel, chips=chips),
        out_shape=[
            jax.ShapeDtypeStruct((features // 2, rank), f32),
            jax.ShapeDtypeStruct((features // 2, rank), bf16),
        ],
        compiler_params=pltpu.CompilerParams(vmem_limit_bytes=32 * 1024 * 1024),
        name="outer_product",
    )(*x_parts, *p_parts)


def local(queries, keys, values, grad_out, layer_input, basis_store, owner, layout):
    seq_count = lax.axis_size("seq")
    dp_count = lax.axis_size("dp")
    chips = seq_count // 2
    place = lax.axis_index("seq")
    chip = place // 2
    blocks, slots = layout.shape[1], layout.shape[2]

    def pair(x):
        return lax.ppermute(x, "seq", [(i, i ^ 1) for i in range(seq_count)])

    def up(x, step):
        moves = [(i, i + 2 * step) for i in range(seq_count) if i + 2 * step < seq_count]
        return lax.ppermute(x, "seq", moves)

    def down(x, step):
        moves = [(i, i - 2 * step) for i in range(seq_count) if i >= 2 * step]
        return lax.ppermute(x, "seq", moves)

    def around(x, step):
        moves = [(i, (i + 2 * step) % seq_count) for i in range(seq_count)]
        return lax.ppermute(x, "seq", moves)

    def across(x, step):
        return lax.ppermute(x, "dp", [(i, (i + step) % dp_count) for i in range(dp_count)])

    kv = jnp.concatenate([keys[0], values[0]], axis=1)
    same = [kv] + [up(kv, step) for step in range(1, chips)]
    other = [pair(part) for part in same]

    basis = basis_store[0]
    bases = [basis] + [across(basis, step) for step in range(1, dp_count)]

    features = layer_input.shape[2] // chips

    def columns(step):
        target = lax.rem(chip + step, chips)
        return lax.dynamic_slice_in_dim(layer_input[0], target * features, features, 1)

    x_parts = [columns(0)] + [around(columns(step), step) for step in range(1, chips)]

    grad_query, keep, send = attention(
        layout.reshape(-1),
        owner,
        queries[0],
        grad_out[0],
        same + other,
        bases,
        blocks,
        slots,
    )

    own, *sends = fold(keep, pair(send), chips)
    total = own
    for step in range(1, chips):
        total = total + down(sends[step - 1], step).astype(f32)
    projected = total.astype(bf16)
    p_parts = [projected] + [around(projected, step) for step in range(1, chips)]
    kept, sent = outer(x_parts, p_parts)
    partial_rank = kept + pair(sent).astype(f32)
    low = partial_rank.astype(bf16)
    for step in range(1, dp_count):
        partial_rank = partial_rank + across(low, step).astype(f32)
    lowrank_grad = partial_rank / dp_count
    return (grad_query[None], lowrank_grad)


def solution(mesh):
    in_specs = (
        P("dp", "seq", None),
        P("dp", "seq", None),
        P("dp", "seq", None),
        P("dp", "seq", None),
        P("dp", "seq", None),
        P("dp", None, None),
        P(),
        P(),
    )
    out_specs = (P("dp", "seq", None), P("seq", None))
    return jax.shard_map(local, mesh=mesh, in_specs=in_specs, out_specs=out_specs, check_vma=False)
```

time: 523 us -> 140 us (0.27)
  local copies, waits for them, and re-layouts: 145 us -> 5.48 us
  other arithmetic: 101 us -> 2.08 us
  matrix products: 76.4 us -> 0 us
  waiting for transfers between devices: 128 us -> 56.6 us
  Pallas kernels: 0 us -> 22.7 us
  starting transfers between devices: 33 us -> 51.4 us
  between operations: 19.1 us -> 0.83 us
  loops' own time: 15.8 us -> 0 us
    dot_general x49 -> x0, matrix products: 76.4 us -> none  [the longest x8 13.5 us: padded_block(): jnp.einsum('hqsk,hskd->qhd', weights_low, value_sel, preferred_element_ty...]
    unnamed x5 -> x0, other arithmetic: 59.1 us -> none
    ppermute x0 -> x24, waiting for transfers between devices: none -> 56.6 us  [the longest x6 23.2 us: around(): return lax.ppermute(x, 'seq', moves)]
    ppermute x0 -> x24, starting transfers between devices: none -> 51.4 us  [the longest x6 18.7 us: across(): lax.ppermute(x, 'dp', [(i, (i + step) % dp_count) for i in range(dp_count)])]
    gather x32 -> x0, local copies, waits for them, and re-layouts: 48.8 us -> none  [the longest x16 35.5 us: padded_block(): value_sel = jnp.take(value_blocks, safe, axis=0)]
    reduce_scatter x1 -> x0, waiting for transfers between devices: 44.9 us -> none  [local(): lax.psum_scatter(lax.dot_general(inputs_local, projected, contract_first,...]
    psum x2 -> x0, waiting for transfers between devices: 43.8 us -> none  [the longest x1 43.8 us: local(): lowrank_grad = lax.psum(partial_rank, 'dp') / lax.axis_size('dp')]
    unnamed x49 -> x23, local copies, waits for them, and re-layouts: 45.2 us -> 3.5 us
  transfers between devices with their start and end apart: 10 -> 24, of which waited for: 5 -> 13; matrix products, arithmetic and copies ran while one was open for 61% -> 2% of each run, Pallas kernels for 0% -> 0%
where the time goes in v1:
time: 140 us; the launch traced here: 139 us
  waiting for transfers between devices  56.6 us (40%)
  starting transfers between devices  51.4 us (37%)
  Pallas kernels  22.7 us (16%)
  local copies, waits for them, and re-layouts  5.48 us (4%)
  other arithmetic  2.08 us (1%)
    ppermute x6, waiting for transfers between devices, around(): return lax.ppermute(x, 'seq', moves)  23.2 us
    pallas_call x1, Pallas kernels, attention(): pl.pallas_call(body, grid_spec=pltpu.PrefetchScalarGridSpec(num_scalar_pr...  22.1 us
    ppermute x6, waiting for transfers between devices, across(): lax.ppermute(x, 'dp', [(i, (i + step) % dp_count) for i in range(dp_count)])  22 us
    ppermute x6, starting transfers between devices, across(): lax.ppermute(x, 'dp', [(i, (i + step) % dp_count) for i in range(dp_count)])  18.7 us
    ppermute x6, starting transfers between devices, around(): return lax.ppermute(x, 'seq', moves)  15.8 us
    ppermute x3, starting transfers between devices, up(): return lax.ppermute(x, 'seq', moves)  10.7 us
    ppermute x3, waiting for transfers between devices, up(): return lax.ppermute(x, 'seq', moves)  7.68 us
    ppermute x3, starting transfers between devices, down(): return lax.ppermute(x, 'seq', moves)  3.88 us
  transfers between devices with their start and end apart: 24, of which 13 were waited for; matrix products, arithmetic and copies ran while one was open for 2% of the time, Pallas kernels for 0%

profile of v1, /device:TPU:0, one launch (start us, length us, event | category | flops | bytes accessed | tf_op | source)
XLA Modules:
  0.0 139.1 jit_solution(17505084118813623702)
XLA Ops:
  0.6 1.0 pad_maximum_fusion.refs_0_.refs_8_
  1.7 4.9 %collective-permute-start = (bf16[128,1024]{1,0:T(8,128)(2,1)S(1)}, bf16[128,1024]{1,0:T(8,128)(2,1)S(1)}, u32[]{:S(2)}, u32[]{:S(2)}) collective-permute-start(bf16[128,1024]{1,0:T(8,128)(2,1)S(1)} %pad_maximum_fusion.refs_0_.refs_8_), channel_id=1, source_target_pairs={{0,2},{1,3},{2,4},{3,5},{4,6},{5,7},{8,10},{9,11},{10,12},{11,13},... | collective-permute-start | bytes 786440 | tf_op jit(solution)/shard_map/ppermute | solution.py:276
  6.7 4.5 %collective-permute-start.1 = (bf16[128,1024]{1,0:T(8,128)(2,1)S(1)}, bf16[128,1024]{1,0:T(8,128)(2,1)S(1)}, u32[]{:S(2)}, u32[]{:S(2)}) collective-permute-start(bf16[128,1024]{1,0:T(8,128)(2,1)S(1)} %pad_maximum_fusion.refs_0_.refs_8_), channel_id=1, source_target_pairs={{0,4},{1,5},{2,6},{3,7},{8,12},{9,13},{10,14},{11,15},{16,20},{17,... | collective-permute-start | bytes 786440 | tf_op jit(solution)/shard_map/ppermute | solution.py:276
  11.2 1.3 collective-permute-start.2
  12.6 1.5 %collective-permute-start.7 = (bf16[1024,256]{1,0:T(8,128)(2,1)S(1)}, bf16[1024,256]{1,0:T(8,128)(2,1)S(1)}, u32[]{:S(2)}, u32[]{:S(2)}) collective-permute-start(bf16[1024,256]{1,0:T(8,128)(2,1)S(1)} %bitcast.16), channel_id=1, source_target_pairs={{0,8},{8,16},{16,24},{24,0},{1,9},{9,17},{17,25},{25,1},{2,10},{10... | collective-permute-start | bytes 1572872 | tf_op jit(solution)/shard_map/ppermute | solution.py:287
  14.3 4.7 %collective-permute-done.1.refs_2_.refs_10_ = bf16[128,1024]{1,0:T(8,128)(2,1)S(1)} collective-permute-done((bf16[128,1024]{1,0:T(8,128)(2,1)S(1)}, bf16[128,1024]{1,0:T(8,128)(2,1)S(1)}, u32[]{:S(2)}, u32[]{:S(2)}) %collective-permute-start.1) | collective-permute-done | bytes 262176 | tf_op jit(solution)/shard_map/ppermute | solution.py:276
  19.0 1.5 %collective-permute-start.8 = (bf16[1024,256]{1,0:T(8,128)(2,1)S(1)}, bf16[1024,256]{1,0:T(8,128)(2,1)S(1)}, u32[]{:S(2)}, u32[]{:S(2)}) collective-permute-start(bf16[1024,256]{1,0:T(8,128)(2,1)S(1)} %bitcast.17), channel_id=1, source_target_pairs={{0,16},{8,24},{16,0},{24,8},{1,17},{9,25},{17,1},{25,9},{2,18},{10... | collective-permute-start | bytes 1572872 | tf_op jit(solution)/shard_map/ppermute | solution.py:287
  20.5 2.9 %collective-permute-done.2.refs_3_.refs_11_ = bf16[128,1024]{1,0:T(8,128)(2,1)S(1)} collective-permute-done((bf16[128,1024]{1,0:T(8,128)(2,1)S(1)}, bf16[128,1024]{1,0:T(8,128)(2,1)S(1)}, u32[]{:S(2)}, u32[]{:S(2)}) %collective-permute-start.2) | collective-permute-done | bytes 262176 | tf_op jit(solution)/shard_map/ppermute | solution.py:276
  23.5 2.4 %collective-permute-start.9 = (bf16[1024,256]{1,0:T(8,128)(2,1)S(1)}, bf16[1024,256]{1,0:T(8,128)(2,1)S(1)}, u32[]{:S(2)}, u32[]{:S(2)}) collective-permute-start(bf16[1024,256]{1,0:T(8,128)(2,1)S(1)} %bitcast.18), channel_id=1, source_target_pairs={{0,24},{8,0},{16,8},{24,16},{1,25},{9,1},{17,9},{25,17},{2,26},{10... | collective-permute-start | bytes 1572872 | tf_op jit(solution)/shard_map/ppermute | solution.py:287
  28.7 10.3 %collective-permute-done.8.refs_18_.refs_22_ = bf16[1024,256]{1,0:T(8,128)(2,1)S(1)} collective-permute-done((bf16[1024,256]{1,0:T(8,128)(2,1)S(1)}, bf16[1024,256]{1,0:T(8,128)(2,1)S(1)}, u32[]{:S(2)}, u32[]{:S(2)}) %collective-permute-start.8) | collective-permute-done | bytes 524320 | tf_op jit(solution)/shard_map/ppermute | solution.py:287
  40.0 22.1 %attention_backward.1 = (bf16[128,4096]{1,0:T(8,128)(2,1)}, f32[512,256]{1,0:T(8,128)}, bf16[512,256]{1,0:T(8,128)(2,1)}) custom-call(s32[1024]{0:T(1024)} %reshape.11.layout_ref, s32[8]{0:T(128)} %owner_ref.1, bf16[128,4096]{1,0:T(8,128)(2,1)} %bitcast.19, bf16[128,4096]{1,0:T(8,128)(2,1)} %bitcast.20, bf16[128,1024]{1,0:T(8,128)(2,1)} %copy-done.1, ...), custom_call_target="tpu_custom_call" | custom-call | flops 2013265920 | bytes 8388608 | tf_op jit(solution)/shard_map/attention_backward/pallas_call | solution.py:170
  62.1 1.5 %collective-permute-start.13 = (bf16[512,256]{1,0:T(8,128)(2,1)}, bf16[512,256]{1,0:T(8,128)(2,1)S(1)}, u32[]{:S(2)}, u32[]{:S(2)}) collective-permute-start(bf16[512,256]{1,0:T(8,128)(2,1)} %get-tuple-element.13), channel_id=1, source_target_pairs={{0,1},{1,0},{2,3},{3,2},{4,5},{5,4},{6,7},{7,6},{8,9},{9,8},{10,11... | collective-permute-start | bytes 786440 | tf_op jit(solution)/shard_map/ppermute | solution.py:272
  63.6 1.4 collective-permute-done.13.came_ref
  65.0 1.0 copy-done
  66.1 1.3 collective-permute-start.14
  67.4 1.3 collective-permute-start.15
  68.7 1.3 collective-permute-start.16
  70.0 1.3 dynamic-slice_bitcast_fusion
  71.2 8.1 %collective-permute-start.10 = (bf16[128,1024]{1,0:T(8,128)(2,1)S(1)}, bf16[128,1024]{1,0:T(8,128)(2,1)S(1)}, u32[]{:S(2)}, u32[]{:S(2)}) collective-permute-start(bf16[128,1024]{1,0:T(8,128)(2,1)S(1)} %get-tuple-element.21), channel_id=1, source_target_pairs={{0,2},{1,3},{2,4},{3,5},{4,6},{5,7},{6,0},{7,1},{8,10},{9,11},{10,... | collective-permute-start | bytes 786440 | tf_op jit(solution)/shard_map/ppermute | solution.py:284
  79.3 4.2 %collective-permute-start.11 = (bf16[128,1024]{1,0:T(8,128)(2,1)S(1)}, bf16[128,1024]{1,0:T(8,128)(2,1)S(1)}, u32[]{:S(2)}, u32[]{:S(2)}) collective-permute-start(bf16[128,1024]{1,0:T(8,128)(2,1)S(1)} %get-tuple-element.23), channel_id=1, source_target_pairs={{0,4},{1,5},{2,6},{3,7},{4,0},{5,1},{6,2},{7,3},{8,12},{9,13},{10,... | collective-permute-start | bytes 786440 | tf_op jit(solution)/shard_map/ppermute | solution.py:284
  84.6 1.1 collective-permute-start.17
  85.7 4.6 %collective-permute-done.10.refs_1_ = bf16[128,1024]{1,0:T(8,128)(2,1)S(1)} collective-permute-done((bf16[128,1024]{1,0:T(8,128)(2,1)S(1)}, bf16[128,1024]{1,0:T(8,128)(2,1)S(1)}, u32[]{:S(2)}, u32[]{:S(2)}) %collective-permute-start.10) | collective-permute-done | bytes 262176 | tf_op jit(solution)/shard_map/ppermute | solution.py:284
  90.3 2.2 %collective-permute-start.19 = (bf16[128,256]{1,0:T(8,128)(2,1)S(1)}, bf16[128,256]{1,0:T(8,128)(2,1)S(1)}, u32[]{:S(2)}, u32[]{:S(2)}) collective-permute-start(bf16[128,256]{1,0:T(8,128)(2,1)S(1)} %add_convert_fusion.refs_4_), channel_id=1, source_target_pairs={{0,6},{1,7},{2,0},{3,1},{4,2},{5,3},{6,4},{7,5},{8,14},{9,15},{10,... | collective-permute-start | bytes 196616 | tf_op jit(solution)/shard_map/ppermute | solution.py:284
  92.5 9.0 %collective-permute-done.11.refs_2_ = bf16[128,1024]{1,0:T(8,128)(2,1)S(1)} collective-permute-done((bf16[128,1024]{1,0:T(8,128)(2,1)S(1)}, bf16[128,1024]{1,0:T(8,128)(2,1)S(1)}, u32[]{:S(2)}, u32[]{:S(2)}) %collective-permute-start.11) | collective-permute-done | bytes 262176 | tf_op jit(solution)/shard_map/ppermute | solution.py:284
  101.6 1.4 %collective-permute-done.17.refs_5_ = bf16[128,256]{1,0:T(8,128)(2,1)S(1)} collective-permute-done((bf16[128,256]{1,0:T(8,128)(2,1)S(1)}, bf16[128,256]{1,0:T(8,128)(2,1)S(1)}, u32[]{:S(2)}, u32[]{:S(2)}) %collective-permute-start.17) | collective-permute-done | bytes 65568 | tf_op jit(solution)/shard_map/ppermute | solution.py:284
  103.0 8.1 %collective-permute-done.18.refs_6_ = bf16[128,256]{1,0:T(8,128)(2,1)S(1)} collective-permute-done((bf16[128,256]{1,0:T(8,128)(2,1)S(1)}, bf16[128,256]{1,0:T(8,128)(2,1)S(1)}, u32[]{:S(2)}, u32[]{:S(2)}) %collective-permute-start.18) | collective-permute-done | bytes 65568 | tf_op jit(solution)/shard_map/ppermute | solution.py:284
  111.7 1.5 %collective-permute-done.20 = bf16[512,256]{1,0:T(8,128)(2,1)S(1)} collective-permute-done((bf16[512,256]{1,0:T(8,128)(2,1)S(1)}, bf16[512,256]{1,0:T(8,128)(2,1)S(1)}, u32[]{:S(2)}, u32[]{:S(2)}) %collective-permute-start.20) | collective-permute-done | bytes 262176 | tf_op jit(solution)/shard_map/ppermute | solution.py:272
  113.3 11.7 %collective-permute-start.21 = (bf16[512,256]{1,0:T(8,128)(2,1)S(1)}, bf16[512,256]{1,0:T(8,128)(2,1)S(1)}, u32[]{:S(2)}, u32[]{:S(2)}) collective-permute-start(bf16[512,256]{1,0:T(8,128)(2,1)S(1)} %fusion), channel_id=1, source_target_pairs={{0,8},{8,16},{16,24},{24,0},{1,9},{9,17},{17,25},{25,1},{2,10},{10... | collective-permute-start | bytes 786440 | tf_op jit(solution)/shard_map/ppermute | solution.py:287
  125.0 1.5 %collective-permute-start.22 = (bf16[512,256]{1,0:T(8,128)(2,1)S(1)}, bf16[512,256]{1,0:T(8,128)(2,1)S(1)}, u32[]{:S(2)}, u32[]{:S(2)}) collective-permute-start(bf16[512,256]{1,0:T(8,128)(2,1)S(1)} %fusion), channel_id=1, source_target_pairs={{0,16},{8,24},{16,0},{24,8},{1,17},{9,25},{17,1},{25,9},{2,18},{10... | collective-permute-start | bytes 786440 | tf_op jit(solution)/shard_map/ppermute | solution.py:287
  126.5 6.6 %collective-permute-done.21 = bf16[512,256]{1,0:T(8,128)(2,1)S(1)} collective-permute-done((bf16[512,256]{1,0:T(8,128)(2,1)S(1)}, bf16[512,256]{1,0:T(8,128)(2,1)S(1)}, u32[]{:S(2)}, u32[]{:S(2)}) %collective-permute-start.21) | collective-permute-done | bytes 262176 | tf_op jit(solution)/shard_map/ppermute | solution.py:287
  133.0 5.1 %collective-permute-done.22 = bf16[512,256]{1,0:T(8,128)(2,1)S(1)} collective-permute-done((bf16[512,256]{1,0:T(8,128)(2,1)S(1)}, bf16[512,256]{1,0:T(8,128)(2,1)S(1)}, u32[]{:S(2)}, u32[]{:S(2)}) %collective-permute-start.22) | collective-permute-done | bytes 262176 | tf_op jit(solution)/shard_map/ppermute | solution.py:287
  138.1 1.0 add_multiply_fusion
  (48 shorter events, 5.6 us)
Async XLA Ops:
  0.6 11.9 %copy-start.2 = (bf16[1,1024,256]{2,1,0:T(8,128)(2,1)S(1)}, bf16[1,1024,256]{2,1,0:T(8,128)(2,1)}, u32[]{:S(2)}) copy-start(bf16[1,1024,256]{2,1,0:T(8,128)(2,1)} %param.13) | copy-start | bytes 1572868
  1.7 37.4 %copy-start.1 = (bf16[128,1024]{1,0:T(8,128)(2,1)}, bf16[128,1024]{1,0:T(8,128)(2,1)S(1)}, u32[]{:S(2)}) copy-start(bf16[128,1024]{1,0:T(8,128)(2,1)S(1)} %pad_maximum_fusion.refs_0_.refs_8_) | copy-start | bytes 786436
  1.7 12.4 %collective-permute-start = (bf16[128,1024]{1,0:T(8,128)(2,1)S(1)}, bf16[128,1024]{1,0:T(8,128)(2,1)S(1)}, u32[]{:S(2)}, u32[]{:S(2)}) collective-permute-start(bf16[128,1024]{1,0:T(8,128)(2,1)S(1)} %pad_maximum_fusion.refs_0_.refs_8_), channel_id=1, source_target_pairs={{0,2},{1,3},{2,4},{3,5},{4,6},{5,7},{8,10},{9,11},{10,12},{11,13},... | collective-permute-start | bytes 786440 | tf_op jit(solution)/shard_map/ppermute | solution.py:276
  6.7 12.3 %collective-permute-start.1 = (bf16[128,1024]{1,0:T(8,128)(2,1)S(1)}, bf16[128,1024]{1,0:T(8,128)(2,1)S(1)}, u32[]{:S(2)}, u32[]{:S(2)}) collective-permute-start(bf16[128,1024]{1,0:T(8,128)(2,1)S(1)} %pad_maximum_fusion.refs_0_.refs_8_), channel_id=1, source_target_pairs={{0,4},{1,5},{2,6},{3,7},{8,12},{9,13},{10,14},{11,15},{16,20},{17,... | collective-permute-start | bytes 786440 | tf_op jit(solution)/shard_map/ppermute | solution.py:276
  11.2 12.3 %collective-permute-start.2 = (bf16[128,1024]{1,0:T(8,128)(2,1)S(1)}, bf16[128,1024]{1,0:T(8,128)(2,1)S(1)}, u32[]{:S(2)}, u32[]{:S(2)}) collective-permute-start(bf16[128,1024]{1,0:T(8,128)(2,1)S(1)} %pad_maximum_fusion.refs_0_.refs_8_), channel_id=1, source_target_pairs={{0,6},{1,7},{8,14},{9,15},{16,22},{17,23},{24,30},{25,31}} | collective-permute-start | bytes 786440 | tf_op jit(solution)/shard_map/ppermute | solution.py:276
  12.5 13.4 %collective-permute-start.3 = (bf16[128,1024]{1,0:T(8,128)(2,1)S(1)}, bf16[128,1024]{1,0:T(8,128)(2,1)S(1)}, u32[]{:S(2)}, u32[]{:S(2)}) collective-permute-start(bf16[128,1024]{1,0:T(8,128)(2,1)S(1)} %pad_maximum_fusion.refs_0_.refs_8_), channel_id=1, source_target_pairs={{0,1},{1,0},{2,3},{3,2},{4,5},{5,4},{6,7},{7,6},{8,9},{9,8},{10,11... | collective-permute-start | bytes 786440 | tf_op jit(solution)/shard_map/ppermute | solution.py:272
  12.6 16.1 %collective-permute-start.7 = (bf16[1024,256]{1,0:T(8,128)(2,1)S(1)}, bf16[1024,256]{1,0:T(8,128)(2,1)S(1)}, u32[]{:S(2)}, u32[]{:S(2)}) collective-permute-start(bf16[1024,256]{1,0:T(8,128)(2,1)S(1)} %bitcast.16), channel_id=1, source_target_pairs={{0,8},{8,16},{16,24},{24,0},{1,9},{9,17},{17,25},{25,1},{2,10},{10... | collective-permute-start | bytes 1572872 | tf_op jit(solution)/shard_map/ppermute | solution.py:287
  14.1 25.0 %copy-start.6 = (bf16[128,1024]{1,0:T(8,128)(2,1)}, bf16[128,1024]{1,0:T(8,128)(2,1)S(1)}, u32[]{:S(2)}) copy-start(bf16[128,1024]{1,0:T(8,128)(2,1)S(1)} %collective-permute-done.refs_1_.refs_9_) | copy-start | bytes 786436
  14.1 11.8 %collective-permute-start.4 = (bf16[128,1024]{1,0:T(8,128)(2,1)S(1)}, bf16[128,1024]{1,0:T(8,128)(2,1)S(1)}, u32[]{:S(2)}, u32[]{:S(2)}) collective-permute-start(bf16[128,1024]{1,0:T(8,128)(2,1)S(1)} %collective-permute-done.refs_1_.refs_9_), channel_id=1, source_target_pairs={{0,1},{1,0},{2,3},{3,2},{4,5},{5,4},{6,7},{7,6},{8,9},{9,8},{10,11... | collective-permute-start | bytes 786440 | tf_op jit(solution)/shard_map/ppermute | solution.py:272
  19.0 20.1 %copy-start.7 = (bf16[128,1024]{1,0:T(8,128)(2,1)}, bf16[128,1024]{1,0:T(8,128)(2,1)S(1)}, u32[]{:S(2)}) copy-start(bf16[128,1024]{1,0:T(8,128)(2,1)S(1)} %collective-permute-done.1.refs_2_.refs_10_) | copy-start | bytes 786436
  19.0 20.0 %collective-permute-start.8 = (bf16[1024,256]{1,0:T(8,128)(2,1)S(1)}, bf16[1024,256]{1,0:T(8,128)(2,1)S(1)}, u32[]{:S(2)}, u32[]{:S(2)}) collective-permute-start(bf16[1024,256]{1,0:T(8,128)(2,1)S(1)} %bitcast.17), channel_id=1, source_target_pairs={{0,16},{8,24},{16,0},{24,8},{1,17},{9,25},{17,1},{25,9},{2,18},{10... | collective-permute-start | bytes 1572872 | tf_op jit(solution)/shard_map/ppermute | solution.py:287
  23.5 15.7 %copy-start.8 = (bf16[128,1024]{1,0:T(8,128)(2,1)}, bf16[128,1024]{1,0:T(8,128)(2,1)S(1)}, u32[]{:S(2)}) copy-start(bf16[128,1024]{1,0:T(8,128)(2,1)S(1)} %collective-permute-done.2.refs_3_.refs_11_) | copy-start | bytes 786436
  23.5 15.6 %collective-permute-start.9 = (bf16[1024,256]{1,0:T(8,128)(2,1)S(1)}, bf16[1024,256]{1,0:T(8,128)(2,1)S(1)}, u32[]{:S(2)}, u32[]{:S(2)}) collective-permute-start(bf16[1024,256]{1,0:T(8,128)(2,1)S(1)} %bitcast.18), channel_id=1, source_target_pairs={{0,24},{8,0},{16,8},{24,16},{1,25},{9,1},{17,9},{25,17},{2,26},{10... | collective-permute-start | bytes 1572872 | tf_op jit(solution)/shard_map/ppermute | solution.py:287
  25.9 13.2 %copy-start.9 = (bf16[128,1024]{1,0:T(8,128)(2,1)}, bf16[128,1024]{1,0:T(8,128)(2,1)S(1)}, u32[]{:S(2)}) copy-start(bf16[128,1024]{1,0:T(8,128)(2,1)S(1)} %collective-permute-done.3.refs_4_.refs_12_) | copy-start | bytes 786436
  25.9 2.8 %collective-permute-start.5 = (bf16[128,1024]{1,0:T(8,128)(2,1)S(1)}, bf16[128,1024]{1,0:T(8,128)(2,1)}, u32[]{:S(2)}, u32[]{:S(2)}) collective-permute-start(bf16[128,1024]{1,0:T(8,128)(2,1)S(1)} %collective-permute-done.1.refs_2_.refs_10_), channel_id=1, source_target_pairs={{0,1},{1,0},{2,3},{3,2},{4,5},{5,4},{6,7},{7,6},{8,9},{9,8},{10,11... | collective-permute-start | bytes 786440 | tf_op jit(solution)/shard_map/ppermute | solution.py:272
  26.7 2.0 %collective-permute-start.6 = (bf16[128,1024]{1,0:T(8,128)(2,1)S(1)}, bf16[128,1024]{1,0:T(8,128)(2,1)}, u32[]{:S(2)}, u32[]{:S(2)}) collective-permute-start(bf16[128,1024]{1,0:T(8,128)(2,1)S(1)} %collective-permute-done.2.refs_3_.refs_11_), channel_id=1, source_target_pairs={{0,1},{1,0},{2,3},{3,2},{4,5},{5,4},{6,7},{7,6},{8,9},{9,8},{10,11... | collective-permute-start | bytes 786440 | tf_op jit(solution)/shard_map/ppermute | solution.py:272
  28.7 10.4 %copy-start.3 = (bf16[1024,256]{1,0:T(8,128)(2,1)}, bf16[1024,256]{1,0:T(8,128)(2,1)S(1)}, u32[]{:S(2)}) copy-start(bf16[1024,256]{1,0:T(8,128)(2,1)S(1)} %collective-permute-done.7.refs_17_.refs_21_) | copy-start | bytes 1572868
  62.1 2.9 %collective-permute-start.13 = (bf16[512,256]{1,0:T(8,128)(2,1)}, bf16[512,256]{1,0:T(8,128)(2,1)S(1)}, u32[]{:S(2)}, u32[]{:S(2)}) collective-permute-start(bf16[512,256]{1,0:T(8,128)(2,1)} %get-tuple-element.13), channel_id=1, source_target_pairs={{0,1},{1,0},{2,3},{3,2},{4,5},{5,4},{6,7},{7,6},{8,9},{9,8},{10,11... | collective-permute-start | bytes 786440 | tf_op jit(solution)/shard_map/ppermute | solution.py:272
  65.0 1.0 copy-start
  66.1 17.5 %collective-permute-start.14 = (bf16[128,256]{1,0:T(8,128)(2,1)S(1)}, bf16[128,256]{1,0:T(8,128)(2,1)S(1)}, u32[]{:S(2)}, u32[]{:S(2)}) collective-permute-start(bf16[128,256]{1,0:T(8,128)(2,1)S(1)} %get-tuple-element.15), channel_id=1, source_target_pairs={{2,0},{3,1},{4,2},{5,3},{6,4},{7,5},{10,8},{11,9},{12,10},{13,11},... | collective-permute-start | bytes 196616 | tf_op jit(solution)/shard_map/ppermute | solution.py:280
  67.4 16.4 %collective-permute-start.15 = (bf16[128,256]{1,0:T(8,128)(2,1)S(1)}, bf16[128,256]{1,0:T(8,128)(2,1)S(1)}, u32[]{:S(2)}, u32[]{:S(2)}) collective-permute-start(bf16[128,256]{1,0:T(8,128)(2,1)S(1)} %get-tuple-element.16), channel_id=1, source_target_pairs={{4,0},{5,1},{6,2},{7,3},{12,8},{13,9},{14,10},{15,11},{20,16},{21,... | collective-permute-start | bytes 196616 | tf_op jit(solution)/shard_map/ppermute | solution.py:280
  68.7 15.9 %collective-permute-start.16 = (bf16[128,256]{1,0:T(8,128)(2,1)S(1)}, bf16[128,256]{1,0:T(8,128)(2,1)S(1)}, u32[]{:S(2)}, u32[]{:S(2)}) collective-permute-start(bf16[128,256]{1,0:T(8,128)(2,1)S(1)} %get-tuple-element.17), channel_id=1, source_target_pairs={{6,0},{7,1},{14,8},{15,9},{22,16},{23,17},{30,24},{31,25}} | collective-permute-start | bytes 196616 | tf_op jit(solution)/shard_map/ppermute | solution.py:280
  71.2 19.1 %collective-permute-start.10 = (bf16[128,1024]{1,0:T(8,128)(2,1)S(1)}, bf16[128,1024]{1,0:T(8,128)(2,1)S(1)}, u32[]{:S(2)}, u32[]{:S(2)}) collective-permute-start(bf16[128,1024]{1,0:T(8,128)(2,1)S(1)} %get-tuple-element.21), channel_id=1, source_target_pairs={{0,2},{1,3},{2,4},{3,5},{4,6},{5,7},{6,0},{7,1},{8,10},{9,11},{10,... | collective-permute-start | bytes 786440 | tf_op jit(solution)/shard_map/ppermute | solution.py:284
  79.3 22.2 %collective-permute-start.11 = (bf16[128,1024]{1,0:T(8,128)(2,1)S(1)}, bf16[128,1024]{1,0:T(8,128)(2,1)S(1)}, u32[]{:S(2)}, u32[]{:S(2)}) collective-permute-start(bf16[128,1024]{1,0:T(8,128)(2,1)S(1)} %get-tuple-element.23), channel_id=1, source_target_pairs={{0,4},{1,5},{2,6},{3,7},{4,0},{5,1},{6,2},{7,3},{8,12},{9,13},{10,... | collective-permute-start | bytes 786440 | tf_op jit(solution)/shard_map/ppermute | solution.py:284
  83.6 18.0 %collective-permute-start.12 = (bf16[128,1024]{1,0:T(8,128)(2,1)S(1)}, bf16[128,1024]{1,0:T(8,128)(2,1)S(1)}, u32[]{:S(2)}, u32[]{:S(2)}) collective-permute-start(bf16[128,1024]{1,0:T(8,128)(2,1)S(1)} %get-tuple-element.20), channel_id=1, source_target_pairs={{0,6},{1,7},{2,0},{3,1},{4,2},{5,3},{6,4},{7,5},{8,14},{9,15},{10,... | collective-permute-start | bytes 786440 | tf_op jit(solution)/shard_map/ppermute | solution.py:284
  84.6 18.4 %collective-permute-start.17 = (bf16[128,256]{1,0:T(8,128)(2,1)S(1)}, bf16[128,256]{1,0:T(8,128)(2,1)S(1)}, u32[]{:S(2)}, u32[]{:S(2)}) collective-permute-start(bf16[128,256]{1,0:T(8,128)(2,1)S(1)} %add_convert_fusion.refs_4_), channel_id=1, source_target_pairs={{0,2},{1,3},{2,4},{3,5},{4,6},{5,7},{6,0},{7,1},{8,10},{9,11},{10,... | collective-permute-start | bytes 196616 | tf_op jit(solution)/shard_map/ppermute | solution.py:284
  85.7 25.4 %collective-permute-start.18 = (bf16[128,256]{1,0:T(8,128)(2,1)S(1)}, bf16[128,256]{1,0:T(8,128)(2,1)S(1)}, u32[]{:S(2)}, u32[]{:S(2)}) collective-permute-start(bf16[128,256]{1,0:T(8,128)(2,1)S(1)} %add_convert_fusion.refs_4_), channel_id=1, source_target_pairs={{0,4},{1,5},{2,6},{3,7},{4,0},{5,1},{6,2},{7,3},{8,12},{9,13},{10,... | collective-permute-start | bytes 196616 | tf_op jit(solution)/shard_map/ppermute | solution.py:284
  90.3 20.8 %collective-permute-start.19 = (bf16[128,256]{1,0:T(8,128)(2,1)S(1)}, bf16[128,256]{1,0:T(8,128)(2,1)S(1)}, u32[]{:S(2)}, u32[]{:S(2)}) collective-permute-start(bf16[128,256]{1,0:T(8,128)(2,1)S(1)} %add_convert_fusion.refs_4_), channel_id=1, source_target_pairs={{0,6},{1,7},{2,0},{3,1},{4,2},{5,3},{6,4},{7,5},{8,14},{9,15},{10,... | collective-permute-start | bytes 196616 | tf_op jit(solution)/shard_map/ppermute | solution.py:284
  111.6 1.6 %collective-permute-start.20 = (bf16[512,256]{1,0:T(8,128)(2,1)S(1)}, bf16[512,256]{1,0:T(8,128)(2,1)S(1)}, u32[]{:S(2)}, u32[]{:S(2)}) collective-permute-start(bf16[512,256]{1,0:T(8,128)(2,1)S(1)} %get-tuple-element.19), channel_id=1, source_target_pairs={{0,1},{1,0},{2,3},{3,2},{4,5},{5,4},{6,7},{7,6},{8,9},{9,8},{10,11... | collective-permute-start | bytes 786440 | tf_op jit(solution)/shard_map/ppermute | solution.py:272
  113.3 19.8 %collective-permute-start.21 = (bf16[512,256]{1,0:T(8,128)(2,1)S(1)}, bf16[512,256]{1,0:T(8,128)(2,1)S(1)}, u32[]{:S(2)}, u32[]{:S(2)}) collective-permute-start(bf16[512,256]{1,0:T(8,128)(2,1)S(1)} %fusion), channel_id=1, source_target_pairs={{0,8},{8,16},{16,24},{24,0},{1,9},{9,17},{17,25},{25,1},{2,10},{10... | collective-permute-start | bytes 786440 | tf_op jit(solution)/shard_map/ppermute | solution.py:287
  125.0 13.2 %collective-permute-start.22 = (bf16[512,256]{1,0:T(8,128)(2,1)S(1)}, bf16[512,256]{1,0:T(8,128)(2,1)S(1)}, u32[]{:S(2)}, u32[]{:S(2)}) collective-permute-start(bf16[512,256]{1,0:T(8,128)(2,1)S(1)} %fusion), channel_id=1, source_target_pairs={{0,16},{8,24},{16,0},{24,8},{1,17},{9,25},{17,1},{25,9},{2,18},{10... | collective-permute-start | bytes 786440 | tf_op jit(solution)/shard_map/ppermute | solution.py:287
  126.5 11.7 %collective-permute-start.23 = (bf16[512,256]{1,0:T(8,128)(2,1)S(1)}, bf16[512,256]{1,0:T(8,128)(2,1)S(1)}, u32[]{:S(2)}, u32[]{:S(2)}) collective-permute-start(bf16[512,256]{1,0:T(8,128)(2,1)S(1)} %fusion), channel_id=1, source_target_pairs={{0,24},{8,0},{16,8},{24,16},{1,25},{9,1},{17,9},{25,17},{2,26},{10... | collective-permute-start | bytes 786440 | tf_op jit(solution)/shard_map/ppermute | solution.py:287
  (3 other events, 2.4 us)

commit v2 on v1

v2 whole, which is shorter than its diff:
```python
import math
from functools import partial

import jax
import jax.numpy as jnp
from jax import lax
from jax.experimental import pallas as pl
from jax.experimental.pallas import tpu as pltpu
from jax.sharding import PartitionSpec as P

HEADS = 32
KV_HEADS = 4
HEAD_DIM = 128
BLOCK = 128
GROUP = HEADS // KV_HEADS
UNROLL = 4
CHUNKS = 1
VMEM_ATT = 24 * 1024 * 1024
MASKED = -1e30

bf16 = jnp.bfloat16
f32 = jnp.float32
NT = (((1,), (1,)), ((), ()))
NN = (((1,), (0,)), ((), ()))
TN = (((0,), (0,)), ((), ()))


def mm(a, b, dims=NN):
    return lax.dot_general(a, b, dims, preferred_element_type=f32)


def lists_by_length(layout, place, chips):
    slots = layout.shape[2]
    chip, core = place // 2, lax.rem(place, 2)
    lists = lax.dynamic_slice_in_dim(layout, place, 1, 1)[:, 0]
    length = jnp.sum((lists >= 0).astype(jnp.int32), axis=1)
    spots = (chip - lists // 2) + chips * ((lists + core) % 2)
    earlier = jnp.arange(slots, dtype=jnp.int32)[None] < length[:, None] - 1
    spots = jnp.where(earlier, spots, 0)
    within = jnp.arange(HEADS, dtype=jnp.int32) % GROUP
    table = jnp.concatenate([within[:, None], length[:, None], spots[:, : slots - 1]], axis=1)
    table = table.reshape(KV_HEADS, GROUP, slots + 1)
    size = length.reshape(KV_HEADS, GROUP)
    inside = jnp.arange(GROUP, dtype=jnp.int32)
    mine, others = size[:, :, None], size[:, None, :]
    ahead = (others > mine) | ((others == mine) & (inside[None, None, :] < inside[None, :, None]))
    rank = jnp.sum(ahead.astype(jnp.int32), axis=2)
    chosen = rank[:, :, None] == inside[None, None, :]
    ordered = jnp.sum(jnp.where(chosen[..., None], table[:, :, None, :], 0), axis=1)
    return ordered.reshape(-1)


def attention_kernel(table_ref, q_ref, do_ref, *refs, chips, slots, first, heads):
    count = 2 * chips
    kv_refs, refs = refs[:count], refs[count:]
    dq_ref, grads_ref, kbuf, ktbuf, vbuf, dk_acc, dv_acc = refs
    row = slots + 1
    scale = HEAD_DIM ** (-0.5)
    to_exp2 = scale * math.log2(math.e)
    rows = lax.broadcasted_iota(jnp.int32, (BLOCK, BLOCK), 0)
    columns = lax.broadcasted_iota(jnp.int32, (BLOCK, BLOCK), 1)
    causal = rows <= columns

    def one_kv_head(kv_head):
        k_lane = slice(kv_head * HEAD_DIM, (kv_head + 1) * HEAD_DIM)
        v_lane = slice((heads + kv_head) * HEAD_DIM, (heads + kv_head + 1) * HEAD_DIM)
        for index in range(count):
            block = kv_refs[index][:, k_lane]
            kbuf[index] = block
            ktbuf[index] = block.T
            vbuf[index] = kv_refs[index][:, v_lane]
        dk_acc[...] = jnp.zeros_like(dk_acc)
        dv_acc[...] = jnp.zeros_like(dv_acc)

        def heads_step(step, carry):
            base = ((first + kv_head) * GROUP + step * UNROLL) * row
            most = table_ref[base + 1]

            def work(width):
                units = range(UNROLL)
                lanes_in, lanes_out, spots, valid = [], [], [], []
                for unit in units:
                    start = base + unit * row
                    head = table_ref[start]
                    length = table_ref[start + 1]
                    spots.append([0] + [table_ref[start + 1 + slot] for slot in range(1, width)])
                    valid.append([None] + [slot < length for slot in range(1, width)])
                    at_in = ((first + kv_head) * GROUP + head) * HEAD_DIM
                    at_out = (kv_head * GROUP + head) * HEAD_DIM
                    lanes_in.append(pl.ds(pl.multiple_of(at_in, HEAD_DIM), HEAD_DIM))
                    lanes_out.append(pl.ds(pl.multiple_of(at_out, HEAD_DIM), HEAD_DIM))
                qs = [q_ref[:, lanes_in[unit]] for unit in units]
                dos = [do_ref[:, lanes_in[unit]] for unit in units]
                scores, dweights = [], []
                for unit in units:
                    ks = jnp.concatenate([kbuf[spot] for spot in spots[unit]], axis=0)
                    scores.append(mm(ks, qs[unit], NT))
                for unit in units:
                    vs = jnp.concatenate([vbuf[spot] for spot in spots[unit]], axis=0)
                    dweights.append(mm(vs, dos[unit], NT))
                lows, dlows = [], []
                for unit in units:
                    pieces = []
                    for slot in range(width):
                        piece = scores[unit][slot * BLOCK : (slot + 1) * BLOCK] * to_exp2
                        shown = causal if slot == 0 else valid[unit][slot]
                        pieces.append(jnp.where(shown, piece, MASKED))
                    masked = jnp.concatenate(pieces, axis=0)
                    top = jnp.max(masked, axis=0, keepdims=True)
                    raw = jnp.exp2(masked - top)
                    weights = raw * (1.0 / jnp.sum(raw, axis=0, keepdims=True))
                    delta = jnp.sum(weights * dweights[unit], axis=0, keepdims=True)
                    lows.append(weights.astype(bf16))
                    dlows.append((weights * (dweights[unit] - delta)).astype(bf16))
                for unit in units:
                    kt = jnp.concatenate([ktbuf[spot] for spot in spots[unit]], axis=1)
                    dq_ref[:, lanes_out[unit]] = (mm(kt, dlows[unit]) * scale).astype(bf16).T
                dk_acc[0] += mm(
                    jnp.concatenate([dlow[:BLOCK] for dlow in dlows], axis=1),
                    jnp.concatenate(qs, axis=0),
                )
                dv_acc[0] += mm(
                    jnp.concatenate([low[:BLOCK] for low in lows], axis=1),
                    jnp.concatenate(dos, axis=0),
                )
                if width > 1:
                    for unit in units:
                        dk = mm(dlows[unit][BLOCK:], qs[unit])
                        dv = mm(lows[unit][BLOCK:], dos[unit])
                        for slot in range(1, width):
                            part = slice((slot - 1) * BLOCK, slot * BLOCK)
                            dk_acc[spots[unit][slot]] += dk[part]
                            dv_acc[spots[unit][slot]] += dv[part]

            for width in range(1, slots + 1):
                pl.when(most == width)(partial(work, width))
            return carry

        lax.fori_loop(0, GROUP // UNROLL, heads_step, 0)
        for index in range(count):
            at = slice(index * BLOCK, (index + 1) * BLOCK)
            grads_ref[at, k_lane] = (dk_acc[index] * scale).astype(bf16)
            grads_ref[at, v_lane] = dv_acc[index].astype(bf16)

    for kv_head in range(heads):
        one_kv_head(kv_head)


def attention(table, queries, grads, kv_parts, slots, first, heads):
    count = len(kv_parts)
    body = partial(attention_kernel, chips=count // 2, slots=slots, first=first, heads=heads)
    whole = pl.BlockSpec(memory_space=pltpu.VMEM)
    pairs = heads * GROUP * 3
    return pl.pallas_call(
        body,
        in_specs=[pl.BlockSpec(memory_space=pltpu.SMEM)] + [whole] * (2 + count),
        out_specs=[whole, whole],
        out_shape=[
            jax.ShapeDtypeStruct((BLOCK, heads * GROUP * HEAD_DIM), bf16),
            jax.ShapeDtypeStruct((count * BLOCK, 2 * heads * HEAD_DIM), bf16),
        ],
        scratch_shapes=[
            pltpu.VMEM((count, BLOCK, HEAD_DIM), bf16),
            pltpu.VMEM((count, HEAD_DIM, BLOCK), bf16),
            pltpu.VMEM((count, BLOCK, HEAD_DIM), bf16),
            pltpu.VMEM((count, BLOCK, HEAD_DIM), f32),
            pltpu.VMEM((count, BLOCK, HEAD_DIM), f32),
        ],
        compiler_params=pltpu.CompilerParams(vmem_limit_bytes=VMEM_ATT),
        cost_estimate=pl.CostEstimate(
            flops=pairs * 100 * BLOCK**3, bytes_accessed=4 << 20, transcendentals=pairs * BLOCK**2
        ),
        name="attention_backward",
    )(table, queries, grads, *kv_parts)

def project_kernel(mine_ref, other_ref, *refs, chips, chunks):
    grads_refs, refs = refs[:chunks], refs[chunks:]
    keep_ref, send_ref, basis = refs
    half = mine_ref.shape[0]
    core = lax.rem(lax.axis_index("seq"), 2)

    @pl.when(core == 0)
    def _():
        basis[:half] = mine_ref[...]
        basis[half:] = other_ref[...]

    @pl.when(core == 1)
    def _():
        basis[:half] = other_ref[...]
        basis[half:] = mine_ref[...]

    chosen = basis[...]
    part = grads_refs[0].shape[1] // 2
    tall = min(chips, 4) * BLOCK

    def product(start):
        rows = slice(start, start + tall)
        keys = [ref[rows, :part] for ref in grads_refs]
        values = [ref[rows, part:] for ref in grads_refs]
        return mm(jnp.concatenate(keys + values, axis=1), chosen)

    for start in range(0, chips * BLOCK, tall):
        send_ref[start : start + tall] = product(chips * BLOCK + start).astype(bf16)
        keep_ref[start : start + tall] = product(start)


def project(mine, other, grads, chips):
    rank = mine.shape[1]
    return pl.pallas_call(
        partial(project_kernel, chips=chips, chunks=len(grads)),
        out_shape=[
            jax.ShapeDtypeStruct((chips * BLOCK, rank), f32),
            jax.ShapeDtypeStruct((chips * BLOCK, rank), bf16),
        ],
        scratch_shapes=[pltpu.VMEM((2 * mine.shape[0], rank), bf16)],
        compiler_params=pltpu.CompilerParams(vmem_limit_bytes=32 * 1024 * 1024),
        name="project",
    )(mine, other, *grads)


def fold_kernel(keep_ref, came_ref, own_ref, *send_refs):
    own_ref[...] = keep_ref[:BLOCK] + came_ref[:BLOCK].astype(f32)
    for index, send_ref in enumerate(send_refs):
        rows = slice((index + 1) * BLOCK, (index + 2) * BLOCK)
        send_ref[...] = (keep_ref[rows] + came_ref[rows].astype(f32)).astype(bf16)


def fold(keep, came, chips):
    rank = keep.shape[1]
    return pl.pallas_call(
        fold_kernel,
        out_shape=[jax.ShapeDtypeStruct((BLOCK, rank), f32)]
        + [jax.ShapeDtypeStruct((BLOCK, rank), bf16)] * (chips - 1),
        compiler_params=pltpu.CompilerParams(vmem_limit_bytes=32 * 1024 * 1024),
        name="fold_parts",
    )(keep, came)


def outer_kernel(*refs, chips):
    x_refs, refs = refs[:chips], refs[chips:]
    p_refs, refs = refs[:chips], refs[chips:]
    keep_ref, send_ref = refs
    core = lax.rem(lax.axis_index("seq"), 2)
    half = keep_ref.shape[0]

    def product(which):
        columns = pl.ds(pl.multiple_of(which * half, half), half)
        inputs = jnp.concatenate([ref[:, columns] for ref in x_refs], axis=0)
        projected = jnp.concatenate([ref[...] for ref in p_refs], axis=0)
        return mm(inputs, projected, TN)

    send_ref[...] = product(1 - core).astype(bf16)
    keep_ref[...] = product(core)


def outer(x_parts, p_parts):
    chips = len(x_parts)
    features = x_parts[0].shape[1]
    rank = p_parts[0].shape[1]
    return pl.pallas_call(
        partial(outer_kernel, chips=chips),
        out_shape=[
            jax.ShapeDtypeStruct((features // 2, rank), f32),
            jax.ShapeDtypeStruct((features // 2, rank), bf16),
        ],
        compiler_params=pltpu.CompilerParams(vmem_limit_bytes=32 * 1024 * 1024),
        name="outer_product",
    )(*x_parts, *p_parts)


def local(queries, keys, values, grad_out, layer_input, basis_store, owner, layout):
    seq_count = lax.axis_size("seq")
    dp_count = lax.axis_size("dp")
    chips = seq_count // 2
    place = lax.axis_index("seq")
    chip, core = place // 2, lax.rem(place, 2)
    me = lax.axis_index("dp")
    slots = layout.shape[2]
    rank = basis_store.shape[2]

    def pair(x):
        return lax.ppermute(x, "seq", [(i, i ^ 1) for i in range(seq_count)])

    def up(x, step):
        moves = [(i, i + 2 * step) for i in range(seq_count) if i + 2 * step < seq_count]
        return lax.ppermute(x, "seq", moves)

    def down(x, step):
        moves = [(i, i - 2 * step) for i in range(seq_count) if i >= 2 * step]
        return lax.ppermute(x, "seq", moves)

    def around(x, step):
        moves = [(i, (i + 2 * step) % seq_count) for i in range(seq_count)]
        return lax.ppermute(x, "seq", moves)

    def across(x, step):
        return lax.ppermute(x, "dp", [(i, i ^ step) for i in range(dp_count)])

    heads = KV_HEADS // CHUNKS
    part = heads * HEAD_DIM

    def gathered(chunk):
        columns = slice(chunk * part, (chunk + 1) * part)
        kv = jnp.concatenate([keys[0][:, columns], values[0][:, columns]], axis=1)
        same = [kv] + [up(kv, step) for step in range(1, chips)]
        return same + [pair(piece) for piece in same]

    kv_parts = [gathered(chunk) for chunk in range(CHUNKS)]
    table = lists_by_length(layout, place, chips)

    pieces = KV_HEADS
    half = lax.dynamic_slice_in_dim(basis_store[0], core * pieces * HEAD_DIM, pieces * HEAD_DIM, 0)
    owners = lax.dynamic_slice_in_dim(owner, core * pieces, pieces, 0)
    from_where = (owners ^ me)[:, None, None]
    mine = half.reshape(pieces, HEAD_DIM, rank)
    for step in range(1, dp_count):
        came = across(half, step).reshape(pieces, HEAD_DIM, rank)
        mine = jnp.where(from_where == step, came, mine)
    mine = mine.reshape(pieces * HEAD_DIM, rank)
    other = pair(mine)

    features = layer_input.shape[2] // chips

    def columns(step):
        target = lax.rem(chip + step, chips)
        return lax.dynamic_slice_in_dim(layer_input[0], target * features, features, 1)

    x_parts = [columns(0)] + [around(columns(step), step) for step in range(1, chips)]

    query_grads, grads = [], []
    for chunk in range(CHUNKS):
        query_grad, grad = attention(
            table, queries[0], grad_out[0], kv_parts[chunk], slots, chunk * heads, heads
        )
        query_grads.append(query_grad)
        grads.append(grad)
    grad_query = jnp.concatenate(query_grads, axis=1)

    keep, send = project(mine, other, grads, chips)
    (send, x_parts) = lax.optimization_barrier((send, x_parts))
    own, *sends = fold(keep, pair(send), chips)
    total = own
    for step in range(1, chips):
        total = total + down(sends[step - 1], step).astype(f32)
    projected = total.astype(bf16)
    p_parts = [projected] + [around(projected, step) for step in range(1, chips)]
    kept, sent = outer(x_parts, p_parts)
    partial_rank = kept + pair(sent).astype(f32)
    low = partial_rank.astype(bf16)
    for step in range(1, dp_count):
        partial_rank = partial_rank + across(low, step).astype(f32)
    lowrank_grad = partial_rank / dp_count
    return (grad_query[None], lowrank_grad)


def solution(mesh):
    in_specs = (
        P("dp", "seq", None),
        P("dp", "seq", None),
        P("dp", "seq", None),
        P("dp", "seq", None),
        P("dp", "seq", None),
        P("dp", None, None),
        P(),
        P(),
    )
    out_specs = (P("dp", "seq", None), P("seq", None))
    return jax.shard_map(local, mesh=mesh, in_specs=in_specs, out_specs=out_specs, check_vma=False)
```

time: 140 us -> 97.3 us (0.69)
  starting transfers between devices: 51.4 us -> 34.5 us
  waiting for transfers between devices: 56.6 us -> 41.1 us
  Pallas kernels: 22.7 us -> 9.83 us
  other arithmetic: 2.08 us -> 6.04 us
    ppermute x6, waiting for transfers between devices: 23.2 us -> 8.64 us  [around(): return lax.ppermute(x, 'seq', moves)]
    pallas_call x1 -> x2, Pallas kernels: 22.1 us -> 9.29 us  [the longest x1 8.55 us: attention(): pl.pallas_call(body, in_specs=[pl.BlockSpec(memory_space=pltpu.SMEM)] + [...]
    ppermute x6, starting transfers between devices: 18.7 us -> 7.05 us  [across(): return lax.ppermute(x, 'dp', [(i, i ^ step) for i in range(dp_count)])]
    ppermute x3, waiting for transfers between devices: 0.82 us -> 12 us  [down(): return lax.ppermute(x, 'seq', moves)]
    ppermute x3, waiting for transfers between devices: 7.68 us -> 0.66 us  [up(): return lax.ppermute(x, 'seq', moves)]
    ppermute x6, waiting for transfers between devices: 22 us -> 16.7 us  [across(): return lax.ppermute(x, 'dp', [(i, i ^ step) for i in range(dp_count)])]
    unnamed x23 -> x4, local copies, waits for them, and re-layouts: 3.5 us -> 0.01 us
    ppermute x6, starting transfers between devices: 15.8 us -> 12.6 us  [around(): return lax.ppermute(x, 'seq', moves)]
  transfers between devices with their start and end apart: 24 -> 25, of which waited for: 13 -> 13; matrix products, arithmetic and copies ran while one was open for 2% -> 9% of each run, Pallas kernels for 0% -> 10%
where the time goes in v2:
time: 97.3 us; the launch traced here: 96.9 us
  waiting for transfers between devices  41.1 us (42%)
  starting transfers between devices  34.5 us (35%)
  Pallas kernels  9.83 us (10%)
  other arithmetic  6.04 us (6%)
  local copies, waits for them, and re-layouts  4.52 us (5%)
    ppermute x6, waiting for transfers between devices, across(): return lax.ppermute(x, 'dp', [(i, i ^ step) for i in range(dp_count)])  16.7 us
    ppermute x6, starting transfers between devices, around(): return lax.ppermute(x, 'seq', moves)  12.6 us
    ppermute x3, waiting for transfers between devices, down(): return lax.ppermute(x, 'seq', moves)  12 us
    ppermute x3, starting transfers between devices, up(): return lax.ppermute(x, 'seq', moves)  10.7 us
    ppermute x6, waiting for transfers between devices, around(): return lax.ppermute(x, 'seq', moves)  8.64 us
    pallas_call x1, Pallas kernels, attention(): pl.pallas_call(body, in_specs=[pl.BlockSpec(memory_space=pltpu.SMEM)] + [...  8.55 us
    ppermute x6, starting transfers between devices, across(): return lax.ppermute(x, 'dp', [(i, i ^ step) for i in range(dp_count)])  7.05 us
    ppermute x3, starting transfers between devices, down(): return lax.ppermute(x, 'seq', moves)  3.88 us
  transfers between devices with their start and end apart: 25, of which 13 were waited for; matrix products, arithmetic and copies ran while one was open for 9% of the time, Pallas kernels for 10%

profile of v2, /device:TPU:0, one launch (start us, length us, event | category | flops | bytes accessed | tf_op | source)
XLA Modules:
  0.0 96.9 jit_solution(2603112534713015029)
XLA Ops:
  0.6 1.0 %pad_maximum_fusion.refs_0_ = bf16[128,1024]{1,0:T(8,128)(2,1)S(1)} fusion(bf16[128,512]{1,0:T(8,128)(2,1)} %bitcast.54, bf16[128,512]{1,0:T(8,128)(2,1)} %bitcast.55), kind=kLoop, calls=%fused_computation.3 | loop fusion | flops 524288 | bytes 524288 | tf_op jit(solution)/shard_map/concatenate | solution.py:304
  1.6 4.9 %collective-permute-start = (bf16[128,1024]{1,0:T(8,128)(2,1)S(1)}, bf16[128,1024]{1,0:T(8,128)(2,1)S(1)}, u32[]{:S(2)}, u32[]{:S(2)}) collective-permute-start(bf16[128,1024]{1,0:T(8,128)(2,1)S(1)} %pad_maximum_fusion.refs_0_), channel_id=1, source_target_pairs={{0,2},{1,3},{2,4},{3,5},{4,6},{5,7},{8,10},{9,11},{10,12},{11,13},... | collective-permute-start | bytes 786440 | tf_op jit(solution)/shard_map/ppermute | solution.py:286
  6.6 4.5 %collective-permute-start.1 = (bf16[128,1024]{1,0:T(8,128)(2,1)S(1)}, bf16[128,1024]{1,0:T(8,128)(2,1)S(1)}, u32[]{:S(2)}, u32[]{:S(2)}) collective-permute-start(bf16[128,1024]{1,0:T(8,128)(2,1)S(1)} %pad_maximum_fusion.refs_0_), channel_id=1, source_target_pairs={{0,4},{1,5},{2,6},{3,7},{8,12},{9,13},{10,14},{11,15},{16,20},{17,... | collective-permute-start | bytes 786440 | tf_op jit(solution)/shard_map/ppermute | solution.py:286
  11.1 1.3 %collective-permute-start.2 = (bf16[128,1024]{1,0:T(8,128)(2,1)S(1)}, bf16[128,1024]{1,0:T(8,128)(2,1)S(1)}, u32[]{:S(2)}, u32[]{:S(2)}) collective-permute-start(bf16[128,1024]{1,0:T(8,128)(2,1)S(1)} %pad_maximum_fusion.refs_0_), channel_id=1, source_target_pairs={{0,6},{1,7},{8,14},{9,15},{16,22},{17,23},{24,30},{25,31}} | collective-permute-start | bytes 786440 | tf_op jit(solution)/shard_map/ppermute | solution.py:286
  12.4 1.8 %dynamic-slice_bitcast_fusion.4 = bf16[512,256]{1,0:T(8,128)(2,1)} fusion(bf16[1,1024,256]{2,1,0:T(8,128)(2,1)} %param.13, s32[]{:T(128)S(6)} %select_n.81), kind=kLoop, calls=%fused_computation.9 | loop fusion | bytes 524292 | tf_op jit(solution)/shard_map/dynamic_slice | solution.py:312
  14.3 2.4 %collective-permute-start.7 = (bf16[512,256]{1,0:T(8,128)(2,1)}, bf16[512,256]{1,0:T(8,128)(2,1)}, u32[]{:S(2)}, u32[]{:S(2)}) collective-permute-start(bf16[512,256]{1,0:T(8,128)(2,1)} %dynamic-slice_bitcast_fusion.4), channel_id=1, source_target_pairs={{0,24},{8,16},{16,8},{24,0},{1,25},{9,17},{17,9},{25,1},{2,26},{10... | collective-permute-start | bytes 786440 | tf_op jit(solution)/shard_map/ppermute | solution.py:297
  18.3 0.7 broadcast_compare_fusion.2
  20.6 2.1 %dynamic-slice_bitcast_fusion = (bf16[128,1024]{1,0:T(8,128)(2,1)}, bf16[128,1024]{1,0:T(8,128)(2,1)}, bf16[128,1024]{1,0:T(8,128)(2,1)S(1)}, bf16[128,1024]{1,0:T(8,128)(2,1)}) fusion(bf16[1,128,4096]{2,1,0:T(8,128)(2,1)} %param.12, s32[]{:T(128)S(6)} %select_n.88, s32[]{:T(128)S(6)} %select_n.86, s32[]{:T(128)S(6)} %select_n.85, s32[]{:T(128)S(6)} %select_n.87), kind=kLoop, calls=%fused_computation.4 | loop fusion | bytes 2097168 | tf_op jit(solution)/shard_map/dynamic_slice | solution.py:326
  23.9 4.7 %collective-permute-done.8 = bf16[512,256]{1,0:T(8,128)(2,1)} collective-permute-done((bf16[512,256]{1,0:T(8,128)(2,1)}, bf16[512,256]{1,0:T(8,128)(2,1)}, u32[]{:S(2)}, u32[]{:S(2)}) %collective-permute-start.8) | collective-permute-done | bytes 262176 | tf_op jit(solution)/shard_map/ppermute | solution.py:297
  28.9 3.8 %collective-permute-start.11 = (bf16[128,1024]{1,0:T(8,128)(2,1)}, bf16[128,1024]{1,0:T(8,128)(2,1)S(1)}, u32[]{:S(2)}, u32[]{:S(2)}) collective-permute-start(bf16[128,1024]{1,0:T(8,128)(2,1)} %get-tuple-element.35), channel_id=1, source_target_pairs={{0,2},{1,3},{2,4},{3,5},{4,6},{5,7},{6,0},{7,1},{8,10},{9,11},{10,... | collective-permute-start | bytes 786440 | tf_op jit(solution)/shard_map/ppermute | solution.py:294
  32.8 1.5 %select_select_fusion.mine_ref = bf16[512,256]{1,0:T(8,128)(2,1)S(1)} fusion(bf16[512,256]{1,0:T(8,128)(2,1)} %collective-permute-done.7, bf16[512,256]{1,0:T(8,128)(2,1)} %collective-permute-done.8, bf16[512,256]{1,0:T(8,128)(2,1)} %collective-permute-done.9, pred[512]{0:T(512)(128)(4,1)S(1)} %get-tuple-element.40, pred[512]{0:T(512)(128)(4,1)S(1)} %get-tuple-element.41, ...), kind=kLoop, calls=%fused_computation.8 | loop fusion | flops 393216 | bytes 1312260 | tf_op jit(solution)/shard_map/jit(_where)/select_n | solution.py:318
  34.2 2.6 %collective-permute-start.12 = (bf16[128,1024]{1,0:T(8,128)(2,1)}, bf16[128,1024]{1,0:T(8,128)(2,1)S(1)}, u32[]{:S(2)}, u32[]{:S(2)}) collective-permute-start(bf16[128,1024]{1,0:T(8,128)(2,1)} %get-tuple-element.37), channel_id=1, source_target_pairs={{0,4},{1,5},{2,6},{3,7},{4,0},{5,1},{6,2},{7,3},{8,12},{9,13},{10,... | collective-permute-start | bytes 786440 | tf_op jit(solution)/shard_map/ppermute | solution.py:294
  36.9 2.3 %collective-permute-start.13 = (bf16[128,1024]{1,0:T(8,128)(2,1)}, bf16[128,1024]{1,0:T(8,128)(2,1)S(1)}, u32[]{:S(2)}, u32[]{:S(2)}) collective-permute-start(bf16[128,1024]{1,0:T(8,128)(2,1)} %get-tuple-element.34), channel_id=1, source_target_pairs={{0,6},{1,7},{2,0},{3,1},{4,2},{5,3},{6,4},{7,5},{8,14},{9,15},{10,... | collective-permute-start | bytes 786440 | tf_op jit(solution)/shard_map/ppermute | solution.py:294
  39.2 8.5 %attention_backward.1 = (bf16[128,4096]{1,0:T(8,128)(2,1)}, bf16[1024,1024]{1,0:T(8,128)(2,1)S(1)}) custom-call(s32[160]{0:T(256)S(1)} %reshape.105.table_ref, bf16[128,4096]{1,0:T(8,128)(2,1)S(1)} %bitcast.52, bf16[128,4096]{1,0:T(8,128)(2,1)S(1)} %bitcast.53, bf16[128,1024]{1,0:T(8,128)(2,1)S(1)} %pad_maximum_fusion.refs_0_, ...), custom_call_target="tpu_custom_call" | custom-call | flops 20132659200 | bytes 4194304 | tf_op jit(solution)/shard_map/attention_backward/pallas_call | solution.py:154
  47.7 0.7 project.1
  48.5 4.4 %collective-permute-done.12.refs_2_ = bf16[128,1024]{1,0:T(8,128)(2,1)S(1)} collective-permute-done((bf16[128,1024]{1,0:T(8,128)(2,1)}, bf16[128,1024]{1,0:T(8,128)(2,1)S(1)}, u32[]{:S(2)}, u32[]{:S(2)}) %collective-permute-start.12) | collective-permute-done | bytes 262176 | tf_op jit(solution)/shard_map/ppermute | solution.py:294
  52.9 1.5 %collective-permute-done.14.came_ref = bf16[512,256]{1,0:T(8,128)(2,1)S(1)} collective-permute-done((bf16[512,256]{1,0:T(8,128)(2,1)S(1)}, bf16[512,256]{1,0:T(8,128)(2,1)S(1)}, u32[]{:S(2)}, u32[]{:S(2)}) %collective-permute-start.14) | collective-permute-done | bytes 262176 | tf_op jit(solution)/shard_map/ppermute | solution.py:282
  54.5 1.3 %collective-permute-start.15 = (bf16[128,256]{1,0:T(8,128)(2,1)S(1)}, bf16[128,256]{1,0:T(8,128)(2,1)S(1)}, u32[]{:S(2)}, u32[]{:S(2)}) collective-permute-start(bf16[128,256]{1,0:T(8,128)(2,1)S(1)} %get-tuple-element.27), channel_id=1, source_target_pairs={{2,0},{3,1},{4,2},{5,3},{6,4},{7,5},{10,8},{11,9},{12,10},{13,11},... | collective-permute-start | bytes 196616 | tf_op jit(solution)/shard_map/ppermute | solution.py:290
  55.8 1.3 %collective-permute-start.16 = (bf16[128,256]{1,0:T(8,128)(2,1)S(1)}, bf16[128,256]{1,0:T(8,128)(2,1)S(1)}, u32[]{:S(2)}, u32[]{:S(2)}) collective-permute-start(bf16[128,256]{1,0:T(8,128)(2,1)S(1)} %get-tuple-element.28), channel_id=1, source_target_pairs={{4,0},{5,1},{6,2},{7,3},{12,8},{13,9},{14,10},{15,11},{20,16},{21,... | collective-permute-start | bytes 196616 | tf_op jit(solution)/shard_map/ppermute | solution.py:290
  57.1 1.3 %collective-permute-start.17 = (bf16[128,256]{1,0:T(8,128)(2,1)S(1)}, bf16[128,256]{1,0:T(8,128)(2,1)S(1)}, u32[]{:S(2)}, u32[]{:S(2)}) collective-permute-start(bf16[128,256]{1,0:T(8,128)(2,1)S(1)} %get-tuple-element.29), channel_id=1, source_target_pairs={{6,0},{7,1},{14,8},{15,9},{22,16},{23,17},{30,24},{31,25}} | collective-permute-start | bytes 196616 | tf_op jit(solution)/shard_map/ppermute | solution.py:290
  58.4 6.5 %collective-permute-done.15 = bf16[128,256]{1,0:T(8,128)(2,1)S(1)} collective-permute-done((bf16[128,256]{1,0:T(8,128)(2,1)S(1)}, bf16[128,256]{1,0:T(8,128)(2,1)S(1)}, u32[]{:S(2)}, u32[]{:S(2)}) %collective-permute-start.15) | collective-permute-done | bytes 65568 | tf_op jit(solution)/shard_map/ppermute | solution.py:290
  64.9 3.4 %collective-permute-done.16 = bf16[128,256]{1,0:T(8,128)(2,1)S(1)} collective-permute-done((bf16[128,256]{1,0:T(8,128)(2,1)S(1)}, bf16[128,256]{1,0:T(8,128)(2,1)S(1)}, u32[]{:S(2)}, u32[]{:S(2)}) %collective-permute-start.16) | collective-permute-done | bytes 65568 | tf_op jit(solution)/shard_map/ppermute | solution.py:290
  68.3 2.1 %collective-permute-done.17 = bf16[128,256]{1,0:T(8,128)(2,1)S(1)} collective-permute-done((bf16[128,256]{1,0:T(8,128)(2,1)S(1)}, bf16[128,256]{1,0:T(8,128)(2,1)S(1)}, u32[]{:S(2)}, u32[]{:S(2)}) %collective-permute-start.17) | collective-permute-done | bytes 65568 | tf_op jit(solution)/shard_map/ppermute | solution.py:290
  70.6 3.7 %collective-permute-start.20 = (bf16[128,256]{1,0:T(8,128)(2,1)S(1)}, bf16[128,256]{1,0:T(8,128)(2,1)S(1)}, u32[]{:S(2)}, u32[]{:S(2)}) collective-permute-start(bf16[128,256]{1,0:T(8,128)(2,1)S(1)} %add_convert_fusion.refs_4_), channel_id=1, source_target_pairs={{0,6},{1,7},{2,0},{3,1},{4,2},{5,3},{6,4},{7,5},{8,14},{9,15},{10,... | collective-permute-start | bytes 196616 | tf_op jit(solution)/shard_map/ppermute | solution.py:294
  74.3 2.9 %collective-permute-done.18.refs_5_ = bf16[128,256]{1,0:T(8,128)(2,1)S(1)} collective-permute-done((bf16[128,256]{1,0:T(8,128)(2,1)S(1)}, bf16[128,256]{1,0:T(8,128)(2,1)S(1)}, u32[]{:S(2)}, u32[]{:S(2)}) %collective-permute-start.18) | collective-permute-done | bytes 65568 | tf_op jit(solution)/shard_map/ppermute | solution.py:294
  77.2 1.3 %collective-permute-done.19.refs_6_ = bf16[128,256]{1,0:T(8,128)(2,1)S(1)} collective-permute-done((bf16[128,256]{1,0:T(8,128)(2,1)S(1)}, bf16[128,256]{1,0:T(8,128)(2,1)S(1)}, u32[]{:S(2)}, u32[]{:S(2)}) %collective-permute-start.19) | collective-permute-done | bytes 65568 | tf_op jit(solution)/shard_map/ppermute | solution.py:294
  79.1 1.5 %collective-permute-done.21 = bf16[512,256]{1,0:T(8,128)(2,1)S(1)} collective-permute-done((bf16[512,256]{1,0:T(8,128)(2,1)S(1)}, bf16[512,256]{1,0:T(8,128)(2,1)S(1)}, u32[]{:S(2)}, u32[]{:S(2)}) %collective-permute-start.21) | collective-permute-done | bytes 262176 | tf_op jit(solution)/shard_map/ppermute | solution.py:282
  80.7 1.6 %collective-permute-start.22 = (bf16[512,256]{1,0:T(8,128)(2,1)S(1)}, bf16[512,256]{1,0:T(8,128)(2,1)S(1)}, u32[]{:S(2)}, u32[]{:S(2)}) collective-permute-start(bf16[512,256]{1,0:T(8,128)(2,1)S(1)} %fusion), channel_id=1, source_target_pairs={{0,8},{8,0},{16,24},{24,16},{1,9},{9,1},{17,25},{25,17},{2,10},{10... | collective-permute-start | bytes 786440 | tf_op jit(solution)/shard_map/ppermute | solution.py:297
  82.2 1.5 %collective-permute-start.23 = (bf16[512,256]{1,0:T(8,128)(2,1)S(1)}, bf16[512,256]{1,0:T(8,128)(2,1)S(1)}, u32[]{:S(2)}, u32[]{:S(2)}) collective-permute-start(bf16[512,256]{1,0:T(8,128)(2,1)S(1)} %fusion), channel_id=1, source_target_pairs={{0,16},{8,24},{16,0},{24,8},{1,17},{9,25},{17,1},{25,9},{2,18},{10... | collective-permute-start | bytes 786440 | tf_op jit(solution)/shard_map/ppermute | solution.py:297
  84.2 5.7 %collective-permute-done.22 = bf16[512,256]{1,0:T(8,128)(2,1)S(1)} collective-permute-done((bf16[512,256]{1,0:T(8,128)(2,1)S(1)}, bf16[512,256]{1,0:T(8,128)(2,1)S(1)}, u32[]{:S(2)}, u32[]{:S(2)}) %collective-permute-start.22) | collective-permute-done | bytes 262176 | tf_op jit(solution)/shard_map/ppermute | solution.py:297
  89.9 6.0 %collective-permute-done.23 = bf16[512,256]{1,0:T(8,128)(2,1)S(1)} collective-permute-done((bf16[512,256]{1,0:T(8,128)(2,1)S(1)}, bf16[512,256]{1,0:T(8,128)(2,1)S(1)}, u32[]{:S(2)}, u32[]{:S(2)}) %collective-permute-start.23) | collective-permute-done | bytes 262176 | tf_op jit(solution)/shard_map/ppermute | solution.py:297
  95.9 1.0 add_multiply_fusion
  (52 shorter events, 6.1 us)
Async XLA Ops:
  1.6 18.4 %collective-permute-start = (bf16[128,1024]{1,0:T(8,128)(2,1)S(1)}, bf16[128,1024]{1,0:T(8,128)(2,1)S(1)}, u32[]{:S(2)}, u32[]{:S(2)}) collective-permute-start(bf16[128,1024]{1,0:T(8,128)(2,1)S(1)} %pad_maximum_fusion.refs_0_), channel_id=1, source_target_pairs={{0,2},{1,3},{2,4},{3,5},{4,6},{5,7},{8,10},{9,11},{10,12},{11,13},... | collective-permute-start | bytes 786440 | tf_op jit(solution)/shard_map/ppermute | solution.py:286
  6.6 16.1 %collective-permute-start.1 = (bf16[128,1024]{1,0:T(8,128)(2,1)S(1)}, bf16[128,1024]{1,0:T(8,128)(2,1)S(1)}, u32[]{:S(2)}, u32[]{:S(2)}) collective-permute-start(bf16[128,1024]{1,0:T(8,128)(2,1)S(1)} %pad_maximum_fusion.refs_0_), channel_id=1, source_target_pairs={{0,4},{1,5},{2,6},{3,7},{8,12},{9,13},{10,14},{11,15},{16,20},{17,... | collective-permute-start | bytes 786440 | tf_op jit(solution)/shard_map/ppermute | solution.py:286
  11.1 12.3 %collective-permute-start.2 = (bf16[128,1024]{1,0:T(8,128)(2,1)S(1)}, bf16[128,1024]{1,0:T(8,128)(2,1)S(1)}, u32[]{:S(2)}, u32[]{:S(2)}) collective-permute-start(bf16[128,1024]{1,0:T(8,128)(2,1)S(1)} %pad_maximum_fusion.refs_0_), channel_id=1, source_target_pairs={{0,6},{1,7},{8,14},{9,15},{16,22},{17,23},{24,30},{25,31}} | collective-permute-start | bytes 786440 | tf_op jit(solution)/shard_map/ppermute | solution.py:286
  12.4 26.7 %copy-start = (bf16[1,128,4096]{2,1,0:T(8,128)(2,1)S(1)}, bf16[1,128,4096]{2,1,0:T(8,128)(2,1)}, u32[]{:S(2)}) copy-start(bf16[1,128,4096]{2,1,0:T(8,128)(2,1)} %param.8) | copy-start | bytes 3145732
  12.4 26.7 %copy-start.1 = (bf16[1,128,4096]{2,1,0:T(8,128)(2,1)S(1)}, bf16[1,128,4096]{2,1,0:T(8,128)(2,1)}, u32[]{:S(2)}) copy-start(bf16[1,128,4096]{2,1,0:T(8,128)(2,1)} %param.11) | copy-start | bytes 3145732
  14.3 9.5 %collective-permute-start.7 = (bf16[512,256]{1,0:T(8,128)(2,1)}, bf16[512,256]{1,0:T(8,128)(2,1)}, u32[]{:S(2)}, u32[]{:S(2)}) collective-permute-start(bf16[512,256]{1,0:T(8,128)(2,1)} %dynamic-slice_bitcast_fusion.4), channel_id=1, source_target_pairs={{0,24},{8,16},{16,8},{24,0},{1,25},{9,17},{17,9},{25,1},{2,26},{10... | collective-permute-start | bytes 786440 | tf_op jit(solution)/shard_map/ppermute | solution.py:297
  16.7 11.9 %collective-permute-start.8 = (bf16[512,256]{1,0:T(8,128)(2,1)}, bf16[512,256]{1,0:T(8,128)(2,1)}, u32[]{:S(2)}, u32[]{:S(2)}) collective-permute-start(bf16[512,256]{1,0:T(8,128)(2,1)} %dynamic-slice_bitcast_fusion.4), channel_id=1, source_target_pairs={{0,16},{8,24},{16,0},{24,8},{1,17},{9,25},{17,1},{25,9},{2,18},{10... | collective-permute-start | bytes 786440 | tf_op jit(solution)/shard_map/ppermute | solution.py:297
  20.1 8.8 %collective-permute-start.9 = (bf16[512,256]{1,0:T(8,128)(2,1)}, bf16[512,256]{1,0:T(8,128)(2,1)}, u32[]{:S(2)}, u32[]{:S(2)}) collective-permute-start(bf16[512,256]{1,0:T(8,128)(2,1)} %dynamic-slice_bitcast_fusion.4), channel_id=1, source_target_pairs={{0,8},{8,0},{16,24},{24,16},{1,9},{9,1},{17,25},{25,17},{2,10},{10... | collective-permute-start | bytes 786440 | tf_op jit(solution)/shard_map/ppermute | solution.py:297
  22.7 11.5 %collective-permute-start.3 = (bf16[128,1024]{1,0:T(8,128)(2,1)S(1)}, bf16[128,1024]{1,0:T(8,128)(2,1)}, u32[]{:S(2)}, u32[]{:S(2)}) collective-permute-start(bf16[128,1024]{1,0:T(8,128)(2,1)S(1)} %pad_maximum_fusion.refs_0_), channel_id=1, source_target_pairs={{0,1},{1,0},{2,3},{3,2},{4,5},{5,4},{6,7},{7,6},{8,9},{9,8},{10,11... | collective-permute-start | bytes 786440 | tf_op jit(solution)/shard_map/ppermute | solution.py:282
  23.4 13.5 %collective-permute-start.4 = (bf16[128,1024]{1,0:T(8,128)(2,1)S(1)}, bf16[128,1024]{1,0:T(8,128)(2,1)}, u32[]{:S(2)}, u32[]{:S(2)}) collective-permute-start(bf16[128,1024]{1,0:T(8,128)(2,1)S(1)} %collective-permute-done.refs_1_), channel_id=1, source_target_pairs={{0,1},{1,0},{2,3},{3,2},{4,5},{5,4},{6,7},{7,6},{8,9},{9,8},{10,11... | collective-permute-start | bytes 786440 | tf_op jit(solution)/shard_map/ppermute | solution.py:282
  23.8 15.4 %collective-permute-start.5 = (bf16[128,1024]{1,0:T(8,128)(2,1)S(1)}, bf16[128,1024]{1,0:T(8,128)(2,1)}, u32[]{:S(2)}, u32[]{:S(2)}) collective-permute-start(bf16[128,1024]{1,0:T(8,128)(2,1)S(1)} %collective-permute-done.1.refs_2_), channel_id=1, source_target_pairs={{0,1},{1,0},{2,3},{3,2},{4,5},{5,4},{6,7},{7,6},{8,9},{9,8},{10,11... | collective-permute-start | bytes 786440 | tf_op jit(solution)/shard_map/ppermute | solution.py:282
  28.6 10.6 %collective-permute-start.6 = (bf16[128,1024]{1,0:T(8,128)(2,1)S(1)}, bf16[128,1024]{1,0:T(8,128)(2,1)}, u32[]{:S(2)}, u32[]{:S(2)}) collective-permute-start(bf16[128,1024]{1,0:T(8,128)(2,1)S(1)} %collective-permute-done.2.refs_3_), channel_id=1, source_target_pairs={{0,1},{1,0},{2,3},{3,2},{4,5},{5,4},{6,7},{7,6},{8,9},{9,8},{10,11... | collective-permute-start | bytes 786440 | tf_op jit(solution)/shard_map/ppermute | solution.py:282
  28.9 19.6 %collective-permute-start.11 = (bf16[128,1024]{1,0:T(8,128)(2,1)}, bf16[128,1024]{1,0:T(8,128)(2,1)S(1)}, u32[]{:S(2)}, u32[]{:S(2)}) collective-permute-start(bf16[128,1024]{1,0:T(8,128)(2,1)} %get-tuple-element.35), channel_id=1, source_target_pairs={{0,2},{1,3},{2,4},{3,5},{4,6},{5,7},{6,0},{7,1},{8,10},{9,11},{10,... | collective-permute-start | bytes 786440 | tf_op jit(solution)/shard_map/ppermute | solution.py:294
  34.2 18.7 %collective-permute-start.12 = (bf16[128,1024]{1,0:T(8,128)(2,1)}, bf16[128,1024]{1,0:T(8,128)(2,1)S(1)}, u32[]{:S(2)}, u32[]{:S(2)}) collective-permute-start(bf16[128,1024]{1,0:T(8,128)(2,1)} %get-tuple-element.37), channel_id=1, source_target_pairs={{0,4},{1,5},{2,6},{3,7},{4,0},{5,1},{6,2},{7,3},{8,12},{9,13},{10,... | collective-permute-start | bytes 786440 | tf_op jit(solution)/shard_map/ppermute | solution.py:294
  36.9 16.0 %collective-permute-start.13 = (bf16[128,1024]{1,0:T(8,128)(2,1)}, bf16[128,1024]{1,0:T(8,128)(2,1)S(1)}, u32[]{:S(2)}, u32[]{:S(2)}) collective-permute-start(bf16[128,1024]{1,0:T(8,128)(2,1)} %get-tuple-element.34), channel_id=1, source_target_pairs={{0,6},{1,7},{2,0},{3,1},{4,2},{5,3},{6,4},{7,5},{8,14},{9,15},{10,... | collective-permute-start | bytes 786440 | tf_op jit(solution)/shard_map/ppermute | solution.py:294
  39.1 8.6 %collective-permute-start.10 = (bf16[512,256]{1,0:T(8,128)(2,1)S(1)}, bf16[512,256]{1,0:T(8,128)(2,1)S(1)}, u32[]{:S(2)}, u32[]{:S(2)}) collective-permute-start(bf16[512,256]{1,0:T(8,128)(2,1)S(1)} %select_select_fusion.mine_ref), channel_id=1, source_target_pairs={{0,1},{1,0},{2,3},{3,2},{4,5},{5,4},{6,7},{7,6},{8,9},{9,8},{10,11... | collective-permute-start | bytes 786440 | tf_op jit(solution)/shard_map/ppermute | solution.py:282
  52.9 1.5 %collective-permute-start.14 = (bf16[512,256]{1,0:T(8,128)(2,1)S(1)}, bf16[512,256]{1,0:T(8,128)(2,1)S(1)}, u32[]{:S(2)}, u32[]{:S(2)}) collective-permute-start(bf16[512,256]{1,0:T(8,128)(2,1)S(1)} %get-tuple-element.25), channel_id=1, source_target_pairs={{0,1},{1,0},{2,3},{3,2},{4,5},{5,4},{6,7},{7,6},{8,9},{9,8},{10,11... | collective-permute-start | bytes 786440 | tf_op jit(solution)/shard_map/ppermute | solution.py:282
  54.5 10.4 %collective-permute-start.15 = (bf16[128,256]{1,0:T(8,128)(2,1)S(1)}, bf16[128,256]{1,0:T(8,128)(2,1)S(1)}, u32[]{:S(2)}, u32[]{:S(2)}) collective-permute-start(bf16[128,256]{1,0:T(8,128)(2,1)S(1)} %get-tuple-element.27), channel_id=1, source_target_pairs={{2,0},{3,1},{4,2},{5,3},{6,4},{7,5},{10,8},{11,9},{12,10},{13,11},... | collective-permute-start | bytes 196616 | tf_op jit(solution)/shard_map/ppermute | solution.py:290
  55.8 12.5 %collective-permute-start.16 = (bf16[128,256]{1,0:T(8,128)(2,1)S(1)}, bf16[128,256]{1,0:T(8,128)(2,1)S(1)}, u32[]{:S(2)}, u32[]{:S(2)}) collective-permute-start(bf16[128,256]{1,0:T(8,128)(2,1)S(1)} %get-tuple-element.28), channel_id=1, source_target_pairs={{4,0},{5,1},{6,2},{7,3},{12,8},{13,9},{14,10},{15,11},{20,16},{21,... | collective-permute-start | bytes 196616 | tf_op jit(solution)/shard_map/ppermute | solution.py:290
  57.1 13.3 %collective-permute-start.17 = (bf16[128,256]{1,0:T(8,128)(2,1)S(1)}, bf16[128,256]{1,0:T(8,128)(2,1)S(1)}, u32[]{:S(2)}, u32[]{:S(2)}) collective-permute-start(bf16[128,256]{1,0:T(8,128)(2,1)S(1)} %get-tuple-element.29), channel_id=1, source_target_pairs={{6,0},{7,1},{14,8},{15,9},{22,16},{23,17},{30,24},{31,25}} | collective-permute-start | bytes 196616 | tf_op jit(solution)/shard_map/ppermute | solution.py:290
  70.4 6.8 %collective-permute-start.18 = (bf16[128,256]{1,0:T(8,128)(2,1)S(1)}, bf16[128,256]{1,0:T(8,128)(2,1)S(1)}, u32[]{:S(2)}, u32[]{:S(2)}) collective-permute-start(bf16[128,256]{1,0:T(8,128)(2,1)S(1)} %add_convert_fusion.refs_4_), channel_id=1, source_target_pairs={{0,2},{1,3},{2,4},{3,5},{4,6},{5,7},{6,0},{7,1},{8,10},{9,11},{10,... | collective-permute-start | bytes 196616 | tf_op jit(solution)/shard_map/ppermute | solution.py:294
  70.5 8.0 %collective-permute-start.19 = (bf16[128,256]{1,0:T(8,128)(2,1)S(1)}, bf16[128,256]{1,0:T(8,128)(2,1)S(1)}, u32[]{:S(2)}, u32[]{:S(2)}) collective-permute-start(bf16[128,256]{1,0:T(8,128)(2,1)S(1)} %add_convert_fusion.refs_4_), channel_id=1, source_target_pairs={{0,4},{1,5},{2,6},{3,7},{4,0},{5,1},{6,2},{7,3},{8,12},{9,13},{10,... | collective-permute-start | bytes 196616 | tf_op jit(solution)/shard_map/ppermute | solution.py:294
  70.6 7.9 %collective-permute-start.20 = (bf16[128,256]{1,0:T(8,128)(2,1)S(1)}, bf16[128,256]{1,0:T(8,128)(2,1)S(1)}, u32[]{:S(2)}, u32[]{:S(2)}) collective-permute-start(bf16[128,256]{1,0:T(8,128)(2,1)S(1)} %add_convert_fusion.refs_4_), channel_id=1, source_target_pairs={{0,6},{1,7},{2,0},{3,1},{4,2},{5,3},{6,4},{7,5},{8,14},{9,15},{10,... | collective-permute-start | bytes 196616 | tf_op jit(solution)/shard_map/ppermute | solution.py:294
  79.0 1.6 %collective-permute-start.21 = (bf16[512,256]{1,0:T(8,128)(2,1)S(1)}, bf16[512,256]{1,0:T(8,128)(2,1)S(1)}, u32[]{:S(2)}, u32[]{:S(2)}) collective-permute-start(bf16[512,256]{1,0:T(8,128)(2,1)S(1)} %get-tuple-element.31), channel_id=1, source_target_pairs={{0,1},{1,0},{2,3},{3,2},{4,5},{5,4},{6,7},{7,6},{8,9},{9,8},{10,11... | collective-permute-start | bytes 786440 | tf_op jit(solution)/shard_map/ppermute | solution.py:282
  80.7 9.2 %collective-permute-start.22 = (bf16[512,256]{1,0:T(8,128)(2,1)S(1)}, bf16[512,256]{1,0:T(8,128)(2,1)S(1)}, u32[]{:S(2)}, u32[]{:S(2)}) collective-permute-start(bf16[512,256]{1,0:T(8,128)(2,1)S(1)} %fusion), channel_id=1, source_target_pairs={{0,8},{8,0},{16,24},{24,16},{1,9},{9,1},{17,25},{25,17},{2,10},{10... | collective-permute-start | bytes 786440 | tf_op jit(solution)/shard_map/ppermute | solution.py:297
  82.2 13.7 %collective-permute-start.23 = (bf16[512,256]{1,0:T(8,128)(2,1)S(1)}, bf16[512,256]{1,0:T(8,128)(2,1)S(1)}, u32[]{:S(2)}, u32[]{:S(2)}) collective-permute-start(bf16[512,256]{1,0:T(8,128)(2,1)S(1)} %fusion), channel_id=1, source_target_pairs={{0,16},{8,24},{16,0},{24,8},{1,17},{9,25},{17,1},{25,9},{2,18},{10... | collective-permute-start | bytes 786440 | tf_op jit(solution)/shard_map/ppermute | solution.py:297
  83.8 12.2 %collective-permute-start.24 = (bf16[512,256]{1,0:T(8,128)(2,1)S(1)}, bf16[512,256]{1,0:T(8,128)(2,1)S(1)}, u32[]{:S(2)}, u32[]{:S(2)}) collective-permute-start(bf16[512,256]{1,0:T(8,128)(2,1)S(1)} %fusion), channel_id=1, source_target_pairs={{0,24},{8,16},{16,8},{24,0},{1,25},{9,17},{17,9},{25,1},{2,26},{10... | collective-permute-start | bytes 786440 | tf_op jit(solution)/shard_map/ppermute | solution.py:297

commit v3 on v2

--- a/solution.py
+++ b/solution.py
@@ -14,7 +14,7 @@
 BLOCK = 128
 GROUP = HEADS // KV_HEADS
 UNROLL = 4
-CHUNKS = 1
+CHUNKS = 2
 VMEM_ATT = 24 * 1024 * 1024
 MASKED = -1e30
 
@@ -236,36 +236,81 @@
     )(keep, came)
 
 
-def outer_kernel(*refs, chips):
-    x_refs, refs = refs[:chips], refs[chips:]
-    p_refs, refs = refs[:chips], refs[chips:]
+def outer_kernel(x_ref, *refs, dp_count):
+    p_refs, refs = refs[:dp_count], refs[dp_count:]
     keep_ref, send_ref = refs
     core = lax.rem(lax.axis_index("seq"), 2)
+    me = lax.axis_index("dp")
     half = keep_ref.shape[0]
+    projected = jnp.concatenate([ref[...] for ref in p_refs], axis=0)
 
     def product(which):
         columns = pl.ds(pl.multiple_of(which * half, half), half)
-        inputs = jnp.concatenate([ref[:, columns] for ref in x_refs], axis=0)
-        projected = jnp.concatenate([ref[...] for ref in p_refs], axis=0)
-        return mm(inputs, projected, TN)
+        inputs = [x_ref[jnp.bitwise_xor(me, step), :, columns] for step in range(dp_count)]
+        return mm(jnp.concatenate(inputs, axis=0), projected, TN)
 
     send_ref[...] = product(1 - core).astype(bf16)
     keep_ref[...] = product(core)
 
 
-def outer(x_parts, p_parts):
-    chips = len(x_parts)
-    features = x_parts[0].shape[1]
+def outer(x_all, p_parts):
+    features = x_all.shape[2]
     rank = p_parts[0].shape[1]
     return pl.pallas_call(
-        partial(outer_kernel, chips=chips),
+        partial(outer_kernel, dp_count=len(p_parts)),
         out_shape=[
             jax.ShapeDtypeStruct((features // 2, rank), f32),
             jax.ShapeDtypeStruct((features // 2, rank), bf16),
         ],
         compiler_params=pltpu.CompilerParams(vmem_limit_bytes=32 * 1024 * 1024),
         name="outer_product",
-    )(*x_parts, *p_parts)
+    )(x_all, *p_parts)
+
+
+def deal_kernel(keep_ref, came_ref, own_ref, *refs):
+    send_refs, total = refs[:-1], refs[-1]
+    chips = len(send_refs) + 1
+    chip = lax.axis_index("seq") // 2
+    share = own_ref.shape[0]
+    total[...] = keep_ref[...] + came_ref[...].astype(f32)
+
+    def rows(step):
+        return pl.ds(pl.multiple_of(lax.rem(chip + step, chips) * share, share), share)
+
+    own_ref[...] = total[rows(0)]
+    for step, send_ref in enumerate(send_refs, 1):
+        send_ref[...] = total[rows(step)].astype(bf16)
+
+
+def deal(keep, came, chips):
+    share, rank = keep.shape[0] // chips, keep.shape[1]
+    return pl.pallas_call(
+        deal_kernel,
+        out_shape=[jax.ShapeDtypeStruct((share, rank), f32)]
+        + [jax.ShapeDtypeStruct((share, rank), bf16)] * (chips - 1),
+        scratch_shapes=[pltpu.VMEM(keep.shape, f32)],
+        compiler_params=pltpu.CompilerParams(vmem_limit_bytes=32 * 1024 * 1024),
+        name="deal_rows",
+    )(keep, came)
+
+
+def lay_kernel(*refs):
+    part_refs, out_ref = refs[:-1], refs[-1]
+    me = lax.axis_index("dp")
+    share = part_refs[0].shape[0]
+    for step, part_ref in enumerate(part_refs):
+        at = pl.multiple_of(jnp.bitwise_xor(me, step) * share, share)
+        out_ref[pl.ds(at, share)] = part_ref[...].astype(f32) * (1.0 / len(part_refs))
+
+
+def lay(parts):
+    share, rank = parts[0].shape
+    return pl.pallas_call(
+        lay_kernel,
+        out_shape=jax.ShapeDtypeStruct((share * len(parts), rank), f32),
+        compiler_params=pltpu.CompilerParams(vmem_limit_bytes=32 * 1024 * 1024),
+        name="lay_rows",
+    )(*parts)
 
 
 def local(queries, keys, values, grad_out, layer_input, basis_store, owner, layout):
@@ -299,13 +344,20 @@
     heads = KV_HEADS // CHUNKS
     part = heads * HEAD_DIM
 
-    def gathered(chunk):
+    def packed(chunk):
         columns = slice(chunk * part, (chunk + 1) * part)
-        kv = jnp.concatenate([keys[0][:, columns], values[0][:, columns]], axis=1)
-        same = [kv] + [up(kv, step) for step in range(1, chips)]
-        return same + [pair(piece) for piece in same]
-
-    kv_parts = [gathered(chunk) for chunk in range(CHUNKS)]
+        return jnp.concatenate([keys[0][:, columns], values[0][:, columns]], axis=1)
+
+    arrived = []
+    for chunk in range(CHUNKS):
+        kv = packed(chunk)
+        same = [kv]
+        for step in range(1, chips):
+            if chunk and step == 2:
+                kv, arrived[chunk - 1] = lax.optimization_barrier((kv, arrived[chunk - 1]))
+            same.append(up(kv, step))
+        arrived.append(same)
+    beside = [pair(same[0]) for same in arrived]
     table = lists_by_length(layout, place, chips)
 
     pieces = KV_HEADS
@@ -313,43 +365,45 @@
     owners = lax.dynamic_slice_in_dim(owner, core * pieces, pieces, 0)
     from_where = (owners ^ me)[:, None, None]
     mine = half.reshape(pieces, HEAD_DIM, rank)
-    for step in range(1, dp_count):
-        came = across(half, step).reshape(pieces, HEAD_DIM, rank)
-        mine = jnp.where(from_where == step, came, mine)
-    mine = mine.reshape(pieces * HEAD_DIM, rank)
+    step = 1
+    while step < dp_count:
+        came = across(mine.reshape(half.shape), step).reshape(mine.shape)
+        mine = jnp.where((from_where & step) != 0, came, mine)
+        step *= 2
+    mine = mine.reshape(half.shape)
     other = pair(mine)
 
-    features = layer_input.shape[2] // chips
-
-    def columns(step):
-        target = lax.rem(chip + step, chips)
-        return lax.dynamic_slice_in_dim(layer_input[0], target * features, features, 1)
-
-    x_parts = [columns(0)] + [around(columns(step), step) for step in range(1, chips)]
+    share = layer_input.shape[2] // (seq_count * dp_count)
+    x_pieces = layer_input[0].reshape(BLOCK, chips, 2, dp_count, share)
+    x_pieces = jnp.transpose(x_pieces, (3, 0, 2, 1, 4)).reshape(dp_count, BLOCK, seq_count * share)
+    x_all = lax.all_to_all(x_pieces, "dp", 0, 0, tiled=True)
 
     query_grads, grads = [], []
     for chunk in range(CHUNKS):
+        if chunk:
+            arrived[chunk][1:], grads = lax.optimization_barrier((arrived[chunk][1:], grads))
+        kv_parts = arrived[chunk] + [beside[chunk]] + [pair(piece) for piece in arrived[chunk][1:]]
         query_grad, grad = attention(
-            table, queries[0], grad_out[0], kv_parts[chunk], slots, chunk * heads, heads
+            table, queries[0], grad_out[0], kv_parts, slots, chunk * heads, heads
         )
         query_grads.append(query_grad)
         grads.append(grad)
     grad_query = jnp.concatenate(query_grads, axis=1)
 
     keep, send = project(mine, other, grads, chips)
-    (send, x_parts) = lax.optimization_barrier((send, x_parts))
     own, *sends = fold(keep, pair(send), chips)
     total = own
     for step in range(1, chips):
         total = total + down(sends[step - 1], step).astype(f32)
     projected = total.astype(bf16)
-    p_parts = [projected] + [around(projected, step) for step in range(1, chips)]
-    kept, sent = outer(x_parts, p_parts)
-    partial_rank = kept + pair(sent).astype(f32)
-    low = partial_rank.astype(bf16)
-    for step in range(1, dp_count):
-        partial_rank = partial_rank + across(low, step).astype(f32)
-    lowrank_grad = partial_rank / dp_count
+    p_parts = [projected] + [across(projected, step) for step in range(1, dp_count)]
+    kept, sent = outer(x_all, p_parts)
+    own, *sends = deal(kept, pair(sent), chips)
+    total = own
+    for step in range(1, chips):
+        total = total + around(sends[step - 1], step).astype(f32)
+    rows = total.astype(bf16)
+    lowrank_grad = lay([rows] + [across(rows, step) for step in range(1, dp_count)])
     return (grad_query[None], lowrank_grad)
 
 

time: 97.3 us -> 86.9 us (0.89)
  waiting for transfers between devices: 41.1 us -> 24.4 us
  starting transfers between devices: 34.5 us -> 40.7 us
  local copies, waits for them, and re-layouts: 4.52 us -> 6.35 us
  other arithmetic: 6.04 us -> 4.25 us
    ppermute x6 -> x3, starting transfers between devices: 12.6 us -> 3.87 us  [around(): return lax.ppermute(x, 'seq', moves)]
    ppermute x6 -> x8, waiting for transfers between devices: 16.7 us -> 8.91 us  [across(): return lax.ppermute(x, 'dp', [(i, i ^ step) for i in range(dp_count)])]
    ppermute x3, waiting for transfers between devices: 12 us -> 7.95 us  [down(): return lax.ppermute(x, 'seq', moves)]
    ppermute x3 -> x6, starting transfers between devices: 10.7 us -> 14.8 us  [up(): return lax.ppermute(x, 'seq', moves)]
    ppermute x6 -> x3, waiting for transfers between devices: 8.64 us -> 4.82 us  [around(): return lax.ppermute(x, 'seq', moves)]
    all_to_all x0 -> x1, starting transfers between devices: none -> 3.65 us  [local(): x_all = lax.all_to_all(x_pieces, 'dp', 0, 0, tiled=True)]
    ppermute x7 -> x11, starting transfers between devices: 0.23 us -> 3.87 us  [pair(): return lax.ppermute(x, 'seq', [(i, i ^ 1) for i in range(seq_count)])]
    ppermute x6 -> x8, starting transfers between devices: 7.05 us -> 10.6 us  [across(): return lax.ppermute(x, 'dp', [(i, i ^ step) for i in range(dp_count)])]
  transfers between devices with their start and end apart: 25 -> 32, of which waited for: 13 -> 13; matrix products, arithmetic and copies ran while one was open for 9% -> 10% of each run, Pallas kernels for 10% -> 10%
where the time goes in v3:
time: 86.9 us; the launch traced here: 86.4 us
  starting transfers between devices  40.7 us (47%)
  waiting for transfers between devices  24.4 us (28%)
  Pallas kernels  9.69 us (11%)
  local copies, waits for them, and re-layouts  6.35 us (7%)
  other arithmetic  4.25 us (5%)
  between operations  1.01 us (1%)
    ppermute x6, starting transfers between devices, up(): return lax.ppermute(x, 'seq', moves)  14.8 us
    ppermute x8, starting transfers between devices, across(): return lax.ppermute(x, 'dp', [(i, i ^ step) for i in range(dp_count)])  10.6 us
    ppermute x8, waiting for transfers between devices, across(): return lax.ppermute(x, 'dp', [(i, i ^ step) for i in range(dp_count)])  8.91 us
    ppermute x3, waiting for transfers between devices, down(): return lax.ppermute(x, 'seq', moves)  7.95 us
    pallas_call x2, Pallas kernels, attention(): pl.pallas_call(body, in_specs=[pl.BlockSpec(memory_space=pltpu.SMEM)] + [...  7.47 us
    ppermute x3, waiting for transfers between devices, around(): return lax.ppermute(x, 'seq', moves)  4.82 us
    ppermute x3, starting transfers between devices, down(): return lax.ppermute(x, 'seq', moves)  3.88 us
    ppermute x3, starting transfers between devices, around(): return lax.ppermute(x, 'seq', moves)  3.87 us
  transfers between devices with their start and end apart: 32, of which 13 were waited for; matrix products, arithmetic and copies ran while one was open for 10% of the time, Pallas kernels for 10%

profile of v3, /device:TPU:0, one launch (start us, length us, event | category | flops | bytes accessed | tf_op | source)
XLA Modules:
  0.0 86.4 jit_solution(14002657693666593569)
XLA Ops:
  1.7 4.9 %collective-permute-start = (bf16[128,512]{1,0:T(8,128)(2,1)S(1)}, bf16[128,512]{1,0:T(8,128)(2,1)S(1)}, u32[]{:S(2)}, u32[]{:S(2)}) collective-permute-start(bf16[128,512]{1,0:T(8,128)(2,1)S(1)} %pad_maximum_fusion.1.refs_0_), channel_id=1, source_target_pairs={{0,2},{1,3},{2,4},{3,5},{4,6},{5,7},{8,10},{9,11},{10,12},{11,13},... | collective-permute-start | bytes 393224 | tf_op jit(solution)/shard_map/ppermute | solution.py:331
  6.7 4.5 %collective-permute-start.1 = (bf16[128,512]{1,0:T(8,128)(2,1)S(1)}, bf16[128,512]{1,0:T(8,128)(2,1)S(1)}, u32[]{:S(2)}, u32[]{:S(2)}) collective-permute-start(bf16[128,512]{1,0:T(8,128)(2,1)S(1)} %pad_maximum_fusion.1.refs_0_), channel_id=1, source_target_pairs={{0,4},{1,5},{2,6},{3,7},{8,12},{9,13},{10,14},{11,15},{16,20},{17,... | collective-permute-start | bytes 393224 | tf_op jit(solution)/shard_map/ppermute | solution.py:331
  11.2 1.3 %collective-permute-start.2 = (bf16[128,512]{1,0:T(8,128)(2,1)S(1)}, bf16[128,512]{1,0:T(8,128)(2,1)S(1)}, u32[]{:S(2)}, u32[]{:S(2)}) collective-permute-start(bf16[128,512]{1,0:T(8,128)(2,1)S(1)} %pad_maximum_fusion.1.refs_0_), channel_id=1, source_target_pairs={{0,6},{1,7},{8,14},{9,15},{16,22},{17,23},{24,30},{25,31}} | collective-permute-start | bytes 393224 | tf_op jit(solution)/shard_map/ppermute | solution.py:331
  12.5 1.3 %collective-permute-start.7 = (bf16[128,512]{1,0:T(8,128)(2,1)S(1)}, bf16[128,512]{1,0:T(8,128)(2,1)S(1)}, u32[]{:S(2)}, u32[]{:S(2)}) collective-permute-start(bf16[128,512]{1,0:T(8,128)(2,1)S(1)} %pad_maximum_fusion.refs_0_), channel_id=1, source_target_pairs={{0,2},{1,3},{2,4},{3,5},{4,6},{5,7},{8,10},{9,11},{10,12},{11,13},... | collective-permute-start | bytes 393224 | tf_op jit(solution)/shard_map/ppermute | solution.py:331
  14.6 1.5 %collective-permute-start.14 = (bf16[512,256]{1,0:T(8,128)(2,1)}, bf16[512,256]{1,0:T(8,128)(2,1)}, u32[]{:S(2)}, u32[]{:S(2)}) collective-permute-start(bf16[512,256]{1,0:T(8,128)(2,1)} %dynamic-slice_bitcast_fusion), channel_id=1, source_target_pairs={{0,8},{8,0},{16,24},{24,16},{1,9},{9,1},{17,25},{25,17},{2,10},{10... | collective-permute-start | bytes 786440 | tf_op jit(solution)/shard_map/ppermute | solution.py:342
  17.2 1.5 %reshape.106 = bf16[4,128,1024]{2,1,0:T(8,128)(2,1)} reshape(bf16[4,128,2,4,128]{4,3,2,1,0:T(4,128)(2,1)S(1)} %bitcast.50) | data formatting | bytes 2097152 | tf_op jit(solution)/shard_map/reshape | solution.py:378
  18.8 3.6 %all-to-all-start = ((bf16[4,128,1024]{2,1,0:T(8,128)(2,1)}), bf16[4,128,1024]{2,1,0:T(8,128)(2,1)S(1)}, u32[]{:S(2)}, u32[]{:S(2)}) async-start(bf16[4,128,1024]{2,1,0:T(8,128)(2,1)} %reshape.106), calls=%async_computation | async-start | bytes 2097152 | tf_op jit(solution)/shard_map/all_to_all | solution.py:379
  27.3 1.3 %collective-permute-start.8 = (bf16[128,512]{1,0:T(8,128)(2,1)S(1)}, bf16[128,512]{1,0:T(8,128)(2,1)S(1)}, u32[]{:S(2)}, u32[]{:S(2)}) collective-permute-start(bf16[128,512]{1,0:T(8,128)(2,1)S(1)} %pad_maximum_fusion.refs_0_), channel_id=1, source_target_pairs={{0,4},{1,5},{2,6},{3,7},{8,12},{9,13},{10,14},{11,15},{16,20},{17,... | collective-permute-start | bytes 393224 | tf_op jit(solution)/shard_map/ppermute | solution.py:331
  28.6 1.5 %collective-permute-start.9 = (bf16[128,512]{1,0:T(8,128)(2,1)S(1)}, bf16[128,512]{1,0:T(8,128)(2,1)S(1)}, u32[]{:S(2)}, u32[]{:S(2)}) collective-permute-start(bf16[128,512]{1,0:T(8,128)(2,1)S(1)} %pad_maximum_fusion.refs_0_), channel_id=1, source_target_pairs={{0,6},{1,7},{8,14},{9,15},{16,22},{17,23},{24,30},{25,31}} | collective-permute-start | bytes 393224 | tf_op jit(solution)/shard_map/ppermute | solution.py:331
  30.1 2.0 %collective-permute-start.15 = (bf16[512,256]{1,0:T(8,128)(2,1)S(1)}, bf16[512,256]{1,0:T(8,128)(2,1)S(1)}, u32[]{:S(2)}, u32[]{:S(2)}) collective-permute-start(bf16[512,256]{1,0:T(8,128)(2,1)S(1)} %broadcast_select_fusion), channel_id=1, source_target_pairs={{0,16},{8,24},{16,0},{24,8},{1,17},{9,25},{17,1},{25,9},{2,18},{10... | collective-permute-start | bytes 786440 | tf_op jit(solution)/shard_map/ppermute | solution.py:342
  32.2 1.2 %copy-done.1 = bf16[1,128,4096]{2,1,0:T(8,128)(2,1)S(1)} copy-done((bf16[1,128,4096]{2,1,0:T(8,128)(2,1)S(1)}, bf16[1,128,4096]{2,1,0:T(8,128)(2,1)}, u32[]{:S(2)}) %copy-start.1) | copy-done | bytes 1048600
  33.4 3.6 %attention_backward.2 = (bf16[128,2048]{1,0:T(8,128)(2,1)S(1)}, bf16[1024,512]{1,0:T(8,128)(2,1)S(1)}) custom-call(s32[160]{0:T(256)S(1)} %reshape.105.table_ref, bf16[128,4096]{1,0:T(8,128)(2,1)S(1)} %bitcast.46, bf16[128,4096]{1,0:T(8,128)(2,1)S(1)} %bitcast.48, bf16[128,512]{1,0:T(8,128)(2,1)S(1)} %pad_maximum_fusion.1.refs_0_, ...), custom_call_target="tpu_custom_call" | custom-call | flops 10066329600 | bytes 4194304 | tf_op jit(solution)/shard_map/attention_backward/pallas_call | solution.py:154
  38.5 2.6 %collective-permute-done.15 = bf16[512,256]{1,0:T(8,128)(2,1)S(1)} collective-permute-done((bf16[512,256]{1,0:T(8,128)(2,1)S(1)}, bf16[512,256]{1,0:T(8,128)(2,1)S(1)}, u32[]{:S(2)}, u32[]{:S(2)}) %collective-permute-start.15) | collective-permute-done | bytes 262176 | tf_op jit(solution)/shard_map/ppermute | solution.py:342
  41.3 3.9 %attention_backward.3 = (bf16[128,2048]{1,0:T(8,128)(2,1)S(1)}, bf16[1024,512]{1,0:T(8,128)(2,1)S(1)}) custom-call(s32[160]{0:T(256)S(1)} %reshape.105.table_ref, bf16[128,4096]{1,0:T(8,128)(2,1)S(1)} %bitcast.47, bf16[128,4096]{1,0:T(8,128)(2,1)S(1)} %bitcast.49, bf16[128,512]{1,0:T(8,128)(2,1)S(1)} %pad_maximum_fusion.refs_0_, ...), custom_call_target="tpu_custom_call" | custom-call | flops 10066329600 | bytes 4194304 | tf_op jit(solution)/shard_map/attention_backward/pallas_call | solution.py:154
  47.0 1.2 %collective-permute-done.17.came_ref = bf16[512,256]{1,0:T(8,128)(2,1)S(1)} collective-permute-done((bf16[512,256]{1,0:T(8,128)(2,1)S(1)}, bf16[512,256]{1,0:T(8,128)(2,1)S(1)}, u32[]{:S(2)}, u32[]{:S(2)}) %collective-permute-start.17) | collective-permute-done | bytes 262176 | tf_op jit(solution)/shard_map/ppermute | solution.py:327
  48.2 1.3 %collective-permute-start.18 = (bf16[128,256]{1,0:T(8,128)(2,1)S(1)}, bf16[128,256]{1,0:T(8,128)(2,1)S(1)}, u32[]{:S(2)}, u32[]{:S(2)}) collective-permute-start(bf16[128,256]{1,0:T(8,128)(2,1)S(1)} %get-tuple-element.43), channel_id=1, source_target_pairs={{2,0},{3,1},{4,2},{5,3},{6,4},{7,5},{10,8},{11,9},{12,10},{13,11},... | collective-permute-start | bytes 196616 | tf_op jit(solution)/shard_map/ppermute | solution.py:335
  49.5 1.3 %collective-permute-start.19 = (bf16[128,256]{1,0:T(8,128)(2,1)S(1)}, bf16[128,256]{1,0:T(8,128)(2,1)S(1)}, u32[]{:S(2)}, u32[]{:S(2)}) collective-permute-start(bf16[128,256]{1,0:T(8,128)(2,1)S(1)} %get-tuple-element.44), channel_id=1, source_target_pairs={{4,0},{5,1},{6,2},{7,3},{12,8},{13,9},{14,10},{15,11},{20,16},{21,... | collective-permute-start | bytes 196616 | tf_op jit(solution)/shard_map/ppermute | solution.py:335
  50.8 1.3 %collective-permute-start.20 = (bf16[128,256]{1,0:T(8,128)(2,1)S(1)}, bf16[128,256]{1,0:T(8,128)(2,1)S(1)}, u32[]{:S(2)}, u32[]{:S(2)}) collective-permute-start(bf16[128,256]{1,0:T(8,128)(2,1)S(1)} %get-tuple-element.45), channel_id=1, source_target_pairs={{6,0},{7,1},{14,8},{15,9},{22,16},{23,17},{30,24},{31,25}} | collective-permute-start | bytes 196616 | tf_op jit(solution)/shard_map/ppermute | solution.py:335
  52.1 2.4 %collective-permute-done.18 = bf16[128,256]{1,0:T(8,128)(2,1)S(1)} collective-permute-done((bf16[128,256]{1,0:T(8,128)(2,1)S(1)}, bf16[128,256]{1,0:T(8,128)(2,1)S(1)}, u32[]{:S(2)}, u32[]{:S(2)}) %collective-permute-start.18) | collective-permute-done | bytes 65568 | tf_op jit(solution)/shard_map/ppermute | solution.py:335
  54.5 2.2 %collective-permute-done.19 = bf16[128,256]{1,0:T(8,128)(2,1)S(1)} collective-permute-done((bf16[128,256]{1,0:T(8,128)(2,1)S(1)}, bf16[128,256]{1,0:T(8,128)(2,1)S(1)}, u32[]{:S(2)}, u32[]{:S(2)}) %collective-permute-start.19) | collective-permute-done | bytes 65568 | tf_op jit(solution)/shard_map/ppermute | solution.py:335
  56.7 3.4 %collective-permute-done.20 = bf16[128,256]{1,0:T(8,128)(2,1)S(1)} collective-permute-done((bf16[128,256]{1,0:T(8,128)(2,1)S(1)}, bf16[128,256]{1,0:T(8,128)(2,1)S(1)}, u32[]{:S(2)}, u32[]{:S(2)}) %collective-permute-start.20) | collective-permute-done | bytes 65568 | tf_op jit(solution)/shard_map/ppermute | solution.py:335
  60.1 1.5 %collective-permute-start.21 = (bf16[128,256]{1,0:T(8,128)(2,1)S(1)}, bf16[128,256]{1,0:T(8,128)(2,1)S(1)}, u32[]{:S(2)}, u32[]{:S(2)}) collective-permute-start(bf16[128,256]{1,0:T(8,128)(2,1)S(1)} %add_convert_fusion.1.refs_0_), channel_id=1, source_target_pairs={{0,8},{8,0},{16,24},{24,16},{1,9},{9,1},{17,25},{25,17},{2,10},{10... | collective-permute-start | bytes 196616 | tf_op jit(solution)/shard_map/ppermute | solution.py:342
  62.2 1.5 %collective-permute-start.23 = (bf16[128,256]{1,0:T(8,128)(2,1)S(1)}, bf16[128,256]{1,0:T(8,128)(2,1)S(1)}, u32[]{:S(2)}, u32[]{:S(2)}) collective-permute-start(bf16[128,256]{1,0:T(8,128)(2,1)S(1)} %add_convert_fusion.1.refs_0_), channel_id=1, source_target_pairs={{0,24},{8,16},{16,8},{24,0},{1,25},{9,17},{17,9},{25,1},{2,26},{10... | collective-permute-start | bytes 196616 | tf_op jit(solution)/shard_map/ppermute | solution.py:342
  64.5 1.6 %collective-permute-done.22.refs_2_ = bf16[128,256]{1,0:T(8,128)(2,1)S(1)} collective-permute-done((bf16[128,256]{1,0:T(8,128)(2,1)S(1)}, bf16[128,256]{1,0:T(8,128)(2,1)S(1)}, u32[]{:S(2)}, u32[]{:S(2)}) %collective-permute-start.22) | collective-permute-done | bytes 65568 | tf_op jit(solution)/shard_map/ppermute | solution.py:342
  66.1 1.3 %collective-permute-done.23.refs_3_ = bf16[128,256]{1,0:T(8,128)(2,1)S(1)} collective-permute-done((bf16[128,256]{1,0:T(8,128)(2,1)S(1)}, bf16[128,256]{1,0:T(8,128)(2,1)S(1)}, u32[]{:S(2)}, u32[]{:S(2)}) %collective-permute-start.23) | collective-permute-done | bytes 65568 | tf_op jit(solution)/shard_map/ppermute | solution.py:342
  68.0 1.5 %collective-permute-done.24.came_ref = bf16[512,256]{1,0:T(8,128)(2,1)S(1)} collective-permute-done((bf16[512,256]{1,0:T(8,128)(2,1)S(1)}, bf16[512,256]{1,0:T(8,128)(2,1)S(1)}, u32[]{:S(2)}, u32[]{:S(2)}) %collective-permute-start.24) | collective-permute-done | bytes 262176 | tf_op jit(solution)/shard_map/ppermute | solution.py:327
  69.7 3.7 %collective-permute-start.27 = (bf16[128,256]{1,0:T(8,128)(2,1)S(1)}, bf16[128,256]{1,0:T(8,128)(2,1)S(1)}, u32[]{:S(2)}, u32[]{:S(2)}) collective-permute-start(bf16[128,256]{1,0:T(8,128)(2,1)S(1)} %get-tuple-element.51), channel_id=1, source_target_pairs={{0,6},{1,7},{2,0},{3,1},{4,2},{5,3},{6,4},{7,5},{8,14},{9,15},{10,... | collective-permute-start | bytes 196616 | tf_op jit(solution)/shard_map/ppermute | solution.py:339
  73.4 2.9 %collective-permute-done.25 = bf16[128,256]{1,0:T(8,128)(2,1)S(1)} collective-permute-done((bf16[128,256]{1,0:T(8,128)(2,1)S(1)}, bf16[128,256]{1,0:T(8,128)(2,1)S(1)}, u32[]{:S(2)}, u32[]{:S(2)}) %collective-permute-start.25) | collective-permute-done | bytes 65568 | tf_op jit(solution)/shard_map/ppermute | solution.py:339
  76.4 1.9 %collective-permute-done.26 = bf16[128,256]{1,0:T(8,128)(2,1)S(1)} collective-permute-done((bf16[128,256]{1,0:T(8,128)(2,1)S(1)}, bf16[128,256]{1,0:T(8,128)(2,1)S(1)}, u32[]{:S(2)}, u32[]{:S(2)}) %collective-permute-start.26) | collective-permute-done | bytes 65568 | tf_op jit(solution)/shard_map/ppermute | solution.py:339
  78.7 1.7 %collective-permute-start.29 = (bf16[128,256]{1,0:T(8,128)(2,1)S(1)}, bf16[128,256]{1,0:T(8,128)(2,1)S(1)}, u32[]{:S(2)}, u32[]{:S(2)}) collective-permute-start(bf16[128,256]{1,0:T(8,128)(2,1)S(1)} %add_convert_fusion.refs_0_), channel_id=1, source_target_pairs={{0,16},{8,24},{16,0},{24,8},{1,17},{9,25},{17,1},{25,9},{2,18},{10... | collective-permute-start | bytes 196616 | tf_op jit(solution)/shard_map/ppermute | solution.py:342
  80.4 1.5 %collective-permute-start.30 = (bf16[128,256]{1,0:T(8,128)(2,1)S(1)}, bf16[128,256]{1,0:T(8,128)(2,1)S(1)}, u32[]{:S(2)}, u32[]{:S(2)}) collective-permute-start(bf16[128,256]{1,0:T(8,128)(2,1)S(1)} %add_convert_fusion.refs_0_), channel_id=1, source_target_pairs={{0,24},{8,16},{16,8},{24,0},{1,25},{9,17},{17,9},{25,1},{2,26},{10... | collective-permute-start | bytes 196616 | tf_op jit(solution)/shard_map/ppermute | solution.py:342
  83.4 2.2 %collective-permute-done.30.refs_3_ = bf16[128,256]{1,0:T(8,128)(2,1)S(1)} collective-permute-done((bf16[128,256]{1,0:T(8,128)(2,1)S(1)}, bf16[128,256]{1,0:T(8,128)(2,1)S(1)}, u32[]{:S(2)}, u32[]{:S(2)}) %collective-permute-start.30) | collective-permute-done | bytes 65568 | tf_op jit(solution)/shard_map/ppermute | solution.py:342
  (79 shorter events, 16.3 us)
Async XLA Ops:
  1.7 23.2 %collective-permute-start = (bf16[128,512]{1,0:T(8,128)(2,1)S(1)}, bf16[128,512]{1,0:T(8,128)(2,1)S(1)}, u32[]{:S(2)}, u32[]{:S(2)}) collective-permute-start(bf16[128,512]{1,0:T(8,128)(2,1)S(1)} %pad_maximum_fusion.1.refs_0_), channel_id=1, source_target_pairs={{0,2},{1,3},{2,4},{3,5},{4,6},{5,7},{8,10},{9,11},{10,12},{11,13},... | collective-permute-start | bytes 393224 | tf_op jit(solution)/shard_map/ppermute | solution.py:331
  6.7 18.3 %collective-permute-start.1 = (bf16[128,512]{1,0:T(8,128)(2,1)S(1)}, bf16[128,512]{1,0:T(8,128)(2,1)S(1)}, u32[]{:S(2)}, u32[]{:S(2)}) collective-permute-start(bf16[128,512]{1,0:T(8,128)(2,1)S(1)} %pad_maximum_fusion.1.refs_0_), channel_id=1, source_target_pairs={{0,4},{1,5},{2,6},{3,7},{8,12},{9,13},{10,14},{11,15},{16,20},{17,... | collective-permute-start | bytes 393224 | tf_op jit(solution)/shard_map/ppermute | solution.py:331
  11.2 13.8 %collective-permute-start.2 = (bf16[128,512]{1,0:T(8,128)(2,1)S(1)}, bf16[128,512]{1,0:T(8,128)(2,1)S(1)}, u32[]{:S(2)}, u32[]{:S(2)}) collective-permute-start(bf16[128,512]{1,0:T(8,128)(2,1)S(1)} %pad_maximum_fusion.1.refs_0_), channel_id=1, source_target_pairs={{0,6},{1,7},{8,14},{9,15},{16,22},{17,23},{24,30},{25,31}} | collective-permute-start | bytes 393224 | tf_op jit(solution)/shard_map/ppermute | solution.py:331
  12.5 24.5 %collective-permute-start.7 = (bf16[128,512]{1,0:T(8,128)(2,1)S(1)}, bf16[128,512]{1,0:T(8,128)(2,1)S(1)}, u32[]{:S(2)}, u32[]{:S(2)}) collective-permute-start(bf16[128,512]{1,0:T(8,128)(2,1)S(1)} %pad_maximum_fusion.refs_0_), channel_id=1, source_target_pairs={{0,2},{1,3},{2,4},{3,5},{4,6},{5,7},{8,10},{9,11},{10,12},{11,13},... | collective-permute-start | bytes 393224 | tf_op jit(solution)/shard_map/ppermute | solution.py:331
  14.6 11.1 %collective-permute-start.14 = (bf16[512,256]{1,0:T(8,128)(2,1)}, bf16[512,256]{1,0:T(8,128)(2,1)}, u32[]{:S(2)}, u32[]{:S(2)}) collective-permute-start(bf16[512,256]{1,0:T(8,128)(2,1)} %dynamic-slice_bitcast_fusion), channel_id=1, source_target_pairs={{0,8},{8,0},{16,24},{24,16},{1,9},{9,1},{17,25},{25,17},{2,10},{10... | collective-permute-start | bytes 786440 | tf_op jit(solution)/shard_map/ppermute | solution.py:342
  18.8 44.9 %all-to-all-start = ((bf16[4,128,1024]{2,1,0:T(8,128)(2,1)}), bf16[4,128,1024]{2,1,0:T(8,128)(2,1)S(1)}, u32[]{:S(2)}, u32[]{:S(2)}) async-start(bf16[4,128,1024]{2,1,0:T(8,128)(2,1)} %reshape.106), calls=%async_computation | async-start | bytes 2097152 | tf_op jit(solution)/shard_map/all_to_all | solution.py:379
  25.0 2.2 %collective-permute-start.3 = (bf16[128,512]{1,0:T(8,128)(2,1)S(1)}, bf16[128,512]{1,0:T(8,128)(2,1)S(1)}, u32[]{:S(2)}, u32[]{:S(2)}) collective-permute-start(bf16[128,512]{1,0:T(8,128)(2,1)S(1)} %pad_maximum_fusion.1.refs_0_), channel_id=1, source_target_pairs={{0,1},{1,0},{2,3},{3,2},{4,5},{5,4},{6,7},{7,6},{8,9},{9,8},{10,11... | collective-permute-start | bytes 393224 | tf_op jit(solution)/shard_map/ppermute | solution.py:327
  25.1 2.3 %collective-permute-start.4 = (bf16[128,512]{1,0:T(8,128)(2,1)S(1)}, bf16[128,512]{1,0:T(8,128)(2,1)S(1)}, u32[]{:S(2)}, u32[]{:S(2)}) collective-permute-start(bf16[128,512]{1,0:T(8,128)(2,1)S(1)} %collective-permute-done.refs_1_), channel_id=1, source_target_pairs={{0,1},{1,0},{2,3},{3,2},{4,5},{5,4},{6,7},{7,6},{8,9},{9,8},{10,11... | collective-permute-start | bytes 393224 | tf_op jit(solution)/shard_map/ppermute | solution.py:327
  25.6 3.1 %collective-permute-start.5 = (bf16[128,512]{1,0:T(8,128)(2,1)S(1)}, bf16[128,512]{1,0:T(8,128)(2,1)S(1)}, u32[]{:S(2)}, u32[]{:S(2)}) collective-permute-start(bf16[128,512]{1,0:T(8,128)(2,1)S(1)} %collective-permute-done.1.refs_2_), channel_id=1, source_target_pairs={{0,1},{1,0},{2,3},{3,2},{4,5},{5,4},{6,7},{7,6},{8,9},{9,8},{10,11... | collective-permute-start | bytes 393224 | tf_op jit(solution)/shard_map/ppermute | solution.py:327
  25.7 4.5 %collective-permute-start.6 = (bf16[128,512]{1,0:T(8,128)(2,1)S(1)}, bf16[128,512]{1,0:T(8,128)(2,1)S(1)}, u32[]{:S(2)}, u32[]{:S(2)}) collective-permute-start(bf16[128,512]{1,0:T(8,128)(2,1)S(1)} %collective-permute-done.2.refs_3_), channel_id=1, source_target_pairs={{0,1},{1,0},{2,3},{3,2},{4,5},{5,4},{6,7},{7,6},{8,9},{9,8},{10,11... | collective-permute-start | bytes 393224 | tf_op jit(solution)/shard_map/ppermute | solution.py:327
  27.2 14.1 %collective-permute-start.10 = (bf16[128,512]{1,0:T(8,128)(2,1)S(1)}, bf16[128,512]{1,0:T(8,128)(2,1)S(1)}, u32[]{:S(2)}, u32[]{:S(2)}) collective-permute-start(bf16[128,512]{1,0:T(8,128)(2,1)S(1)} %pad_maximum_fusion.refs_0_), channel_id=1, source_target_pairs={{0,1},{1,0},{2,3},{3,2},{4,5},{5,4},{6,7},{7,6},{8,9},{9,8},{10,11... | collective-permute-start | bytes 393224 | tf_op jit(solution)/shard_map/ppermute | solution.py:327
  27.3 9.7 %collective-permute-start.8 = (bf16[128,512]{1,0:T(8,128)(2,1)S(1)}, bf16[128,512]{1,0:T(8,128)(2,1)S(1)}, u32[]{:S(2)}, u32[]{:S(2)}) collective-permute-start(bf16[128,512]{1,0:T(8,128)(2,1)S(1)} %pad_maximum_fusion.refs_0_), channel_id=1, source_target_pairs={{0,4},{1,5},{2,6},{3,7},{8,12},{9,13},{10,14},{11,15},{16,20},{17,... | collective-permute-start | bytes 393224 | tf_op jit(solution)/shard_map/ppermute | solution.py:331
  28.6 8.4 %collective-permute-start.9 = (bf16[128,512]{1,0:T(8,128)(2,1)S(1)}, bf16[128,512]{1,0:T(8,128)(2,1)S(1)}, u32[]{:S(2)}, u32[]{:S(2)}) collective-permute-start(bf16[128,512]{1,0:T(8,128)(2,1)S(1)} %pad_maximum_fusion.refs_0_), channel_id=1, source_target_pairs={{0,6},{1,7},{8,14},{9,15},{16,22},{17,23},{24,30},{25,31}} | collective-permute-start | bytes 393224 | tf_op jit(solution)/shard_map/ppermute | solution.py:331
  30.1 10.9 %collective-permute-start.15 = (bf16[512,256]{1,0:T(8,128)(2,1)S(1)}, bf16[512,256]{1,0:T(8,128)(2,1)S(1)}, u32[]{:S(2)}, u32[]{:S(2)}) collective-permute-start(bf16[512,256]{1,0:T(8,128)(2,1)S(1)} %broadcast_select_fusion), channel_id=1, source_target_pairs={{0,16},{8,24},{16,0},{24,8},{1,17},{9,25},{17,1},{25,9},{2,18},{10... | collective-permute-start | bytes 786440 | tf_op jit(solution)/shard_map/ppermute | solution.py:342
  37.1 4.2 %collective-permute-start.11 = (bf16[128,512]{1,0:T(8,128)(2,1)S(1)}, bf16[128,512]{1,0:T(8,128)(2,1)S(1)}, u32[]{:S(2)}, u32[]{:S(2)}) collective-permute-start(bf16[128,512]{1,0:T(8,128)(2,1)S(1)} %collective-permute-done.7.refs_1_), channel_id=1, source_target_pairs={{0,1},{1,0},{2,3},{3,2},{4,5},{5,4},{6,7},{7,6},{8,9},{9,8},{10,11... | collective-permute-start | bytes 393224 | tf_op jit(solution)/shard_map/ppermute | solution.py:327
  38.0 3.3 %collective-permute-start.12 = (bf16[128,512]{1,0:T(8,128)(2,1)S(1)}, bf16[128,512]{1,0:T(8,128)(2,1)S(1)}, u32[]{:S(2)}, u32[]{:S(2)}) collective-permute-start(bf16[128,512]{1,0:T(8,128)(2,1)S(1)} %collective-permute-done.8.refs_2_), channel_id=1, source_target_pairs={{0,1},{1,0},{2,3},{3,2},{4,5},{5,4},{6,7},{7,6},{8,9},{9,8},{10,11... | collective-permute-start | bytes 393224 | tf_op jit(solution)/shard_map/ppermute | solution.py:327
  38.1 3.2 %collective-permute-start.13 = (bf16[128,512]{1,0:T(8,128)(2,1)S(1)}, bf16[128,512]{1,0:T(8,128)(2,1)S(1)}, u32[]{:S(2)}, u32[]{:S(2)}) collective-permute-start(bf16[128,512]{1,0:T(8,128)(2,1)S(1)} %collective-permute-done.9.refs_3_), channel_id=1, source_target_pairs={{0,1},{1,0},{2,3},{3,2},{4,5},{5,4},{6,7},{7,6},{8,9},{9,8},{10,11... | collective-permute-start | bytes 393224 | tf_op jit(solution)/shard_map/ppermute | solution.py:327
  41.2 4.0 %collective-permute-start.16 = (bf16[512,256]{1,0:T(8,128)(2,1)S(1)}, bf16[512,256]{1,0:T(8,128)(2,1)S(1)}, u32[]{:S(2)}, u32[]{:S(2)}) collective-permute-start(bf16[512,256]{1,0:T(8,128)(2,1)S(1)} %broadcast_select_fusion.1.mine_ref), channel_id=1, source_target_pairs={{0,1},{1,0},{2,3},{3,2},{4,5},{5,4},{6,7},{7,6},{8,9},{9,8},{10,11... | collective-permute-start | bytes 786440 | tf_op jit(solution)/shard_map/ppermute | solution.py:327
  46.0 2.2 %collective-permute-start.17 = (bf16[512,256]{1,0:T(8,128)(2,1)S(1)}, bf16[512,256]{1,0:T(8,128)(2,1)S(1)}, u32[]{:S(2)}, u32[]{:S(2)}) collective-permute-start(bf16[512,256]{1,0:T(8,128)(2,1)S(1)} %get-tuple-element.41), channel_id=1, source_target_pairs={{0,1},{1,0},{2,3},{3,2},{4,5},{5,4},{6,7},{7,6},{8,9},{9,8},{10,11... | collective-permute-start | bytes 786440 | tf_op jit(solution)/shard_map/ppermute | solution.py:327
  48.2 6.3 %collective-permute-start.18 = (bf16[128,256]{1,0:T(8,128)(2,1)S(1)}, bf16[128,256]{1,0:T(8,128)(2,1)S(1)}, u32[]{:S(2)}, u32[]{:S(2)}) collective-permute-start(bf16[128,256]{1,0:T(8,128)(2,1)S(1)} %get-tuple-element.43), channel_id=1, source_target_pairs={{2,0},{3,1},{4,2},{5,3},{6,4},{7,5},{10,8},{11,9},{12,10},{13,11},... | collective-permute-start | bytes 196616 | tf_op jit(solution)/shard_map/ppermute | solution.py:335
  49.5 7.2 %collective-permute-start.19 = (bf16[128,256]{1,0:T(8,128)(2,1)S(1)}, bf16[128,256]{1,0:T(8,128)(2,1)S(1)}, u32[]{:S(2)}, u32[]{:S(2)}) collective-permute-start(bf16[128,256]{1,0:T(8,128)(2,1)S(1)} %get-tuple-element.44), channel_id=1, source_target_pairs={{4,0},{5,1},{6,2},{7,3},{12,8},{13,9},{14,10},{15,11},{20,16},{21,... | collective-permute-start | bytes 196616 | tf_op jit(solution)/shard_map/ppermute | solution.py:335
  50.8 9.3 %collective-permute-start.20 = (bf16[128,256]{1,0:T(8,128)(2,1)S(1)}, bf16[128,256]{1,0:T(8,128)(2,1)S(1)}, u32[]{:S(2)}, u32[]{:S(2)}) collective-permute-start(bf16[128,256]{1,0:T(8,128)(2,1)S(1)} %get-tuple-element.45), channel_id=1, source_target_pairs={{6,0},{7,1},{14,8},{15,9},{22,16},{23,17},{30,24},{31,25}} | collective-permute-start | bytes 196616 | tf_op jit(solution)/shard_map/ppermute | solution.py:335
  60.1 4.3 %collective-permute-start.21 = (bf16[128,256]{1,0:T(8,128)(2,1)S(1)}, bf16[128,256]{1,0:T(8,128)(2,1)S(1)}, u32[]{:S(2)}, u32[]{:S(2)}) collective-permute-start(bf16[128,256]{1,0:T(8,128)(2,1)S(1)} %add_convert_fusion.1.refs_0_), channel_id=1, source_target_pairs={{0,8},{8,0},{16,24},{24,16},{1,9},{9,1},{17,25},{25,17},{2,10},{10... | collective-permute-start | bytes 196616 | tf_op jit(solution)/shard_map/ppermute | solution.py:342
  61.7 4.4 %collective-permute-start.22 = (bf16[128,256]{1,0:T(8,128)(2,1)S(1)}, bf16[128,256]{1,0:T(8,128)(2,1)S(1)}, u32[]{:S(2)}, u32[]{:S(2)}) collective-permute-start(bf16[128,256]{1,0:T(8,128)(2,1)S(1)} %add_convert_fusion.1.refs_0_), channel_id=1, source_target_pairs={{0,16},{8,24},{16,0},{24,8},{1,17},{9,25},{17,1},{25,9},{2,18},{10... | collective-permute-start | bytes 196616 | tf_op jit(solution)/shard_map/ppermute | solution.py:342
  62.2 5.2 %collective-permute-start.23 = (bf16[128,256]{1,0:T(8,128)(2,1)S(1)}, bf16[128,256]{1,0:T(8,128)(2,1)S(1)}, u32[]{:S(2)}, u32[]{:S(2)}) collective-permute-start(bf16[128,256]{1,0:T(8,128)(2,1)S(1)} %add_convert_fusion.1.refs_0_), channel_id=1, source_target_pairs={{0,24},{8,16},{16,8},{24,0},{1,25},{9,17},{17,9},{25,1},{2,26},{10... | collective-permute-start | bytes 196616 | tf_op jit(solution)/shard_map/ppermute | solution.py:342
  67.9 1.6 %collective-permute-start.24 = (bf16[512,256]{1,0:T(8,128)(2,1)S(1)}, bf16[512,256]{1,0:T(8,128)(2,1)S(1)}, u32[]{:S(2)}, u32[]{:S(2)}) collective-permute-start(bf16[512,256]{1,0:T(8,128)(2,1)S(1)} %get-tuple-element.47), channel_id=1, source_target_pairs={{0,1},{1,0},{2,3},{3,2},{4,5},{5,4},{6,7},{7,6},{8,9},{9,8},{10,11... | collective-permute-start | bytes 786440 | tf_op jit(solution)/shard_map/ppermute | solution.py:327
  69.6 6.8 %collective-permute-start.25 = (bf16[128,256]{1,0:T(8,128)(2,1)S(1)}, bf16[128,256]{1,0:T(8,128)(2,1)S(1)}, u32[]{:S(2)}, u32[]{:S(2)}) collective-permute-start(bf16[128,256]{1,0:T(8,128)(2,1)S(1)} %get-tuple-element.49), channel_id=1, source_target_pairs={{0,2},{1,3},{2,4},{3,5},{4,6},{5,7},{6,0},{7,1},{8,10},{9,11},{10,... | collective-permute-start | bytes 196616 | tf_op jit(solution)/shard_map/ppermute | solution.py:339
  69.6 8.6 %collective-permute-start.26 = (bf16[128,256]{1,0:T(8,128)(2,1)S(1)}, bf16[128,256]{1,0:T(8,128)(2,1)S(1)}, u32[]{:S(2)}, u32[]{:S(2)}) collective-permute-start(bf16[128,256]{1,0:T(8,128)(2,1)S(1)} %get-tuple-element.50), channel_id=1, source_target_pairs={{0,4},{1,5},{2,6},{3,7},{4,0},{5,1},{6,2},{7,3},{8,12},{9,13},{10,... | collective-permute-start | bytes 196616 | tf_op jit(solution)/shard_map/ppermute | solution.py:339
  69.7 8.5 %collective-permute-start.27 = (bf16[128,256]{1,0:T(8,128)(2,1)S(1)}, bf16[128,256]{1,0:T(8,128)(2,1)S(1)}, u32[]{:S(2)}, u32[]{:S(2)}) collective-permute-start(bf16[128,256]{1,0:T(8,128)(2,1)S(1)} %get-tuple-element.51), channel_id=1, source_target_pairs={{0,6},{1,7},{2,0},{3,1},{4,2},{5,3},{6,4},{7,5},{8,14},{9,15},{10,... | collective-permute-start | bytes 196616 | tf_op jit(solution)/shard_map/ppermute | solution.py:339
  78.3 4.6 %collective-permute-start.28 = (bf16[128,256]{1,0:T(8,128)(2,1)S(1)}, bf16[128,256]{1,0:T(8,128)(2,1)S(1)}, u32[]{:S(2)}, u32[]{:S(2)}) collective-permute-start(bf16[128,256]{1,0:T(8,128)(2,1)S(1)} %add_convert_fusion.refs_0_), channel_id=1, source_target_pairs={{0,8},{8,0},{16,24},{24,16},{1,9},{9,1},{17,25},{25,17},{2,10},{10... | collective-permute-start | bytes 196616 | tf_op jit(solution)/shard_map/ppermute | solution.py:342
  78.7 4.7 %collective-permute-start.29 = (bf16[128,256]{1,0:T(8,128)(2,1)S(1)}, bf16[128,256]{1,0:T(8,128)(2,1)S(1)}, u32[]{:S(2)}, u32[]{:S(2)}) collective-permute-start(bf16[128,256]{1,0:T(8,128)(2,1)S(1)} %add_convert_fusion.refs_0_), channel_id=1, source_target_pairs={{0,16},{8,24},{16,0},{24,8},{1,17},{9,25},{17,1},{25,9},{2,18},{10... | collective-permute-start | bytes 196616 | tf_op jit(solution)/shard_map/ppermute | solution.py:342
  80.4 5.2 %collective-permute-start.30 = (bf16[128,256]{1,0:T(8,128)(2,1)S(1)}, bf16[128,256]{1,0:T(8,128)(2,1)S(1)}, u32[]{:S(2)}, u32[]{:S(2)}) collective-permute-start(bf16[128,256]{1,0:T(8,128)(2,1)S(1)} %add_convert_fusion.refs_0_), channel_id=1, source_target_pairs={{0,24},{8,16},{16,8},{24,0},{1,25},{9,17},{17,9},{25,1},{2,26},{10... | collective-permute-start | bytes 196616 | tf_op jit(solution)/shard_map/ppermute | solution.py:342
  (5 other events, 48.9 us)

commit v4 on v3

--- a/solution.py
+++ b/solution.py
@@ -326,17 +326,15 @@
     def pair(x):
         return lax.ppermute(x, "seq", [(i, i ^ 1) for i in range(seq_count)])
 
-    def up(x, step):
-        moves = [(i, i + 2 * step) for i in range(seq_count) if i + 2 * step < seq_count]
-        return lax.ppermute(x, "seq", moves)
-
-    def down(x, step):
-        moves = [(i, i - 2 * step) for i in range(seq_count) if i >= 2 * step]
-        return lax.ppermute(x, "seq", moves)
-
     def around(x, step):
         moves = [(i, (i + 2 * step) % seq_count) for i in range(seq_count)]
         return lax.ppermute(x, "seq", moves)
+
+    def up(x, step):
+        return around(x, step)
+
+    def down(x, step):
+        return around(x, -step)
 
     def across(x, step):
         return lax.ppermute(x, "dp", [(i, i ^ step) for i in range(dp_count)])

time: 86.9 us -> 81.1 us (0.933)
  waiting for transfers between devices: 24.4 us -> 21.5 us
  starting transfers between devices: 40.7 us -> 37.9 us
    ppermute x9 -> x0, starting transfers between devices: 18.7 us -> none  [the longest x6 14.8 us: up(): return lax.ppermute(x, 'seq', moves)]
    ppermute x3 -> x12, starting transfers between devices: 3.87 us -> 20.6 us  [around(): return lax.ppermute(x, 'seq', moves)]
    ppermute x9 -> x0, waiting for transfers between devices: 7.97 us -> none  [the longest x3 7.95 us: down(): return lax.ppermute(x, 'seq', moves)]
    ppermute x3 -> x12, waiting for transfers between devices: 4.82 us -> 10.5 us  [around(): return lax.ppermute(x, 'seq', moves)]
  transfers between devices with their start and end apart: 32 -> 32, of which waited for: 13 -> 12; matrix products, arithmetic and copies ran while one was open for 10% -> 10% of each run, Pallas kernels for 10% -> 10%
where the time goes in v4:
time: 81.1 us; the launch traced here: 80.5 us
  starting transfers between devices  37.9 us (47%)
  waiting for transfers between devices  21.5 us (27%)
  Pallas kernels  9.69 us (12%)
  local copies, waits for them, and re-layouts  6.34 us (8%)
  other arithmetic  4.25 us (5%)
  between operations  0.9 us (1%)
    ppermute x12, starting transfers between devices, around(): return lax.ppermute(x, 'seq', moves)  20.6 us
    ppermute x12, waiting for transfers between devices, around(): return lax.ppermute(x, 'seq', moves)  10.5 us
    ppermute x8, starting transfers between devices, across(): return lax.ppermute(x, 'dp', [(i, i ^ step) for i in range(dp_count)])  10.2 us
    ppermute x8, waiting for transfers between devices, across(): return lax.ppermute(x, 'dp', [(i, i ^ step) for i in range(dp_count)])  8.27 us
    pallas_call x2, Pallas kernels, attention(): pl.pallas_call(body, in_specs=[pl.BlockSpec(memory_space=pltpu.SMEM)] + [...  7.47 us
    all_to_all x1, starting transfers between devices, local(): x_all = lax.all_to_all(x_pieces, 'dp', 0, 0, tiled=True)  3.65 us
    ppermute x11, starting transfers between devices, pair(): return lax.ppermute(x, 'seq', [(i, i ^ 1) for i in range(seq_count)])  3.4 us
    ppermute x11, waiting for transfers between devices, pair(): return lax.ppermute(x, 'seq', [(i, i ^ 1) for i in range(seq_count)])  2.71 us
  transfers between devices with their start and end apart: 32, of which 12 were waited for; matrix products, arithmetic and copies ran while one was open for 10% of the time, Pallas kernels for 10%

profile of v4, /device:TPU:0, one launch (start us, length us, event | category | flops | bytes accessed | tf_op | source)
XLA Modules:
  0.0 80.5 jit_solution(14491084569074974871)
XLA Ops:
  0.7 1.1 %fusion.9 = (bf16[128,256]{1,0:T(8,128)(2,1)S(1)}, bf16[128,256]{1,0:T(8,128)(2,1)S(1)}, bf16[128,256]{1,0:T(8,128)(2,1)S(1)}, bf16[128,256]{1,0:T(8,128)(2,1)S(1)}) fusion(bf16[128,512]{1,0:T(8,128)(2,1)} %bitcast.51, bf16[128,512]{1,0:T(8,128)(2,1)} %bitcast.52), kind=kLoop, calls=%fused_computation.45 | loop fusion | bytes 524288 | tf_op jit(solution)/shard_map/slice | solution.py:347
  1.7 3.1 %collective-permute-start = (bf16[128,512]{1,0:T(8,128)(2,1)S(1)}, bf16[128,512]{1,0:T(8,128)(2,1)S(1)}, u32[]{:S(2)}, u32[]{:S(2)}) collective-permute-start(bf16[128,512]{1,0:T(8,128)(2,1)S(1)} %pad_maximum_fusion.1.refs_0_), channel_id=1, source_target_pairs={{0,2},{1,3},{2,4},{3,5},{4,6},{5,7},{6,0},{7,1},{8,10},{9,11},{10,... | collective-permute-start | bytes 393224 | tf_op jit(solution)/shard_map/ppermute | solution.py:331
  4.8 2.6 %collective-permute-start.1 = (bf16[128,512]{1,0:T(8,128)(2,1)S(1)}, bf16[128,512]{1,0:T(8,128)(2,1)S(1)}, u32[]{:S(2)}, u32[]{:S(2)}) collective-permute-start(bf16[128,512]{1,0:T(8,128)(2,1)S(1)} %pad_maximum_fusion.1.refs_0_), channel_id=1, source_target_pairs={{0,4},{1,5},{2,6},{3,7},{4,0},{5,1},{6,2},{7,3},{8,12},{9,13},{10,... | collective-permute-start | bytes 393224 | tf_op jit(solution)/shard_map/ppermute | solution.py:331
  7.4 1.3 %collective-permute-start.2 = (bf16[128,512]{1,0:T(8,128)(2,1)S(1)}, bf16[128,512]{1,0:T(8,128)(2,1)S(1)}, u32[]{:S(2)}, u32[]{:S(2)}) collective-permute-start(bf16[128,512]{1,0:T(8,128)(2,1)S(1)} %pad_maximum_fusion.1.refs_0_), channel_id=1, source_target_pairs={{0,6},{1,7},{2,0},{3,1},{4,2},{5,3},{6,4},{7,5},{8,14},{9,15},{10,... | collective-permute-start | bytes 393224 | tf_op jit(solution)/shard_map/ppermute | solution.py:331
  10.2 1.5 %collective-permute-start.14 = (bf16[512,256]{1,0:T(8,128)(2,1)}, bf16[512,256]{1,0:T(8,128)(2,1)}, u32[]{:S(2)}, u32[]{:S(2)}) collective-permute-start(bf16[512,256]{1,0:T(8,128)(2,1)} %dynamic-slice_bitcast_fusion), channel_id=1, source_target_pairs={{0,8},{8,0},{16,24},{24,16},{1,9},{9,1},{17,25},{25,17},{2,10},{10... | collective-permute-start | bytes 786440 | tf_op jit(solution)/shard_map/ppermute | solution.py:340
  12.9 1.5 %reshape.106 = bf16[4,128,1024]{2,1,0:T(8,128)(2,1)} reshape(bf16[4,128,2,4,128]{4,3,2,1,0:T(4,128)(2,1)S(1)} %bitcast.50) | data formatting | bytes 2097152 | tf_op jit(solution)/shard_map/reshape | solution.py:376
  14.4 3.6 %all-to-all-start = ((bf16[4,128,1024]{2,1,0:T(8,128)(2,1)}), bf16[4,128,1024]{2,1,0:T(8,128)(2,1)S(1)}, u32[]{:S(2)}, u32[]{:S(2)}) async-start(bf16[4,128,1024]{2,1,0:T(8,128)(2,1)} %reshape.106), calls=%async_computation | async-start | bytes 2097152 | tf_op jit(solution)/shard_map/all_to_all | solution.py:377
  21.7 1.1 %broadcast_select_fusion = bf16[512,256]{1,0:T(8,128)(2,1)S(1)} fusion(bf16[512,256]{1,0:T(8,128)(2,1)} %collective-permute-done.14, pred[512]{0:T(512)(128)(4,1)S(1)} %broadcast_bitcast_fusion, bf16[1,1024,256]{2,1,0:T(8,128)(2,1)S(1)} %copy-done.3, s32[]{:T(128)S(6)} %select_n.65), kind=kLoop, calls=%fused_computation.3 | loop fusion | flops 131072 | bytes 786948 | tf_op jit(solution)/shard_map/jit(_where)/select_n | solution.py:369
  23.4 3.4 %collective-permute-start.9 = (bf16[128,512]{1,0:T(8,128)(2,1)S(1)}, bf16[128,512]{1,0:T(8,128)(2,1)S(1)}, u32[]{:S(2)}, u32[]{:S(2)}) collective-permute-start(bf16[128,512]{1,0:T(8,128)(2,1)S(1)} %pad_maximum_fusion.refs_0_), channel_id=1, source_target_pairs={{0,6},{1,7},{2,0},{3,1},{4,2},{5,3},{6,4},{7,5},{8,14},{9,15},{10,... | collective-permute-start | bytes 393224 | tf_op jit(solution)/shard_map/ppermute | solution.py:331
  26.8 1.6 %collective-permute-start.15 = (bf16[512,256]{1,0:T(8,128)(2,1)S(1)}, bf16[512,256]{1,0:T(8,128)(2,1)S(1)}, u32[]{:S(2)}, u32[]{:S(2)}) collective-permute-start(bf16[512,256]{1,0:T(8,128)(2,1)S(1)} %broadcast_select_fusion), channel_id=1, source_target_pairs={{0,16},{8,24},{16,0},{24,8},{1,17},{9,25},{17,1},{25,9},{2,18},{10... | collective-permute-start | bytes 786440 | tf_op jit(solution)/shard_map/ppermute | solution.py:340
  28.4 1.2 %copy-done.1 = bf16[1,128,4096]{2,1,0:T(8,128)(2,1)S(1)} copy-done((bf16[1,128,4096]{2,1,0:T(8,128)(2,1)S(1)}, bf16[1,128,4096]{2,1,0:T(8,128)(2,1)}, u32[]{:S(2)}) %copy-start.1) | copy-done | bytes 1048600
  29.6 3.6 %attention_backward.2 = (bf16[128,2048]{1,0:T(8,128)(2,1)S(1)}, bf16[1024,512]{1,0:T(8,128)(2,1)S(1)}) custom-call(s32[160]{0:T(256)S(1)} %reshape.105.table_ref, bf16[128,4096]{1,0:T(8,128)(2,1)S(1)} %bitcast.46, bf16[128,4096]{1,0:T(8,128)(2,1)S(1)} %bitcast.48, bf16[128,512]{1,0:T(8,128)(2,1)S(1)} %pad_maximum_fusion.1.refs_0_, ...), custom_call_target="tpu_custom_call" | custom-call | flops 10066329600 | bytes 4194304 | tf_op jit(solution)/shard_map/attention_backward/pallas_call | solution.py:154
  34.2 1.9 %collective-permute-done.15 = bf16[512,256]{1,0:T(8,128)(2,1)S(1)} collective-permute-done((bf16[512,256]{1,0:T(8,128)(2,1)S(1)}, bf16[512,256]{1,0:T(8,128)(2,1)S(1)}, u32[]{:S(2)}, u32[]{:S(2)}) %collective-permute-start.15) | collective-permute-done | bytes 262176 | tf_op jit(solution)/shard_map/ppermute | solution.py:340
  36.4 3.9 %attention_backward.3 = (bf16[128,2048]{1,0:T(8,128)(2,1)S(1)}, bf16[1024,512]{1,0:T(8,128)(2,1)S(1)}) custom-call(s32[160]{0:T(256)S(1)} %reshape.105.table_ref, bf16[128,4096]{1,0:T(8,128)(2,1)S(1)} %bitcast.47, bf16[128,4096]{1,0:T(8,128)(2,1)S(1)} %bitcast.49, bf16[128,512]{1,0:T(8,128)(2,1)S(1)} %pad_maximum_fusion.refs_0_, ...), custom_call_target="tpu_custom_call" | custom-call | flops 10066329600 | bytes 4194304 | tf_op jit(solution)/shard_map/attention_backward/pallas_call | solution.py:154
  41.1 1.1 %collective-permute-start.17 = (bf16[512,256]{1,0:T(8,128)(2,1)S(1)}, bf16[512,256]{1,0:T(8,128)(2,1)S(1)}, u32[]{:S(2)}, u32[]{:S(2)}) collective-permute-start(bf16[512,256]{1,0:T(8,128)(2,1)S(1)} %get-tuple-element.41), channel_id=1, source_target_pairs={{0,1},{1,0},{2,3},{3,2},{4,5},{5,4},{6,7},{7,6},{8,9},{9,8},{10,11... | collective-permute-start | bytes 786440 | tf_op jit(solution)/shard_map/ppermute | solution.py:327
  42.1 1.2 %collective-permute-done.17.came_ref = bf16[512,256]{1,0:T(8,128)(2,1)S(1)} collective-permute-done((bf16[512,256]{1,0:T(8,128)(2,1)S(1)}, bf16[512,256]{1,0:T(8,128)(2,1)S(1)}, u32[]{:S(2)}, u32[]{:S(2)}) %collective-permute-start.17) | collective-permute-done | bytes 262176 | tf_op jit(solution)/shard_map/ppermute | solution.py:327
  43.3 4.1 %collective-permute-start.18 = (bf16[128,256]{1,0:T(8,128)(2,1)S(1)}, bf16[128,256]{1,0:T(8,128)(2,1)S(1)}, u32[]{:S(2)}, u32[]{:S(2)}) collective-permute-start(bf16[128,256]{1,0:T(8,128)(2,1)S(1)} %get-tuple-element.43), channel_id=1, source_target_pairs={{0,6},{1,7},{2,0},{3,1},{4,2},{5,3},{6,4},{7,5},{8,14},{9,15},{10,... | collective-permute-start | bytes 196616 | tf_op jit(solution)/shard_map/ppermute | solution.py:331
  48.1 1.7 %collective-permute-done.18 = bf16[128,256]{1,0:T(8,128)(2,1)S(1)} collective-permute-done((bf16[128,256]{1,0:T(8,128)(2,1)S(1)}, bf16[128,256]{1,0:T(8,128)(2,1)S(1)}, u32[]{:S(2)}, u32[]{:S(2)}) %collective-permute-start.18) | collective-permute-done | bytes 65568 | tf_op jit(solution)/shard_map/ppermute | solution.py:331
  49.9 4.4 %collective-permute-done.19 = bf16[128,256]{1,0:T(8,128)(2,1)S(1)} collective-permute-done((bf16[128,256]{1,0:T(8,128)(2,1)S(1)}, bf16[128,256]{1,0:T(8,128)(2,1)S(1)}, u32[]{:S(2)}, u32[]{:S(2)}) %collective-permute-start.19) | collective-permute-done | bytes 65568 | tf_op jit(solution)/shard_map/ppermute | solution.py:331
  54.3 1.5 %collective-permute-start.21 = (bf16[128,256]{1,0:T(8,128)(2,1)S(1)}, bf16[128,256]{1,0:T(8,128)(2,1)S(1)}, u32[]{:S(2)}, u32[]{:S(2)}) collective-permute-start(bf16[128,256]{1,0:T(8,128)(2,1)S(1)} %add_convert_fusion.1.refs_0_), channel_id=1, source_target_pairs={{0,8},{8,0},{16,24},{24,16},{1,9},{9,1},{17,25},{25,17},{2,10},{10... | collective-permute-start | bytes 196616 | tf_op jit(solution)/shard_map/ppermute | solution.py:340
  55.8 1.1 %collective-permute-start.22 = (bf16[128,256]{1,0:T(8,128)(2,1)S(1)}, bf16[128,256]{1,0:T(8,128)(2,1)S(1)}, u32[]{:S(2)}, u32[]{:S(2)}) collective-permute-start(bf16[128,256]{1,0:T(8,128)(2,1)S(1)} %add_convert_fusion.1.refs_0_), channel_id=1, source_target_pairs={{0,16},{8,24},{16,0},{24,8},{1,17},{9,25},{17,1},{25,9},{2,18},{10... | collective-permute-start | bytes 196616 | tf_op jit(solution)/shard_map/ppermute | solution.py:340
  58.6 2.2 %collective-permute-done.22.refs_2_ = bf16[128,256]{1,0:T(8,128)(2,1)S(1)} collective-permute-done((bf16[128,256]{1,0:T(8,128)(2,1)S(1)}, bf16[128,256]{1,0:T(8,128)(2,1)S(1)}, u32[]{:S(2)}, u32[]{:S(2)}) %collective-permute-start.22) | collective-permute-done | bytes 65568 | tf_op jit(solution)/shard_map/ppermute | solution.py:340
  60.7 1.3 %collective-permute-done.23.refs_3_ = bf16[128,256]{1,0:T(8,128)(2,1)S(1)} collective-permute-done((bf16[128,256]{1,0:T(8,128)(2,1)S(1)}, bf16[128,256]{1,0:T(8,128)(2,1)S(1)}, u32[]{:S(2)}, u32[]{:S(2)}) %collective-permute-start.23) | collective-permute-done | bytes 65568 | tf_op jit(solution)/shard_map/ppermute | solution.py:340
  62.6 1.5 %collective-permute-done.24.came_ref = bf16[512,256]{1,0:T(8,128)(2,1)S(1)} collective-permute-done((bf16[512,256]{1,0:T(8,128)(2,1)S(1)}, bf16[512,256]{1,0:T(8,128)(2,1)S(1)}, u32[]{:S(2)}, u32[]{:S(2)}) %collective-permute-start.24) | collective-permute-done | bytes 262176 | tf_op jit(solution)/shard_map/ppermute | solution.py:327
  64.3 2.0 %collective-permute-start.26 = (bf16[128,256]{1,0:T(8,128)(2,1)S(1)}, bf16[128,256]{1,0:T(8,128)(2,1)S(1)}, u32[]{:S(2)}, u32[]{:S(2)}) collective-permute-start(bf16[128,256]{1,0:T(8,128)(2,1)S(1)} %get-tuple-element.50), channel_id=1, source_target_pairs={{0,4},{1,5},{2,6},{3,7},{4,0},{5,1},{6,2},{7,3},{8,12},{9,13},{10,... | collective-permute-start | bytes 196616 | tf_op jit(solution)/shard_map/ppermute | solution.py:331
  66.3 2.3 %collective-permute-start.27 = (bf16[128,256]{1,0:T(8,128)(2,1)S(1)}, bf16[128,256]{1,0:T(8,128)(2,1)S(1)}, u32[]{:S(2)}, u32[]{:S(2)}) collective-permute-start(bf16[128,256]{1,0:T(8,128)(2,1)S(1)} %get-tuple-element.51), channel_id=1, source_target_pairs={{0,6},{1,7},{2,0},{3,1},{4,2},{5,3},{6,4},{7,5},{8,14},{9,15},{10,... | collective-permute-start | bytes 196616 | tf_op jit(solution)/shard_map/ppermute | solution.py:331
  68.6 2.5 %collective-permute-done.25 = bf16[128,256]{1,0:T(8,128)(2,1)S(1)} collective-permute-done((bf16[128,256]{1,0:T(8,128)(2,1)S(1)}, bf16[128,256]{1,0:T(8,128)(2,1)S(1)}, u32[]{:S(2)}, u32[]{:S(2)}) %collective-permute-start.25) | collective-permute-done | bytes 65568 | tf_op jit(solution)/shard_map/ppermute | solution.py:331
  71.1 1.9 %collective-permute-done.26 = bf16[128,256]{1,0:T(8,128)(2,1)S(1)} collective-permute-done((bf16[128,256]{1,0:T(8,128)(2,1)S(1)}, bf16[128,256]{1,0:T(8,128)(2,1)S(1)}, u32[]{:S(2)}, u32[]{:S(2)}) %collective-permute-start.26) | collective-permute-done | bytes 65568 | tf_op jit(solution)/shard_map/ppermute | solution.py:331
  73.6 0.9 %collective-permute-start.29 = (bf16[128,256]{1,0:T(8,128)(2,1)S(1)}, bf16[128,256]{1,0:T(8,128)(2,1)S(1)}, u32[]{:S(2)}, u32[]{:S(2)}) collective-permute-start(bf16[128,256]{1,0:T(8,128)(2,1)S(1)} %add_convert_fusion.refs_0_), channel_id=1, source_target_pairs={{0,16},{8,24},{16,0},{24,8},{1,17},{9,25},{17,1},{25,9},{2,18},{10... | collective-permute-start | bytes 196616 | tf_op jit(solution)/shard_map/ppermute | solution.py:340
  74.5 2.0 %collective-permute-start.30 = (bf16[128,256]{1,0:T(8,128)(2,1)S(1)}, bf16[128,256]{1,0:T(8,128)(2,1)S(1)}, u32[]{:S(2)}, u32[]{:S(2)}) collective-permute-start(bf16[128,256]{1,0:T(8,128)(2,1)S(1)} %add_convert_fusion.refs_0_), channel_id=1, source_target_pairs={{0,24},{8,16},{16,8},{24,0},{1,25},{9,17},{17,9},{25,1},{2,26},{10... | collective-permute-start | bytes 196616 | tf_op jit(solution)/shard_map/ppermute | solution.py:340
  76.5 1.0 %maximum_bitcast_fusion = bf16[1,128,4096]{2,1,0:T(8,128)(2,1)} fusion(bf16[128,2048]{1,0:T(8,128)(2,1)S(1)} %get-tuple-element.37, bf16[128,2048]{1,0:T(8,128)(2,1)S(1)} %get-tuple-element.31), kind=kLoop, calls=%fused_computation | loop fusion | flops 2097152 | bytes 2097152 | tf_op jit(solution)/shard_map/broadcast_in_dim | solution.py:405
  77.9 1.8 %collective-permute-done.30.refs_3_ = bf16[128,256]{1,0:T(8,128)(2,1)S(1)} collective-permute-done((bf16[128,256]{1,0:T(8,128)(2,1)S(1)}, bf16[128,256]{1,0:T(8,128)(2,1)S(1)}, u32[]{:S(2)}, u32[]{:S(2)}) %collective-permute-start.30) | collective-permute-done | bytes 65568 | tf_op jit(solution)/shard_map/ppermute | solution.py:340
  (79 shorter events, 13.8 us)
Async XLA Ops:
  1.7 18.9 %collective-permute-start = (bf16[128,512]{1,0:T(8,128)(2,1)S(1)}, bf16[128,512]{1,0:T(8,128)(2,1)S(1)}, u32[]{:S(2)}, u32[]{:S(2)}) collective-permute-start(bf16[128,512]{1,0:T(8,128)(2,1)S(1)} %pad_maximum_fusion.1.refs_0_), channel_id=1, source_target_pairs={{0,2},{1,3},{2,4},{3,5},{4,6},{5,7},{6,0},{7,1},{8,10},{9,11},{10,... | collective-permute-start | bytes 393224 | tf_op jit(solution)/shard_map/ppermute | solution.py:331
  4.8 15.8 %collective-permute-start.1 = (bf16[128,512]{1,0:T(8,128)(2,1)S(1)}, bf16[128,512]{1,0:T(8,128)(2,1)S(1)}, u32[]{:S(2)}, u32[]{:S(2)}) collective-permute-start(bf16[128,512]{1,0:T(8,128)(2,1)S(1)} %pad_maximum_fusion.1.refs_0_), channel_id=1, source_target_pairs={{0,4},{1,5},{2,6},{3,7},{4,0},{5,1},{6,2},{7,3},{8,12},{9,13},{10,... | collective-permute-start | bytes 393224 | tf_op jit(solution)/shard_map/ppermute | solution.py:331
  7.4 13.2 %collective-permute-start.2 = (bf16[128,512]{1,0:T(8,128)(2,1)S(1)}, bf16[128,512]{1,0:T(8,128)(2,1)S(1)}, u32[]{:S(2)}, u32[]{:S(2)}) collective-permute-start(bf16[128,512]{1,0:T(8,128)(2,1)S(1)} %pad_maximum_fusion.1.refs_0_), channel_id=1, source_target_pairs={{0,6},{1,7},{2,0},{3,1},{4,2},{5,3},{6,4},{7,5},{8,14},{9,15},{10,... | collective-permute-start | bytes 393224 | tf_op jit(solution)/shard_map/ppermute | solution.py:331
  8.8 24.5 %collective-permute-start.7 = (bf16[128,512]{1,0:T(8,128)(2,1)S(1)}, bf16[128,512]{1,0:T(8,128)(2,1)S(1)}, u32[]{:S(2)}, u32[]{:S(2)}) collective-permute-start(bf16[128,512]{1,0:T(8,128)(2,1)S(1)} %pad_maximum_fusion.refs_0_), channel_id=1, source_target_pairs={{0,2},{1,3},{2,4},{3,5},{4,6},{5,7},{6,0},{7,1},{8,10},{9,11},{10,... | collective-permute-start | bytes 393224 | tf_op jit(solution)/shard_map/ppermute | solution.py:331
  10.2 11.1 %collective-permute-start.14 = (bf16[512,256]{1,0:T(8,128)(2,1)}, bf16[512,256]{1,0:T(8,128)(2,1)}, u32[]{:S(2)}, u32[]{:S(2)}) collective-permute-start(bf16[512,256]{1,0:T(8,128)(2,1)} %dynamic-slice_bitcast_fusion), channel_id=1, source_target_pairs={{0,8},{8,0},{16,24},{24,16},{1,9},{9,1},{17,25},{25,17},{2,10},{10... | collective-permute-start | bytes 786440 | tf_op jit(solution)/shard_map/ppermute | solution.py:340
  14.4 43.4 %all-to-all-start = ((bf16[4,128,1024]{2,1,0:T(8,128)(2,1)}), bf16[4,128,1024]{2,1,0:T(8,128)(2,1)S(1)}, u32[]{:S(2)}, u32[]{:S(2)}) async-start(bf16[4,128,1024]{2,1,0:T(8,128)(2,1)} %reshape.106), calls=%async_computation | async-start | bytes 2097152 | tf_op jit(solution)/shard_map/all_to_all | solution.py:377
  20.7 2.2 %collective-permute-start.3 = (bf16[128,512]{1,0:T(8,128)(2,1)S(1)}, bf16[128,512]{1,0:T(8,128)(2,1)S(1)}, u32[]{:S(2)}, u32[]{:S(2)}) collective-permute-start(bf16[128,512]{1,0:T(8,128)(2,1)S(1)} %pad_maximum_fusion.1.refs_0_), channel_id=1, source_target_pairs={{0,1},{1,0},{2,3},{3,2},{4,5},{5,4},{6,7},{7,6},{8,9},{9,8},{10,11... | collective-permute-start | bytes 393224 | tf_op jit(solution)/shard_map/ppermute | solution.py:327
  20.7 2.3 %collective-permute-start.4 = (bf16[128,512]{1,0:T(8,128)(2,1)S(1)}, bf16[128,512]{1,0:T(8,128)(2,1)S(1)}, u32[]{:S(2)}, u32[]{:S(2)}) collective-permute-start(bf16[128,512]{1,0:T(8,128)(2,1)S(1)} %collective-permute-done.refs_1_), channel_id=1, source_target_pairs={{0,1},{1,0},{2,3},{3,2},{4,5},{5,4},{6,7},{7,6},{8,9},{9,8},{10,11... | collective-permute-start | bytes 393224 | tf_op jit(solution)/shard_map/ppermute | solution.py:327
  21.2 2.2 %collective-permute-start.5 = (bf16[128,512]{1,0:T(8,128)(2,1)S(1)}, bf16[128,512]{1,0:T(8,128)(2,1)S(1)}, u32[]{:S(2)}, u32[]{:S(2)}) collective-permute-start(bf16[128,512]{1,0:T(8,128)(2,1)S(1)} %collective-permute-done.1.refs_2_), channel_id=1, source_target_pairs={{0,1},{1,0},{2,3},{3,2},{4,5},{5,4},{6,7},{7,6},{8,9},{9,8},{10,11... | collective-permute-start | bytes 393224 | tf_op jit(solution)/shard_map/ppermute | solution.py:327
  21.3 5.5 %collective-permute-start.6 = (bf16[128,512]{1,0:T(8,128)(2,1)S(1)}, bf16[128,512]{1,0:T(8,128)(2,1)S(1)}, u32[]{:S(2)}, u32[]{:S(2)}) collective-permute-start(bf16[128,512]{1,0:T(8,128)(2,1)S(1)} %collective-permute-done.2.refs_3_), channel_id=1, source_target_pairs={{0,1},{1,0},{2,3},{3,2},{4,5},{5,4},{6,7},{7,6},{8,9},{9,8},{10,11... | collective-permute-start | bytes 393224 | tf_op jit(solution)/shard_map/ppermute | solution.py:327
  22.8 13.5 %collective-permute-start.10 = (bf16[128,512]{1,0:T(8,128)(2,1)S(1)}, bf16[128,512]{1,0:T(8,128)(2,1)S(1)}, u32[]{:S(2)}, u32[]{:S(2)}) collective-permute-start(bf16[128,512]{1,0:T(8,128)(2,1)S(1)} %pad_maximum_fusion.refs_0_), channel_id=1, source_target_pairs={{0,1},{1,0},{2,3},{3,2},{4,5},{5,4},{6,7},{7,6},{8,9},{9,8},{10,11... | collective-permute-start | bytes 393224 | tf_op jit(solution)/shard_map/ppermute | solution.py:327
  23.0 10.3 %collective-permute-start.8 = (bf16[128,512]{1,0:T(8,128)(2,1)S(1)}, bf16[128,512]{1,0:T(8,128)(2,1)S(1)}, u32[]{:S(2)}, u32[]{:S(2)}) collective-permute-start(bf16[128,512]{1,0:T(8,128)(2,1)S(1)} %pad_maximum_fusion.refs_0_), channel_id=1, source_target_pairs={{0,4},{1,5},{2,6},{3,7},{4,0},{5,1},{6,2},{7,3},{8,12},{9,13},{10,... | collective-permute-start | bytes 393224 | tf_op jit(solution)/shard_map/ppermute | solution.py:331
  23.4 9.9 %collective-permute-start.9 = (bf16[128,512]{1,0:T(8,128)(2,1)S(1)}, bf16[128,512]{1,0:T(8,128)(2,1)S(1)}, u32[]{:S(2)}, u32[]{:S(2)}) collective-permute-start(bf16[128,512]{1,0:T(8,128)(2,1)S(1)} %pad_maximum_fusion.refs_0_), channel_id=1, source_target_pairs={{0,6},{1,7},{2,0},{3,1},{4,2},{5,3},{6,4},{7,5},{8,14},{9,15},{10,... | collective-permute-start | bytes 393224 | tf_op jit(solution)/shard_map/ppermute | solution.py:331
  26.8 9.4 %collective-permute-start.15 = (bf16[512,256]{1,0:T(8,128)(2,1)S(1)}, bf16[512,256]{1,0:T(8,128)(2,1)S(1)}, u32[]{:S(2)}, u32[]{:S(2)}) collective-permute-start(bf16[512,256]{1,0:T(8,128)(2,1)S(1)} %broadcast_select_fusion), channel_id=1, source_target_pairs={{0,16},{8,24},{16,0},{24,8},{1,17},{9,25},{17,1},{25,9},{2,18},{10... | collective-permute-start | bytes 786440 | tf_op jit(solution)/shard_map/ppermute | solution.py:340
  33.3 3.1 %collective-permute-start.11 = (bf16[128,512]{1,0:T(8,128)(2,1)S(1)}, bf16[128,512]{1,0:T(8,128)(2,1)S(1)}, u32[]{:S(2)}, u32[]{:S(2)}) collective-permute-start(bf16[128,512]{1,0:T(8,128)(2,1)S(1)} %collective-permute-done.7.refs_1_), channel_id=1, source_target_pairs={{0,1},{1,0},{2,3},{3,2},{4,5},{5,4},{6,7},{7,6},{8,9},{9,8},{10,11... | collective-permute-start | bytes 393224 | tf_op jit(solution)/shard_map/ppermute | solution.py:327
  33.7 2.7 %collective-permute-start.12 = (bf16[128,512]{1,0:T(8,128)(2,1)S(1)}, bf16[128,512]{1,0:T(8,128)(2,1)S(1)}, u32[]{:S(2)}, u32[]{:S(2)}) collective-permute-start(bf16[128,512]{1,0:T(8,128)(2,1)S(1)} %collective-permute-done.8.refs_2_), channel_id=1, source_target_pairs={{0,1},{1,0},{2,3},{3,2},{4,5},{5,4},{6,7},{7,6},{8,9},{9,8},{10,11... | collective-permute-start | bytes 393224 | tf_op jit(solution)/shard_map/ppermute | solution.py:327
  33.8 2.6 %collective-permute-start.13 = (bf16[128,512]{1,0:T(8,128)(2,1)S(1)}, bf16[128,512]{1,0:T(8,128)(2,1)S(1)}, u32[]{:S(2)}, u32[]{:S(2)}) collective-permute-start(bf16[128,512]{1,0:T(8,128)(2,1)S(1)} %collective-permute-done.9.refs_3_), channel_id=1, source_target_pairs={{0,1},{1,0},{2,3},{3,2},{4,5},{5,4},{6,7},{7,6},{8,9},{9,8},{10,11... | collective-permute-start | bytes 393224 | tf_op jit(solution)/shard_map/ppermute | solution.py:327
  36.3 4.0 %collective-permute-start.16 = (bf16[512,256]{1,0:T(8,128)(2,1)S(1)}, bf16[512,256]{1,0:T(8,128)(2,1)S(1)}, u32[]{:S(2)}, u32[]{:S(2)}) collective-permute-start(bf16[512,256]{1,0:T(8,128)(2,1)S(1)} %broadcast_select_fusion.1.mine_ref), channel_id=1, source_target_pairs={{0,1},{1,0},{2,3},{3,2},{4,5},{5,4},{6,7},{7,6},{8,9},{9,8},{10,11... | collective-permute-start | bytes 786440 | tf_op jit(solution)/shard_map/ppermute | solution.py:327
  41.1 2.2 %collective-permute-start.17 = (bf16[512,256]{1,0:T(8,128)(2,1)S(1)}, bf16[512,256]{1,0:T(8,128)(2,1)S(1)}, u32[]{:S(2)}, u32[]{:S(2)}) collective-permute-start(bf16[512,256]{1,0:T(8,128)(2,1)S(1)} %get-tuple-element.41), channel_id=1, source_target_pairs={{0,1},{1,0},{2,3},{3,2},{4,5},{5,4},{6,7},{7,6},{8,9},{9,8},{10,11... | collective-permute-start | bytes 786440 | tf_op jit(solution)/shard_map/ppermute | solution.py:327
  43.3 6.5 %collective-permute-start.18 = (bf16[128,256]{1,0:T(8,128)(2,1)S(1)}, bf16[128,256]{1,0:T(8,128)(2,1)S(1)}, u32[]{:S(2)}, u32[]{:S(2)}) collective-permute-start(bf16[128,256]{1,0:T(8,128)(2,1)S(1)} %get-tuple-element.43), channel_id=1, source_target_pairs={{0,6},{1,7},{2,0},{3,1},{4,2},{5,3},{6,4},{7,5},{8,14},{9,15},{10,... | collective-permute-start | bytes 196616 | tf_op jit(solution)/shard_map/ppermute | solution.py:331
  47.4 6.8 %collective-permute-start.19 = (bf16[128,256]{1,0:T(8,128)(2,1)S(1)}, bf16[128,256]{1,0:T(8,128)(2,1)S(1)}, u32[]{:S(2)}, u32[]{:S(2)}) collective-permute-start(bf16[128,256]{1,0:T(8,128)(2,1)S(1)} %get-tuple-element.44), channel_id=1, source_target_pairs={{0,4},{1,5},{2,6},{3,7},{4,0},{5,1},{6,2},{7,3},{8,12},{9,13},{10,... | collective-permute-start | bytes 196616 | tf_op jit(solution)/shard_map/ppermute | solution.py:331
  47.4 6.8 %collective-permute-start.20 = (bf16[128,256]{1,0:T(8,128)(2,1)S(1)}, bf16[128,256]{1,0:T(8,128)(2,1)S(1)}, u32[]{:S(2)}, u32[]{:S(2)}) collective-permute-start(bf16[128,256]{1,0:T(8,128)(2,1)S(1)} %get-tuple-element.45), channel_id=1, source_target_pairs={{0,2},{1,3},{2,4},{3,5},{4,6},{5,7},{6,0},{7,1},{8,10},{9,11},{10,... | collective-permute-start | bytes 196616 | tf_op jit(solution)/shard_map/ppermute | solution.py:331
  54.3 4.3 %collective-permute-start.21 = (bf16[128,256]{1,0:T(8,128)(2,1)S(1)}, bf16[128,256]{1,0:T(8,128)(2,1)S(1)}, u32[]{:S(2)}, u32[]{:S(2)}) collective-permute-start(bf16[128,256]{1,0:T(8,128)(2,1)S(1)} %add_convert_fusion.1.refs_0_), channel_id=1, source_target_pairs={{0,8},{8,0},{16,24},{24,16},{1,9},{9,1},{17,25},{25,17},{2,10},{10... | collective-permute-start | bytes 196616 | tf_op jit(solution)/shard_map/ppermute | solution.py:340
  55.8 5.0 %collective-permute-start.22 = (bf16[128,256]{1,0:T(8,128)(2,1)S(1)}, bf16[128,256]{1,0:T(8,128)(2,1)S(1)}, u32[]{:S(2)}, u32[]{:S(2)}) collective-permute-start(bf16[128,256]{1,0:T(8,128)(2,1)S(1)} %add_convert_fusion.1.refs_0_), channel_id=1, source_target_pairs={{0,16},{8,24},{16,0},{24,8},{1,17},{9,25},{17,1},{25,9},{2,18},{10... | collective-permute-start | bytes 196616 | tf_op jit(solution)/shard_map/ppermute | solution.py:340
  56.9 5.2 %collective-permute-start.23 = (bf16[128,256]{1,0:T(8,128)(2,1)S(1)}, bf16[128,256]{1,0:T(8,128)(2,1)S(1)}, u32[]{:S(2)}, u32[]{:S(2)}) collective-permute-start(bf16[128,256]{1,0:T(8,128)(2,1)S(1)} %add_convert_fusion.1.refs_0_), channel_id=1, source_target_pairs={{0,24},{8,16},{16,8},{24,0},{1,25},{9,17},{17,9},{25,1},{2,26},{10... | collective-permute-start | bytes 196616 | tf_op jit(solution)/shard_map/ppermute | solution.py:340
  62.6 1.6 %collective-permute-start.24 = (bf16[512,256]{1,0:T(8,128)(2,1)S(1)}, bf16[512,256]{1,0:T(8,128)(2,1)S(1)}, u32[]{:S(2)}, u32[]{:S(2)}) collective-permute-start(bf16[512,256]{1,0:T(8,128)(2,1)S(1)} %get-tuple-element.47), channel_id=1, source_target_pairs={{0,1},{1,0},{2,3},{3,2},{4,5},{5,4},{6,7},{7,6},{8,9},{9,8},{10,11... | collective-permute-start | bytes 786440 | tf_op jit(solution)/shard_map/ppermute | solution.py:327
  64.2 6.8 %collective-permute-start.25 = (bf16[128,256]{1,0:T(8,128)(2,1)S(1)}, bf16[128,256]{1,0:T(8,128)(2,1)S(1)}, u32[]{:S(2)}, u32[]{:S(2)}) collective-permute-start(bf16[128,256]{1,0:T(8,128)(2,1)S(1)} %get-tuple-element.49), channel_id=1, source_target_pairs={{0,2},{1,3},{2,4},{3,5},{4,6},{5,7},{6,0},{7,1},{8,10},{9,11},{10,... | collective-permute-start | bytes 196616 | tf_op jit(solution)/shard_map/ppermute | solution.py:331
  64.3 8.6 %collective-permute-start.26 = (bf16[128,256]{1,0:T(8,128)(2,1)S(1)}, bf16[128,256]{1,0:T(8,128)(2,1)S(1)}, u32[]{:S(2)}, u32[]{:S(2)}) collective-permute-start(bf16[128,256]{1,0:T(8,128)(2,1)S(1)} %get-tuple-element.50), channel_id=1, source_target_pairs={{0,4},{1,5},{2,6},{3,7},{4,0},{5,1},{6,2},{7,3},{8,12},{9,13},{10,... | collective-permute-start | bytes 196616 | tf_op jit(solution)/shard_map/ppermute | solution.py:331
  66.3 6.7 %collective-permute-start.27 = (bf16[128,256]{1,0:T(8,128)(2,1)S(1)}, bf16[128,256]{1,0:T(8,128)(2,1)S(1)}, u32[]{:S(2)}, u32[]{:S(2)}) collective-permute-start(bf16[128,256]{1,0:T(8,128)(2,1)S(1)} %get-tuple-element.51), channel_id=1, source_target_pairs={{0,6},{1,7},{2,0},{3,1},{4,2},{5,3},{6,4},{7,5},{8,14},{9,15},{10,... | collective-permute-start | bytes 196616 | tf_op jit(solution)/shard_map/ppermute | solution.py:331
  73.0 4.6 %collective-permute-start.28 = (bf16[128,256]{1,0:T(8,128)(2,1)S(1)}, bf16[128,256]{1,0:T(8,128)(2,1)S(1)}, u32[]{:S(2)}, u32[]{:S(2)}) collective-permute-start(bf16[128,256]{1,0:T(8,128)(2,1)S(1)} %add_convert_fusion.refs_0_), channel_id=1, source_target_pairs={{0,8},{8,0},{16,24},{24,16},{1,9},{9,1},{17,25},{25,17},{2,10},{10... | collective-permute-start | bytes 196616 | tf_op jit(solution)/shard_map/ppermute | solution.py:340
  73.6 4.3 %collective-permute-start.29 = (bf16[128,256]{1,0:T(8,128)(2,1)S(1)}, bf16[128,256]{1,0:T(8,128)(2,1)S(1)}, u32[]{:S(2)}, u32[]{:S(2)}) collective-permute-start(bf16[128,256]{1,0:T(8,128)(2,1)S(1)} %add_convert_fusion.refs_0_), channel_id=1, source_target_pairs={{0,16},{8,24},{16,0},{24,8},{1,17},{9,25},{17,1},{25,9},{2,18},{10... | collective-permute-start | bytes 196616 | tf_op jit(solution)/shard_map/ppermute | solution.py:340
  74.5 5.2 %collective-permute-start.30 = (bf16[128,256]{1,0:T(8,128)(2,1)S(1)}, bf16[128,256]{1,0:T(8,128)(2,1)S(1)}, u32[]{:S(2)}, u32[]{:S(2)}) collective-permute-start(bf16[128,256]{1,0:T(8,128)(2,1)S(1)} %add_convert_fusion.refs_0_), channel_id=1, source_target_pairs={{0,24},{8,16},{16,8},{24,0},{1,25},{9,17},{17,9},{25,1},{2,26},{10... | collective-permute-start | bytes 196616 | tf_op jit(solution)/shard_map/ppermute | solution.py:340
  (5 other events, 40.8 us)

commit v5 on v4

--- a/solution.py
+++ b/solution.py
@@ -313,6 +313,30 @@
     )(*parts)
 
 
+def split_kernel(x_ref, out_ref, *, chips):
+    dp_count, _, width = out_ref.shape
+    share = width // (2 * chips)
+    for place in range(2 * chips):
+        to = (place % 2 * chips + place // 2) * share
+        for group in range(dp_count):
+            at = (place * dp_count + group) * share
+            out_ref[group, :, to : to + share] = x_ref[:, at : at + share]
+
+
+def split_input(x, chips, dp_count):
+    features = x.shape[1]
+    share = features // (2 * chips * dp_count)
+    if share % 128 != 0:
+        pieces = jnp.transpose(x.reshape(BLOCK, chips, 2, dp_count, share), (3, 0, 2, 1, 4))
+        return pieces.reshape(dp_count, BLOCK, features // dp_count)
+    return pl.pallas_call(
+        partial(split_kernel, chips=chips),
+        out_shape=jax.ShapeDtypeStruct((dp_count, BLOCK, features // dp_count), bf16),
+        compiler_params=pltpu.CompilerParams(vmem_limit_bytes=16 * 1024 * 1024),
+        name="split_input",
+    )(x)
+
+
 def local(queries, keys, values, grad_out, layer_input, basis_store, owner, layout):
     seq_count = lax.axis_size("seq")
     dp_count = lax.axis_size("dp")
@@ -351,7 +375,7 @@
         kv = packed(chunk)
         same = [kv]
         for step in range(1, chips):
-            if chunk and step == 2:
+            if chunk and step == 3:
                 kv, arrived[chunk - 1] = lax.optimization_barrier((kv, arrived[chunk - 1]))
             same.append(up(kv, step))
         arrived.append(same)
@@ -371,9 +395,7 @@
     mine = mine.reshape(half.shape)
     other = pair(mine)
 
-    share = layer_input.shape[2] // (seq_count * dp_count)
-    x_pieces = layer_input[0].reshape(BLOCK, chips, 2, dp_count, share)
-    x_pieces = jnp.transpose(x_pieces, (3, 0, 2, 1, 4)).reshape(dp_count, BLOCK, seq_count * share)
+    x_pieces = split_input(layer_input[0], chips, dp_count)
     x_all = lax.all_to_all(x_pieces, "dp", 0, 0, tiled=True)
 
     query_grads, grads = [], []

time: 81.1 us -> 79.5 us (0.980)
  local copies, waits for them, and re-layouts: 6.34 us -> 3.64 us
  starting transfers between devices: 37.9 us -> 39.5 us
  waiting for transfers between devices: 21.5 us -> 19.9 us
  Pallas kernels: 9.69 us -> 10.9 us
    reshape x1 -> x0, local copies, waits for them, and re-layouts: 1.55 us -> none  [local(): jnp.transpose(x_pieces, (3, 0, 2, 1, 4))]
    ppermute x12, starting transfers between devices: 20.6 us -> 22 us  [around(): return lax.ppermute(x, 'seq', moves)]
    pallas_call x0 -> x1, Pallas kernels: none -> 1.25 us  [split_input(): pl.pallas_call(partial(split_kernel, chips=chips), out_shape=jax.ShapeDty...]
    another operation x2 -> x0, local copies, waits for them, and re-layouts: 1.16 us -> none  [local(): x_pieces = layer_input[0].reshape(BLOCK, chips, 2, dp_count, share)]
    ppermute x8, waiting for transfers between devices: 8.27 us -> 7.17 us  [across(): return lax.ppermute(x, 'dp', [(i, i ^ step) for i in range(dp_count)])]
  transfers between devices with their start and end apart: 32 -> 32, of which waited for: 12 -> 12; matrix products, arithmetic and copies ran while one was open for 10% -> 7% of each run, Pallas kernels for 10% -> 12%
where the time goes in v5:
time: 79.5 us; the launch traced here: 79.1 us
  starting transfers between devices  39.5 us (50%)
  waiting for transfers between devices  19.9 us (25%)
  Pallas kernels  10.9 us (14%)
  other arithmetic  4.25 us (5%)
  local copies, waits for them, and re-layouts  3.64 us (5%)
  between operations  0.88 us (1%)
    ppermute x12, starting transfers between devices, around(): return lax.ppermute(x, 'seq', moves)  22 us
    ppermute x8, starting transfers between devices, across(): return lax.ppermute(x, 'dp', [(i, i ^ step) for i in range(dp_count)])  10.2 us
    ppermute x12, waiting for transfers between devices, around(): return lax.ppermute(x, 'seq', moves)  10 us
    pallas_call x2, Pallas kernels, attention(): pl.pallas_call(body, in_specs=[pl.BlockSpec(memory_space=pltpu.SMEM)] + [...  7.42 us
    ppermute x8, waiting for transfers between devices, across(): return lax.ppermute(x, 'dp', [(i, i ^ step) for i in range(dp_count)])  7.17 us
    all_to_all x1, starting transfers between devices, local(): x_all = lax.all_to_all(x_pieces, 'dp', 0, 0, tiled=True)  3.65 us
    ppermute x11, starting transfers between devices, pair(): return lax.ppermute(x, 'seq', [(i, i ^ 1) for i in range(seq_count)])  3.65 us
    ppermute x11, waiting for transfers between devices, pair(): return lax.ppermute(x, 'seq', [(i, i ^ 1) for i in range(seq_count)])  2.71 us
  transfers between devices with their start and end apart: 32, of which 12 were waited for; matrix products, arithmetic and copies ran while one was open for 7% of the time, Pallas kernels for 12%

profile of v5, /device:TPU:0, one launch (start us, length us, event | category | flops | bytes accessed | tf_op | source)
XLA Modules:
  0.0 79.1 jit_solution(17538742163489304752)
XLA Ops:
  0.7 1.1 %fusion.9 = (bf16[128,256]{1,0:T(8,128)(2,1)S(1)}, bf16[128,256]{1,0:T(8,128)(2,1)S(1)}, bf16[128,256]{1,0:T(8,128)(2,1)S(1)}, bf16[128,256]{1,0:T(8,128)(2,1)S(1)}) fusion(bf16[128,512]{1,0:T(8,128)(2,1)} %bitcast.49, bf16[128,512]{1,0:T(8,128)(2,1)} %bitcast.50), kind=kLoop, calls=%fused_computation.44 | loop fusion | bytes 524288 | tf_op jit(solution)/shard_map/slice | solution.py:371
  1.7 3.1 %collective-permute-start = (bf16[128,512]{1,0:T(8,128)(2,1)S(1)}, bf16[128,512]{1,0:T(8,128)(2,1)S(1)}, u32[]{:S(2)}, u32[]{:S(2)}) collective-permute-start(bf16[128,512]{1,0:T(8,128)(2,1)S(1)} %pad_maximum_fusion.1.refs_0_), channel_id=1, source_target_pairs={{0,2},{1,3},{2,4},{3,5},{4,6},{5,7},{6,0},{7,1},{8,10},{9,11},{10,... | collective-permute-start | bytes 393224 | tf_op jit(solution)/shard_map/ppermute | solution.py:355
  4.8 2.6 %collective-permute-start.1 = (bf16[128,512]{1,0:T(8,128)(2,1)S(1)}, bf16[128,512]{1,0:T(8,128)(2,1)S(1)}, u32[]{:S(2)}, u32[]{:S(2)}) collective-permute-start(bf16[128,512]{1,0:T(8,128)(2,1)S(1)} %pad_maximum_fusion.1.refs_0_), channel_id=1, source_target_pairs={{0,4},{1,5},{2,6},{3,7},{4,0},{5,1},{6,2},{7,3},{8,12},{9,13},{10,... | collective-permute-start | bytes 393224 | tf_op jit(solution)/shard_map/ppermute | solution.py:355
  7.4 1.3 %collective-permute-start.2 = (bf16[128,512]{1,0:T(8,128)(2,1)S(1)}, bf16[128,512]{1,0:T(8,128)(2,1)S(1)}, u32[]{:S(2)}, u32[]{:S(2)}) collective-permute-start(bf16[128,512]{1,0:T(8,128)(2,1)S(1)} %pad_maximum_fusion.1.refs_0_), channel_id=1, source_target_pairs={{0,6},{1,7},{2,0},{3,1},{4,2},{5,3},{6,4},{7,5},{8,14},{9,15},{10,... | collective-permute-start | bytes 393224 | tf_op jit(solution)/shard_map/ppermute | solution.py:355
  10.2 1.5 %collective-permute-start.14 = (bf16[512,256]{1,0:T(8,128)(2,1)}, bf16[512,256]{1,0:T(8,128)(2,1)}, u32[]{:S(2)}, u32[]{:S(2)}) collective-permute-start(bf16[512,256]{1,0:T(8,128)(2,1)} %dynamic-slice_bitcast_fusion), channel_id=1, source_target_pairs={{0,8},{8,0},{16,24},{24,16},{1,9},{9,1},{17,25},{25,17},{2,10},{10... | collective-permute-start | bytes 786440 | tf_op jit(solution)/shard_map/ppermute | solution.py:364
  11.7 1.3 %split_input.1 = bf16[4,128,1024]{2,1,0:T(8,128)(2,1)} custom-call(bf16[128,4096]{1,0:T(8,128)(2,1)S(1)} %bitcast.44), custom_call_target="tpu_custom_call" | custom-call | tf_op jit(solution)/shard_map/split_input/pallas_call | solution.py:332
  13.0 3.6 %all-to-all-start = ((bf16[4,128,1024]{2,1,0:T(8,128)(2,1)}), bf16[4,128,1024]{2,1,0:T(8,128)(2,1)S(1)}, u32[]{:S(2)}, u32[]{:S(2)}) async-start(bf16[4,128,1024]{2,1,0:T(8,128)(2,1)} %split_input.1), calls=%async_computation | async-start | bytes 2097152 | tf_op jit(solution)/shard_map/all_to_all | solution.py:399
  20.3 1.1 %broadcast_select_fusion = bf16[512,256]{1,0:T(8,128)(2,1)S(1)} fusion(bf16[512,256]{1,0:T(8,128)(2,1)} %collective-permute-done.14, pred[512]{0:T(512)(128)(4,1)S(1)} %broadcast_bitcast_fusion, bf16[1,1024,256]{2,1,0:T(8,128)(2,1)S(1)} %copy-done.3, s32[]{:T(128)S(6)} %select_n.65), kind=kLoop, calls=%fused_computation.2 | loop fusion | flops 131072 | bytes 786948 | tf_op jit(solution)/shard_map/jit(_where)/select_n | solution.py:393
  21.4 1.9 %collective-permute-start.8 = (bf16[128,512]{1,0:T(8,128)(2,1)S(1)}, bf16[128,512]{1,0:T(8,128)(2,1)S(1)}, u32[]{:S(2)}, u32[]{:S(2)}) collective-permute-start(bf16[128,512]{1,0:T(8,128)(2,1)S(1)} %pad_maximum_fusion.refs_0_), channel_id=1, source_target_pairs={{0,4},{1,5},{2,6},{3,7},{4,0},{5,1},{6,2},{7,3},{8,12},{9,13},{10,... | collective-permute-start | bytes 393224 | tf_op jit(solution)/shard_map/ppermute | solution.py:355
  23.3 3.4 %collective-permute-start.9 = (bf16[128,512]{1,0:T(8,128)(2,1)S(1)}, bf16[128,512]{1,0:T(8,128)(2,1)S(1)}, u32[]{:S(2)}, u32[]{:S(2)}) collective-permute-start(bf16[128,512]{1,0:T(8,128)(2,1)S(1)} %pad_maximum_fusion.refs_0_), channel_id=1, source_target_pairs={{0,6},{1,7},{2,0},{3,1},{4,2},{5,3},{6,4},{7,5},{8,14},{9,15},{10,... | collective-permute-start | bytes 393224 | tf_op jit(solution)/shard_map/ppermute | solution.py:355
  26.8 1.5 %collective-permute-start.15 = (bf16[512,256]{1,0:T(8,128)(2,1)S(1)}, bf16[512,256]{1,0:T(8,128)(2,1)S(1)}, u32[]{:S(2)}, u32[]{:S(2)}) collective-permute-start(bf16[512,256]{1,0:T(8,128)(2,1)S(1)} %broadcast_select_fusion), channel_id=1, source_target_pairs={{0,16},{8,24},{16,0},{24,8},{1,17},{9,25},{17,1},{25,9},{2,18},{10... | collective-permute-start | bytes 786440 | tf_op jit(solution)/shard_map/ppermute | solution.py:364
  28.3 1.2 %copy-done.2 = bf16[1,128,4096]{2,1,0:T(8,128)(2,1)S(1)} copy-done((bf16[1,128,4096]{2,1,0:T(8,128)(2,1)S(1)}, bf16[1,128,4096]{2,1,0:T(8,128)(2,1)}, u32[]{:S(2)}) %copy-start.2) | copy-done | bytes 1048600
  29.5 3.6 %attention_backward.2 = (bf16[128,2048]{1,0:T(8,128)(2,1)S(1)}, bf16[1024,512]{1,0:T(8,128)(2,1)S(1)}) custom-call(s32[160]{0:T(256)S(1)} %reshape.102.table_ref, bf16[128,4096]{1,0:T(8,128)(2,1)S(1)} %bitcast.45, bf16[128,4096]{1,0:T(8,128)(2,1)S(1)} %bitcast.47, bf16[128,512]{1,0:T(8,128)(2,1)S(1)} %pad_maximum_fusion.1.refs_0_, ...), custom_call_target="tpu_custom_call" | custom-call | flops 10066329600 | bytes 4194304 | tf_op jit(solution)/shard_map/attention_backward/pallas_call | solution.py:154
  35.4 3.8 %attention_backward.3 = (bf16[128,2048]{1,0:T(8,128)(2,1)S(1)}, bf16[1024,512]{1,0:T(8,128)(2,1)S(1)}) custom-call(s32[160]{0:T(256)S(1)} %reshape.102.table_ref, bf16[128,4096]{1,0:T(8,128)(2,1)S(1)} %bitcast.46, bf16[128,4096]{1,0:T(8,128)(2,1)S(1)} %bitcast.48, bf16[128,512]{1,0:T(8,128)(2,1)S(1)} %pad_maximum_fusion.refs_0_, ...), custom_call_target="tpu_custom_call" | custom-call | flops 10066329600 | bytes 4194304 | tf_op jit(solution)/shard_map/attention_backward/pallas_call | solution.py:154
  40.0 1.2 %collective-permute-start.17 = (bf16[512,256]{1,0:T(8,128)(2,1)S(1)}, bf16[512,256]{1,0:T(8,128)(2,1)S(1)}, u32[]{:S(2)}, u32[]{:S(2)}) collective-permute-start(bf16[512,256]{1,0:T(8,128)(2,1)S(1)} %get-tuple-element.41), channel_id=1, source_target_pairs={{0,1},{1,0},{2,3},{3,2},{4,5},{5,4},{6,7},{7,6},{8,9},{9,8},{10,11... | collective-permute-start | bytes 786440 | tf_op jit(solution)/shard_map/ppermute | solution.py:351
  41.2 1.2 %collective-permute-done.17.came_ref = bf16[512,256]{1,0:T(8,128)(2,1)S(1)} collective-permute-done((bf16[512,256]{1,0:T(8,128)(2,1)S(1)}, bf16[512,256]{1,0:T(8,128)(2,1)S(1)}, u32[]{:S(2)}, u32[]{:S(2)}) %collective-permute-start.17) | collective-permute-done | bytes 262176 | tf_op jit(solution)/shard_map/ppermute | solution.py:351
  42.5 3.4 %collective-permute-start.18 = (bf16[128,256]{1,0:T(8,128)(2,1)S(1)}, bf16[128,256]{1,0:T(8,128)(2,1)S(1)}, u32[]{:S(2)}, u32[]{:S(2)}) collective-permute-start(bf16[128,256]{1,0:T(8,128)(2,1)S(1)} %get-tuple-element.43), channel_id=1, source_target_pairs={{0,6},{1,7},{2,0},{3,1},{4,2},{5,3},{6,4},{7,5},{8,14},{9,15},{10,... | collective-permute-start | bytes 196616 | tf_op jit(solution)/shard_map/ppermute | solution.py:355
  46.5 1.8 %collective-permute-done.18 = bf16[128,256]{1,0:T(8,128)(2,1)S(1)} collective-permute-done((bf16[128,256]{1,0:T(8,128)(2,1)S(1)}, bf16[128,256]{1,0:T(8,128)(2,1)S(1)}, u32[]{:S(2)}, u32[]{:S(2)}) %collective-permute-start.18) | collective-permute-done | bytes 65568 | tf_op jit(solution)/shard_map/ppermute | solution.py:355
  48.3 4.4 %collective-permute-done.19 = bf16[128,256]{1,0:T(8,128)(2,1)S(1)} collective-permute-done((bf16[128,256]{1,0:T(8,128)(2,1)S(1)}, bf16[128,256]{1,0:T(8,128)(2,1)S(1)}, u32[]{:S(2)}, u32[]{:S(2)}) %collective-permute-start.19) | collective-permute-done | bytes 65568 | tf_op jit(solution)/shard_map/ppermute | solution.py:355
  52.7 2.0 %collective-permute-start.21 = (bf16[128,256]{1,0:T(8,128)(2,1)S(1)}, bf16[128,256]{1,0:T(8,128)(2,1)S(1)}, u32[]{:S(2)}, u32[]{:S(2)}) collective-permute-start(bf16[128,256]{1,0:T(8,128)(2,1)S(1)} %add_convert_fusion.1.refs_0_), channel_id=1, source_target_pairs={{0,8},{8,0},{16,24},{24,16},{1,9},{9,1},{17,25},{25,17},{2,10},{10... | collective-permute-start | bytes 196616 | tf_op jit(solution)/shard_map/ppermute | solution.py:364
  56.3 0.9 %collective-permute-done.21.refs_1_ = bf16[128,256]{1,0:T(8,128)(2,1)S(1)} collective-permute-done((bf16[128,256]{1,0:T(8,128)(2,1)S(1)}, bf16[128,256]{1,0:T(8,128)(2,1)S(1)}, u32[]{:S(2)}, u32[]{:S(2)}) %collective-permute-start.21) | collective-permute-done | bytes 65568 | tf_op jit(solution)/shard_map/ppermute | solution.py:364
  57.3 2.2 %collective-permute-done.22.refs_2_ = bf16[128,256]{1,0:T(8,128)(2,1)S(1)} collective-permute-done((bf16[128,256]{1,0:T(8,128)(2,1)S(1)}, bf16[128,256]{1,0:T(8,128)(2,1)S(1)}, u32[]{:S(2)}, u32[]{:S(2)}) %collective-permute-start.22) | collective-permute-done | bytes 65568 | tf_op jit(solution)/shard_map/ppermute | solution.py:364
  59.4 1.2 %collective-permute-done.23.refs_3_ = bf16[128,256]{1,0:T(8,128)(2,1)S(1)} collective-permute-done((bf16[128,256]{1,0:T(8,128)(2,1)S(1)}, bf16[128,256]{1,0:T(8,128)(2,1)S(1)}, u32[]{:S(2)}, u32[]{:S(2)}) %collective-permute-start.23) | collective-permute-done | bytes 65568 | tf_op jit(solution)/shard_map/ppermute | solution.py:364
  61.2 1.5 %collective-permute-done.24.came_ref = bf16[512,256]{1,0:T(8,128)(2,1)S(1)} collective-permute-done((bf16[512,256]{1,0:T(8,128)(2,1)S(1)}, bf16[512,256]{1,0:T(8,128)(2,1)S(1)}, u32[]{:S(2)}, u32[]{:S(2)}) %collective-permute-start.24) | collective-permute-done | bytes 262176 | tf_op jit(solution)/shard_map/ppermute | solution.py:351
  63.2 2.1 %collective-permute-start.26 = (bf16[128,256]{1,0:T(8,128)(2,1)S(1)}, bf16[128,256]{1,0:T(8,128)(2,1)S(1)}, u32[]{:S(2)}, u32[]{:S(2)}) collective-permute-start(bf16[128,256]{1,0:T(8,128)(2,1)S(1)} %get-tuple-element.50), channel_id=1, source_target_pairs={{0,4},{1,5},{2,6},{3,7},{4,0},{5,1},{6,2},{7,3},{8,12},{9,13},{10,... | collective-permute-start | bytes 196616 | tf_op jit(solution)/shard_map/ppermute | solution.py:355
  65.4 2.3 %collective-permute-start.27 = (bf16[128,256]{1,0:T(8,128)(2,1)S(1)}, bf16[128,256]{1,0:T(8,128)(2,1)S(1)}, u32[]{:S(2)}, u32[]{:S(2)}) collective-permute-start(bf16[128,256]{1,0:T(8,128)(2,1)S(1)} %get-tuple-element.51), channel_id=1, source_target_pairs={{0,6},{1,7},{2,0},{3,1},{4,2},{5,3},{6,4},{7,5},{8,14},{9,15},{10,... | collective-permute-start | bytes 196616 | tf_op jit(solution)/shard_map/ppermute | solution.py:355
  67.7 1.9 %collective-permute-done.25 = bf16[128,256]{1,0:T(8,128)(2,1)S(1)} collective-permute-done((bf16[128,256]{1,0:T(8,128)(2,1)S(1)}, bf16[128,256]{1,0:T(8,128)(2,1)S(1)}, u32[]{:S(2)}, u32[]{:S(2)}) %collective-permute-start.25) | collective-permute-done | bytes 65568 | tf_op jit(solution)/shard_map/ppermute | solution.py:355
  69.6 1.9 %collective-permute-done.26 = bf16[128,256]{1,0:T(8,128)(2,1)S(1)} collective-permute-done((bf16[128,256]{1,0:T(8,128)(2,1)S(1)}, bf16[128,256]{1,0:T(8,128)(2,1)S(1)}, u32[]{:S(2)}, u32[]{:S(2)}) %collective-permute-start.26) | collective-permute-done | bytes 65568 | tf_op jit(solution)/shard_map/ppermute | solution.py:355
  72.1 0.9 %collective-permute-start.29 = (bf16[128,256]{1,0:T(8,128)(2,1)S(1)}, bf16[128,256]{1,0:T(8,128)(2,1)S(1)}, u32[]{:S(2)}, u32[]{:S(2)}) collective-permute-start(bf16[128,256]{1,0:T(8,128)(2,1)S(1)} %add_convert_fusion.refs_0_), channel_id=1, source_target_pairs={{0,16},{8,24},{16,0},{24,8},{1,17},{9,25},{17,1},{25,9},{2,18},{10... | collective-permute-start | bytes 196616 | tf_op jit(solution)/shard_map/ppermute | solution.py:364
  73.0 2.0 %collective-permute-start.30 = (bf16[128,256]{1,0:T(8,128)(2,1)S(1)}, bf16[128,256]{1,0:T(8,128)(2,1)S(1)}, u32[]{:S(2)}, u32[]{:S(2)}) collective-permute-start(bf16[128,256]{1,0:T(8,128)(2,1)S(1)} %add_convert_fusion.refs_0_), channel_id=1, source_target_pairs={{0,24},{8,16},{16,8},{24,0},{1,25},{9,17},{17,9},{25,1},{2,26},{10... | collective-permute-start | bytes 196616 | tf_op jit(solution)/shard_map/ppermute | solution.py:364
  75.1 1.0 %maximum_bitcast_fusion = bf16[1,128,4096]{2,1,0:T(8,128)(2,1)} fusion(bf16[128,2048]{1,0:T(8,128)(2,1)S(1)} %get-tuple-element.37, bf16[128,2048]{1,0:T(8,128)(2,1)S(1)} %get-tuple-element.31), kind=kLoop, calls=%fused_computation | loop fusion | flops 2097152 | bytes 2097152 | tf_op jit(solution)/shard_map/broadcast_in_dim | solution.py:427
  76.4 1.8 %collective-permute-done.30.refs_3_ = bf16[128,256]{1,0:T(8,128)(2,1)S(1)} collective-permute-done((bf16[128,256]{1,0:T(8,128)(2,1)S(1)}, bf16[128,256]{1,0:T(8,128)(2,1)S(1)}, u32[]{:S(2)}, u32[]{:S(2)}) %collective-permute-start.30) | collective-permute-done | bytes 65568 | tf_op jit(solution)/shard_map/ppermute | solution.py:364
  (77 shorter events, 13.2 us)
Async XLA Ops:
  1.7 17.4 %collective-permute-start = (bf16[128,512]{1,0:T(8,128)(2,1)S(1)}, bf16[128,512]{1,0:T(8,128)(2,1)S(1)}, u32[]{:S(2)}, u32[]{:S(2)}) collective-permute-start(bf16[128,512]{1,0:T(8,128)(2,1)S(1)} %pad_maximum_fusion.1.refs_0_), channel_id=1, source_target_pairs={{0,2},{1,3},{2,4},{3,5},{4,6},{5,7},{6,0},{7,1},{8,10},{9,11},{10,... | collective-permute-start | bytes 393224 | tf_op jit(solution)/shard_map/ppermute | solution.py:355
  4.8 14.4 %collective-permute-start.1 = (bf16[128,512]{1,0:T(8,128)(2,1)S(1)}, bf16[128,512]{1,0:T(8,128)(2,1)S(1)}, u32[]{:S(2)}, u32[]{:S(2)}) collective-permute-start(bf16[128,512]{1,0:T(8,128)(2,1)S(1)} %pad_maximum_fusion.1.refs_0_), channel_id=1, source_target_pairs={{0,4},{1,5},{2,6},{3,7},{4,0},{5,1},{6,2},{7,3},{8,12},{9,13},{10,... | collective-permute-start | bytes 393224 | tf_op jit(solution)/shard_map/ppermute | solution.py:355
  7.4 11.8 %collective-permute-start.2 = (bf16[128,512]{1,0:T(8,128)(2,1)S(1)}, bf16[128,512]{1,0:T(8,128)(2,1)S(1)}, u32[]{:S(2)}, u32[]{:S(2)}) collective-permute-start(bf16[128,512]{1,0:T(8,128)(2,1)S(1)} %pad_maximum_fusion.1.refs_0_), channel_id=1, source_target_pairs={{0,6},{1,7},{2,0},{3,1},{4,2},{5,3},{6,4},{7,5},{8,14},{9,15},{10,... | collective-permute-start | bytes 393224 | tf_op jit(solution)/shard_map/ppermute | solution.py:355
  8.8 24.4 %collective-permute-start.7 = (bf16[128,512]{1,0:T(8,128)(2,1)S(1)}, bf16[128,512]{1,0:T(8,128)(2,1)S(1)}, u32[]{:S(2)}, u32[]{:S(2)}) collective-permute-start(bf16[128,512]{1,0:T(8,128)(2,1)S(1)} %pad_maximum_fusion.refs_0_), channel_id=1, source_target_pairs={{0,2},{1,3},{2,4},{3,5},{4,6},{5,7},{6,0},{7,1},{8,10},{9,11},{10,... | collective-permute-start | bytes 393224 | tf_op jit(solution)/shard_map/ppermute | solution.py:355
  10.2 9.6 %collective-permute-start.14 = (bf16[512,256]{1,0:T(8,128)(2,1)}, bf16[512,256]{1,0:T(8,128)(2,1)}, u32[]{:S(2)}, u32[]{:S(2)}) collective-permute-start(bf16[512,256]{1,0:T(8,128)(2,1)} %dynamic-slice_bitcast_fusion), channel_id=1, source_target_pairs={{0,8},{8,0},{16,24},{24,16},{1,9},{9,1},{17,25},{25,17},{2,10},{10... | collective-permute-start | bytes 786440 | tf_op jit(solution)/shard_map/ppermute | solution.py:364
  13.0 43.4 %all-to-all-start = ((bf16[4,128,1024]{2,1,0:T(8,128)(2,1)}), bf16[4,128,1024]{2,1,0:T(8,128)(2,1)S(1)}, u32[]{:S(2)}, u32[]{:S(2)}) async-start(bf16[4,128,1024]{2,1,0:T(8,128)(2,1)} %split_input.1), calls=%async_computation | async-start | bytes 2097152 | tf_op jit(solution)/shard_map/all_to_all | solution.py:399
  19.2 2.2 %collective-permute-start.3 = (bf16[128,512]{1,0:T(8,128)(2,1)S(1)}, bf16[128,512]{1,0:T(8,128)(2,1)S(1)}, u32[]{:S(2)}, u32[]{:S(2)}) collective-permute-start(bf16[128,512]{1,0:T(8,128)(2,1)S(1)} %pad_maximum_fusion.1.refs_0_), channel_id=1, source_target_pairs={{0,1},{1,0},{2,3},{3,2},{4,5},{5,4},{6,7},{7,6},{8,9},{9,8},{10,11... | collective-permute-start | bytes 393224 | tf_op jit(solution)/shard_map/ppermute | solution.py:351
  19.3 4.0 %collective-permute-start.4 = (bf16[128,512]{1,0:T(8,128)(2,1)S(1)}, bf16[128,512]{1,0:T(8,128)(2,1)S(1)}, u32[]{:S(2)}, u32[]{:S(2)}) collective-permute-start(bf16[128,512]{1,0:T(8,128)(2,1)S(1)} %collective-permute-done.refs_1_), channel_id=1, source_target_pairs={{0,1},{1,0},{2,3},{3,2},{4,5},{5,4},{6,7},{7,6},{8,9},{9,8},{10,11... | collective-permute-start | bytes 393224 | tf_op jit(solution)/shard_map/ppermute | solution.py:351
  19.8 3.6 %collective-permute-start.5 = (bf16[128,512]{1,0:T(8,128)(2,1)S(1)}, bf16[128,512]{1,0:T(8,128)(2,1)S(1)}, u32[]{:S(2)}, u32[]{:S(2)}) collective-permute-start(bf16[128,512]{1,0:T(8,128)(2,1)S(1)} %collective-permute-done.1.refs_2_), channel_id=1, source_target_pairs={{0,1},{1,0},{2,3},{3,2},{4,5},{5,4},{6,7},{7,6},{8,9},{9,8},{10,11... | collective-permute-start | bytes 393224 | tf_op jit(solution)/shard_map/ppermute | solution.py:351
  19.8 6.9 %collective-permute-start.6 = (bf16[128,512]{1,0:T(8,128)(2,1)S(1)}, bf16[128,512]{1,0:T(8,128)(2,1)S(1)}, u32[]{:S(2)}, u32[]{:S(2)}) collective-permute-start(bf16[128,512]{1,0:T(8,128)(2,1)S(1)} %collective-permute-done.2.refs_3_), channel_id=1, source_target_pairs={{0,1},{1,0},{2,3},{3,2},{4,5},{5,4},{6,7},{7,6},{8,9},{9,8},{10,11... | collective-permute-start | bytes 393224 | tf_op jit(solution)/shard_map/ppermute | solution.py:351
  21.4 11.8 %collective-permute-start.8 = (bf16[128,512]{1,0:T(8,128)(2,1)S(1)}, bf16[128,512]{1,0:T(8,128)(2,1)S(1)}, u32[]{:S(2)}, u32[]{:S(2)}) collective-permute-start(bf16[128,512]{1,0:T(8,128)(2,1)S(1)} %pad_maximum_fusion.refs_0_), channel_id=1, source_target_pairs={{0,4},{1,5},{2,6},{3,7},{4,0},{5,1},{6,2},{7,3},{8,12},{9,13},{10,... | collective-permute-start | bytes 393224 | tf_op jit(solution)/shard_map/ppermute | solution.py:355
  23.3 12.1 %collective-permute-start.10 = (bf16[128,512]{1,0:T(8,128)(2,1)S(1)}, bf16[128,512]{1,0:T(8,128)(2,1)S(1)}, u32[]{:S(2)}, u32[]{:S(2)}) collective-permute-start(bf16[128,512]{1,0:T(8,128)(2,1)S(1)} %pad_maximum_fusion.refs_0_), channel_id=1, source_target_pairs={{0,1},{1,0},{2,3},{3,2},{4,5},{5,4},{6,7},{7,6},{8,9},{9,8},{10,11... | collective-permute-start | bytes 393224 | tf_op jit(solution)/shard_map/ppermute | solution.py:351
  23.3 9.8 %collective-permute-start.9 = (bf16[128,512]{1,0:T(8,128)(2,1)S(1)}, bf16[128,512]{1,0:T(8,128)(2,1)S(1)}, u32[]{:S(2)}, u32[]{:S(2)}) collective-permute-start(bf16[128,512]{1,0:T(8,128)(2,1)S(1)} %pad_maximum_fusion.refs_0_), channel_id=1, source_target_pairs={{0,6},{1,7},{2,0},{3,1},{4,2},{5,3},{6,4},{7,5},{8,14},{9,15},{10,... | collective-permute-start | bytes 393224 | tf_op jit(solution)/shard_map/ppermute | solution.py:355
  26.8 8.4 %collective-permute-start.15 = (bf16[512,256]{1,0:T(8,128)(2,1)S(1)}, bf16[512,256]{1,0:T(8,128)(2,1)S(1)}, u32[]{:S(2)}, u32[]{:S(2)}) collective-permute-start(bf16[512,256]{1,0:T(8,128)(2,1)S(1)} %broadcast_select_fusion), channel_id=1, source_target_pairs={{0,16},{8,24},{16,0},{24,8},{1,17},{9,25},{17,1},{25,9},{2,18},{10... | collective-permute-start | bytes 786440 | tf_op jit(solution)/shard_map/ppermute | solution.py:364
  33.2 2.2 %collective-permute-start.11 = (bf16[128,512]{1,0:T(8,128)(2,1)S(1)}, bf16[128,512]{1,0:T(8,128)(2,1)S(1)}, u32[]{:S(2)}, u32[]{:S(2)}) collective-permute-start(bf16[128,512]{1,0:T(8,128)(2,1)S(1)} %collective-permute-done.7.refs_1_), channel_id=1, source_target_pairs={{0,1},{1,0},{2,3},{3,2},{4,5},{5,4},{6,7},{7,6},{8,9},{9,8},{10,11... | collective-permute-start | bytes 393224 | tf_op jit(solution)/shard_map/ppermute | solution.py:351
  33.8 1.6 %collective-permute-start.12 = (bf16[128,512]{1,0:T(8,128)(2,1)S(1)}, bf16[128,512]{1,0:T(8,128)(2,1)S(1)}, u32[]{:S(2)}, u32[]{:S(2)}) collective-permute-start(bf16[128,512]{1,0:T(8,128)(2,1)S(1)} %collective-permute-done.8.refs_2_), channel_id=1, source_target_pairs={{0,1},{1,0},{2,3},{3,2},{4,5},{5,4},{6,7},{7,6},{8,9},{9,8},{10,11... | collective-permute-start | bytes 393224 | tf_op jit(solution)/shard_map/ppermute | solution.py:351
  33.9 1.5 %collective-permute-start.13 = (bf16[128,512]{1,0:T(8,128)(2,1)S(1)}, bf16[128,512]{1,0:T(8,128)(2,1)S(1)}, u32[]{:S(2)}, u32[]{:S(2)}) collective-permute-start(bf16[128,512]{1,0:T(8,128)(2,1)S(1)} %collective-permute-done.9.refs_3_), channel_id=1, source_target_pairs={{0,1},{1,0},{2,3},{3,2},{4,5},{5,4},{6,7},{7,6},{8,9},{9,8},{10,11... | collective-permute-start | bytes 393224 | tf_op jit(solution)/shard_map/ppermute | solution.py:351
  35.3 3.9 %collective-permute-start.16 = (bf16[512,256]{1,0:T(8,128)(2,1)S(1)}, bf16[512,256]{1,0:T(8,128)(2,1)S(1)}, u32[]{:S(2)}, u32[]{:S(2)}) collective-permute-start(bf16[512,256]{1,0:T(8,128)(2,1)S(1)} %broadcast_select_fusion.1.mine_ref), channel_id=1, source_target_pairs={{0,1},{1,0},{2,3},{3,2},{4,5},{5,4},{6,7},{7,6},{8,9},{9,8},{10,11... | collective-permute-start | bytes 786440 | tf_op jit(solution)/shard_map/ppermute | solution.py:351
  40.0 2.4 %collective-permute-start.17 = (bf16[512,256]{1,0:T(8,128)(2,1)S(1)}, bf16[512,256]{1,0:T(8,128)(2,1)S(1)}, u32[]{:S(2)}, u32[]{:S(2)}) collective-permute-start(bf16[512,256]{1,0:T(8,128)(2,1)S(1)} %get-tuple-element.41), channel_id=1, source_target_pairs={{0,1},{1,0},{2,3},{3,2},{4,5},{5,4},{6,7},{7,6},{8,9},{9,8},{10,11... | collective-permute-start | bytes 786440 | tf_op jit(solution)/shard_map/ppermute | solution.py:351
  42.5 5.9 %collective-permute-start.18 = (bf16[128,256]{1,0:T(8,128)(2,1)S(1)}, bf16[128,256]{1,0:T(8,128)(2,1)S(1)}, u32[]{:S(2)}, u32[]{:S(2)}) collective-permute-start(bf16[128,256]{1,0:T(8,128)(2,1)S(1)} %get-tuple-element.43), channel_id=1, source_target_pairs={{0,6},{1,7},{2,0},{3,1},{4,2},{5,3},{6,4},{7,5},{8,14},{9,15},{10,... | collective-permute-start | bytes 196616 | tf_op jit(solution)/shard_map/ppermute | solution.py:355
  45.9 6.8 %collective-permute-start.19 = (bf16[128,256]{1,0:T(8,128)(2,1)S(1)}, bf16[128,256]{1,0:T(8,128)(2,1)S(1)}, u32[]{:S(2)}, u32[]{:S(2)}) collective-permute-start(bf16[128,256]{1,0:T(8,128)(2,1)S(1)} %get-tuple-element.44), channel_id=1, source_target_pairs={{0,4},{1,5},{2,6},{3,7},{4,0},{5,1},{6,2},{7,3},{8,12},{9,13},{10,... | collective-permute-start | bytes 196616 | tf_op jit(solution)/shard_map/ppermute | solution.py:355
  45.9 6.8 %collective-permute-start.20 = (bf16[128,256]{1,0:T(8,128)(2,1)S(1)}, bf16[128,256]{1,0:T(8,128)(2,1)S(1)}, u32[]{:S(2)}, u32[]{:S(2)}) collective-permute-start(bf16[128,256]{1,0:T(8,128)(2,1)S(1)} %get-tuple-element.45), channel_id=1, source_target_pairs={{0,2},{1,3},{2,4},{3,5},{4,6},{5,7},{6,0},{7,1},{8,10},{9,11},{10,... | collective-permute-start | bytes 196616 | tf_op jit(solution)/shard_map/ppermute | solution.py:355
  52.7 4.5 %collective-permute-start.21 = (bf16[128,256]{1,0:T(8,128)(2,1)S(1)}, bf16[128,256]{1,0:T(8,128)(2,1)S(1)}, u32[]{:S(2)}, u32[]{:S(2)}) collective-permute-start(bf16[128,256]{1,0:T(8,128)(2,1)S(1)} %add_convert_fusion.1.refs_0_), channel_id=1, source_target_pairs={{0,8},{8,0},{16,24},{24,16},{1,9},{9,1},{17,25},{25,17},{2,10},{10... | collective-permute-start | bytes 196616 | tf_op jit(solution)/shard_map/ppermute | solution.py:364
  54.8 4.6 %collective-permute-start.22 = (bf16[128,256]{1,0:T(8,128)(2,1)S(1)}, bf16[128,256]{1,0:T(8,128)(2,1)S(1)}, u32[]{:S(2)}, u32[]{:S(2)}) collective-permute-start(bf16[128,256]{1,0:T(8,128)(2,1)S(1)} %add_convert_fusion.1.refs_0_), channel_id=1, source_target_pairs={{0,16},{8,24},{16,0},{24,8},{1,17},{9,25},{17,1},{25,9},{2,18},{10... | collective-permute-start | bytes 196616 | tf_op jit(solution)/shard_map/ppermute | solution.py:364
  55.4 5.2 %collective-permute-start.23 = (bf16[128,256]{1,0:T(8,128)(2,1)S(1)}, bf16[128,256]{1,0:T(8,128)(2,1)S(1)}, u32[]{:S(2)}, u32[]{:S(2)}) collective-permute-start(bf16[128,256]{1,0:T(8,128)(2,1)S(1)} %add_convert_fusion.1.refs_0_), channel_id=1, source_target_pairs={{0,24},{8,16},{16,8},{24,0},{1,25},{9,17},{17,9},{25,1},{2,26},{10... | collective-permute-start | bytes 196616 | tf_op jit(solution)/shard_map/ppermute | solution.py:364
  61.1 1.6 %collective-permute-start.24 = (bf16[512,256]{1,0:T(8,128)(2,1)S(1)}, bf16[512,256]{1,0:T(8,128)(2,1)S(1)}, u32[]{:S(2)}, u32[]{:S(2)}) collective-permute-start(bf16[512,256]{1,0:T(8,128)(2,1)S(1)} %get-tuple-element.47), channel_id=1, source_target_pairs={{0,1},{1,0},{2,3},{3,2},{4,5},{5,4},{6,7},{7,6},{8,9},{9,8},{10,11... | collective-permute-start | bytes 786440 | tf_op jit(solution)/shard_map/ppermute | solution.py:351
  62.8 6.8 %collective-permute-start.25 = (bf16[128,256]{1,0:T(8,128)(2,1)S(1)}, bf16[128,256]{1,0:T(8,128)(2,1)S(1)}, u32[]{:S(2)}, u32[]{:S(2)}) collective-permute-start(bf16[128,256]{1,0:T(8,128)(2,1)S(1)} %get-tuple-element.49), channel_id=1, source_target_pairs={{0,2},{1,3},{2,4},{3,5},{4,6},{5,7},{6,0},{7,1},{8,10},{9,11},{10,... | collective-permute-start | bytes 196616 | tf_op jit(solution)/shard_map/ppermute | solution.py:355
  63.2 8.3 %collective-permute-start.26 = (bf16[128,256]{1,0:T(8,128)(2,1)S(1)}, bf16[128,256]{1,0:T(8,128)(2,1)S(1)}, u32[]{:S(2)}, u32[]{:S(2)}) collective-permute-start(bf16[128,256]{1,0:T(8,128)(2,1)S(1)} %get-tuple-element.50), channel_id=1, source_target_pairs={{0,4},{1,5},{2,6},{3,7},{4,0},{5,1},{6,2},{7,3},{8,12},{9,13},{10,... | collective-permute-start | bytes 196616 | tf_op jit(solution)/shard_map/ppermute | solution.py:355
  65.4 6.1 %collective-permute-start.27 = (bf16[128,256]{1,0:T(8,128)(2,1)S(1)}, bf16[128,256]{1,0:T(8,128)(2,1)S(1)}, u32[]{:S(2)}, u32[]{:S(2)}) collective-permute-start(bf16[128,256]{1,0:T(8,128)(2,1)S(1)} %get-tuple-element.51), channel_id=1, source_target_pairs={{0,6},{1,7},{2,0},{3,1},{4,2},{5,3},{6,4},{7,5},{8,14},{9,15},{10,... | collective-permute-start | bytes 196616 | tf_op jit(solution)/shard_map/ppermute | solution.py:355
  71.5 4.6 %collective-permute-start.28 = (bf16[128,256]{1,0:T(8,128)(2,1)S(1)}, bf16[128,256]{1,0:T(8,128)(2,1)S(1)}, u32[]{:S(2)}, u32[]{:S(2)}) collective-permute-start(bf16[128,256]{1,0:T(8,128)(2,1)S(1)} %add_convert_fusion.refs_0_), channel_id=1, source_target_pairs={{0,8},{8,0},{16,24},{24,16},{1,9},{9,1},{17,25},{25,17},{2,10},{10... | collective-permute-start | bytes 196616 | tf_op jit(solution)/shard_map/ppermute | solution.py:364
  72.1 4.3 %collective-permute-start.29 = (bf16[128,256]{1,0:T(8,128)(2,1)S(1)}, bf16[128,256]{1,0:T(8,128)(2,1)S(1)}, u32[]{:S(2)}, u32[]{:S(2)}) collective-permute-start(bf16[128,256]{1,0:T(8,128)(2,1)S(1)} %add_convert_fusion.refs_0_), channel_id=1, source_target_pairs={{0,16},{8,24},{16,0},{24,8},{1,17},{9,25},{17,1},{25,9},{2,18},{10... | collective-permute-start | bytes 196616 | tf_op jit(solution)/shard_map/ppermute | solution.py:364
  73.0 5.2 %collective-permute-start.30 = (bf16[128,256]{1,0:T(8,128)(2,1)S(1)}, bf16[128,256]{1,0:T(8,128)(2,1)S(1)}, u32[]{:S(2)}, u32[]{:S(2)}) collective-permute-start(bf16[128,256]{1,0:T(8,128)(2,1)S(1)} %add_convert_fusion.refs_0_), channel_id=1, source_target_pairs={{0,24},{8,16},{16,8},{24,0},{1,25},{9,17},{17,9},{25,1},{2,26},{10... | collective-permute-start | bytes 196616 | tf_op jit(solution)/shard_map/ppermute | solution.py:364
  (5 other events, 42.1 us)

commit v6 on v5

--- a/solution.py
+++ b/solution.py
@@ -173,9 +173,8 @@
         name="attention_backward",
     )(table, queries, grads, *kv_parts)
 
-def project_kernel(mine_ref, other_ref, *refs, chips, chunks):
-    grads_refs, refs = refs[:chunks], refs[chunks:]
-    keep_ref, send_ref, basis = refs
+def project_kernel(mine_ref, other_ref, *refs, chips, first):
+    grads_refs, out_ref, basis = refs[:-2], refs[-2], refs[-1]
     half = mine_ref.shape[0]
     core = lax.rem(lax.axis_index("seq"), 2)
 
@@ -200,18 +199,14 @@
         return mm(jnp.concatenate(keys + values, axis=1), chosen)
 
     for start in range(0, chips * BLOCK, tall):
-        send_ref[start : start + tall] = product(chips * BLOCK + start).astype(bf16)
-        keep_ref[start : start + tall] = product(start)
-
-
-def project(mine, other, grads, chips):
+        out_ref[start : start + tall] = product(first + start).astype(out_ref.dtype)
+
+
+def project(mine, other, grads, chips, first, dtype):
     rank = mine.shape[1]
     return pl.pallas_call(
-        partial(project_kernel, chips=chips, chunks=len(grads)),
-        out_shape=[
-            jax.ShapeDtypeStruct((chips * BLOCK, rank), f32),
-            jax.ShapeDtypeStruct((chips * BLOCK, rank), bf16),
-        ],
+        partial(project_kernel, chips=chips, first=first),
+        out_shape=jax.ShapeDtypeStruct((chips * BLOCK, rank), dtype),
         scratch_shapes=[pltpu.VMEM((2 * mine.shape[0], rank), bf16)],
         compiler_params=pltpu.CompilerParams(vmem_limit_bytes=32 * 1024 * 1024),
         name="project",
@@ -410,17 +405,19 @@
         grads.append(grad)
     grad_query = jnp.concatenate(query_grads, axis=1)
 
-    keep, send = project(mine, other, grads, chips)
+    send = project(mine, other, grads, chips, chips * BLOCK, bf16)
+    keep = project(mine, other, grads, chips, 0, f32)
     own, *sends = fold(keep, pair(send), chips)
+    order = sorted(range(1, chips), key=lambda step: abs(2 * step - chips))
     total = own
-    for step in range(1, chips):
+    for step in order:
         total = total + down(sends[step - 1], step).astype(f32)
     projected = total.astype(bf16)
     p_parts = [projected] + [across(projected, step) for step in range(1, dp_count)]
     kept, sent = outer(x_all, p_parts)
     own, *sends = deal(kept, pair(sent), chips)
     total = own
-    for step in range(1, chips):
+    for step in order:
         total = total + around(sends[step - 1], step).astype(f32)
     rows = total.astype(bf16)
     lowrank_grad = lay([rows] + [across(rows, step) for step in range(1, dp_count)])

time: 79.5 us -> 78.9 us (level)
  waiting for transfers between devices: 19.9 us -> 19.1 us
where the time goes in v6:
time: 78.9 us; the launch traced here: 78.4 us
  starting transfers between devices  39.4 us (50%)
  waiting for transfers between devices  19.1 us (24%)
  Pallas kernels  11.1 us (14%)
  other arithmetic  4.25 us (5%)
  local copies, waits for them, and re-layouts  3.64 us (5%)
  between operations  0.89 us (1%)
    ppermute x12, starting transfers between devices, around(): return lax.ppermute(x, 'seq', moves)  22 us
    ppermute x8, starting transfers between devices, across(): return lax.ppermute(x, 'dp', [(i, i ^ step) for i in range(dp_count)])  10.1 us
    ppermute x12, waiting for transfers between devices, around(): return lax.ppermute(x, 'seq', moves)  9.41 us
    ppermute x8, waiting for transfers between devices, across(): return lax.ppermute(x, 'dp', [(i, i ^ step) for i in range(dp_count)])  7.47 us
    pallas_call x2, Pallas kernels, attention(): pl.pallas_call(body, in_specs=[pl.BlockSpec(memory_space=pltpu.SMEM)] + [...  7.42 us
    ppermute x11, starting transfers between devices, pair(): return lax.ppermute(x, 'seq', [(i, i ^ 1) for i in range(seq_count)])  3.65 us
    all_to_all x1, starting transfers between devices, local(): x_all = lax.all_to_all(x_pieces, 'dp', 0, 0, tiled=True)  3.65 us
    ppermute x11, waiting for transfers between devices, pair(): return lax.ppermute(x, 'seq', [(i, i ^ 1) for i in range(seq_count)])  2.23 us
  transfers between devices with their start and end apart: 32, of which 12 were waited for; matrix products, arithmetic and copies ran while one was open for 7% of the time, Pallas kernels for 12%

profile of v6, /device:TPU:0, one launch (start us, length us, event | category | flops | bytes accessed | tf_op | source)
XLA Modules:
  0.0 78.4 jit_solution(6485965084708365663)
XLA Ops:
  0.7 1.1 %fusion.9 = (bf16[128,256]{1,0:T(8,128)(2,1)S(1)}, bf16[128,256]{1,0:T(8,128)(2,1)S(1)}, bf16[128,256]{1,0:T(8,128)(2,1)S(1)}, bf16[128,256]{1,0:T(8,128)(2,1)S(1)}) fusion(bf16[128,512]{1,0:T(8,128)(2,1)} %bitcast.49, bf16[128,512]{1,0:T(8,128)(2,1)} %bitcast.50), kind=kLoop, calls=%fused_computation.44 | loop fusion | bytes 524288 | tf_op jit(solution)/shard_map/slice | solution.py:366
  1.7 3.1 %collective-permute-start = (bf16[128,512]{1,0:T(8,128)(2,1)S(1)}, bf16[128,512]{1,0:T(8,128)(2,1)S(1)}, u32[]{:S(2)}, u32[]{:S(2)}) collective-permute-start(bf16[128,512]{1,0:T(8,128)(2,1)S(1)} %pad_maximum_fusion.1.refs_0_), channel_id=1, source_target_pairs={{0,2},{1,3},{2,4},{3,5},{4,6},{5,7},{6,0},{7,1},{8,10},{9,11},{10,... | collective-permute-start | bytes 393224 | tf_op jit(solution)/shard_map/ppermute | solution.py:350
  4.8 2.6 %collective-permute-start.1 = (bf16[128,512]{1,0:T(8,128)(2,1)S(1)}, bf16[128,512]{1,0:T(8,128)(2,1)S(1)}, u32[]{:S(2)}, u32[]{:S(2)}) collective-permute-start(bf16[128,512]{1,0:T(8,128)(2,1)S(1)} %pad_maximum_fusion.1.refs_0_), channel_id=1, source_target_pairs={{0,4},{1,5},{2,6},{3,7},{4,0},{5,1},{6,2},{7,3},{8,12},{9,13},{10,... | collective-permute-start | bytes 393224 | tf_op jit(solution)/shard_map/ppermute | solution.py:350
  7.4 1.3 %collective-permute-start.2 = (bf16[128,512]{1,0:T(8,128)(2,1)S(1)}, bf16[128,512]{1,0:T(8,128)(2,1)S(1)}, u32[]{:S(2)}, u32[]{:S(2)}) collective-permute-start(bf16[128,512]{1,0:T(8,128)(2,1)S(1)} %pad_maximum_fusion.1.refs_0_), channel_id=1, source_target_pairs={{0,6},{1,7},{2,0},{3,1},{4,2},{5,3},{6,4},{7,5},{8,14},{9,15},{10,... | collective-permute-start | bytes 393224 | tf_op jit(solution)/shard_map/ppermute | solution.py:350
  10.2 1.5 %collective-permute-start.14 = (bf16[512,256]{1,0:T(8,128)(2,1)}, bf16[512,256]{1,0:T(8,128)(2,1)}, u32[]{:S(2)}, u32[]{:S(2)}) collective-permute-start(bf16[512,256]{1,0:T(8,128)(2,1)} %dynamic-slice_bitcast_fusion), channel_id=1, source_target_pairs={{0,8},{8,0},{16,24},{24,16},{1,9},{9,1},{17,25},{25,17},{2,10},{10... | collective-permute-start | bytes 786440 | tf_op jit(solution)/shard_map/ppermute | solution.py:359
  11.7 1.3 %split_input.1 = bf16[4,128,1024]{2,1,0:T(8,128)(2,1)} custom-call(bf16[128,4096]{1,0:T(8,128)(2,1)S(1)} %bitcast.44), custom_call_target="tpu_custom_call" | custom-call | tf_op jit(solution)/shard_map/split_input/pallas_call | solution.py:327
  13.0 3.6 %all-to-all-start = ((bf16[4,128,1024]{2,1,0:T(8,128)(2,1)}), bf16[4,128,1024]{2,1,0:T(8,128)(2,1)S(1)}, u32[]{:S(2)}, u32[]{:S(2)}) async-start(bf16[4,128,1024]{2,1,0:T(8,128)(2,1)} %split_input.1), calls=%async_computation | async-start | bytes 2097152 | tf_op jit(solution)/shard_map/all_to_all | solution.py:394
  20.3 1.1 %broadcast_select_fusion = bf16[512,256]{1,0:T(8,128)(2,1)S(1)} fusion(bf16[512,256]{1,0:T(8,128)(2,1)} %collective-permute-done.14, pred[512]{0:T(512)(128)(4,1)S(1)} %broadcast_bitcast_fusion, bf16[1,1024,256]{2,1,0:T(8,128)(2,1)S(1)} %copy-done.3, s32[]{:T(128)S(6)} %select_n.65), kind=kLoop, calls=%fused_computation.2 | loop fusion | flops 131072 | bytes 786948 | tf_op jit(solution)/shard_map/jit(_where)/select_n | solution.py:388
  21.4 1.9 %collective-permute-start.8 = (bf16[128,512]{1,0:T(8,128)(2,1)S(1)}, bf16[128,512]{1,0:T(8,128)(2,1)S(1)}, u32[]{:S(2)}, u32[]{:S(2)}) collective-permute-start(bf16[128,512]{1,0:T(8,128)(2,1)S(1)} %pad_maximum_fusion.refs_0_), channel_id=1, source_target_pairs={{0,4},{1,5},{2,6},{3,7},{4,0},{5,1},{6,2},{7,3},{8,12},{9,13},{10,... | collective-permute-start | bytes 393224 | tf_op jit(solution)/shard_map/ppermute | solution.py:350
  23.3 3.4 %collective-permute-start.9 = (bf16[128,512]{1,0:T(8,128)(2,1)S(1)}, bf16[128,512]{1,0:T(8,128)(2,1)S(1)}, u32[]{:S(2)}, u32[]{:S(2)}) collective-permute-start(bf16[128,512]{1,0:T(8,128)(2,1)S(1)} %pad_maximum_fusion.refs_0_), channel_id=1, source_target_pairs={{0,6},{1,7},{2,0},{3,1},{4,2},{5,3},{6,4},{7,5},{8,14},{9,15},{10,... | collective-permute-start | bytes 393224 | tf_op jit(solution)/shard_map/ppermute | solution.py:350
  26.8 1.5 %collective-permute-start.15 = (bf16[512,256]{1,0:T(8,128)(2,1)S(1)}, bf16[512,256]{1,0:T(8,128)(2,1)S(1)}, u32[]{:S(2)}, u32[]{:S(2)}) collective-permute-start(bf16[512,256]{1,0:T(8,128)(2,1)S(1)} %broadcast_select_fusion), channel_id=1, source_target_pairs={{0,16},{8,24},{16,0},{24,8},{1,17},{9,25},{17,1},{25,9},{2,18},{10... | collective-permute-start | bytes 786440 | tf_op jit(solution)/shard_map/ppermute | solution.py:359
  28.3 1.2 %copy-done.2 = bf16[1,128,4096]{2,1,0:T(8,128)(2,1)S(1)} copy-done((bf16[1,128,4096]{2,1,0:T(8,128)(2,1)S(1)}, bf16[1,128,4096]{2,1,0:T(8,128)(2,1)}, u32[]{:S(2)}) %copy-start.2) | copy-done | bytes 1048600
  29.5 3.6 %attention_backward.2 = (bf16[128,2048]{1,0:T(8,128)(2,1)S(1)}, bf16[1024,512]{1,0:T(8,128)(2,1)S(1)}) custom-call(s32[160]{0:T(256)S(1)} %reshape.102.table_ref, bf16[128,4096]{1,0:T(8,128)(2,1)S(1)} %bitcast.45, bf16[128,4096]{1,0:T(8,128)(2,1)S(1)} %bitcast.47, bf16[128,512]{1,0:T(8,128)(2,1)S(1)} %pad_maximum_fusion.1.refs_0_, ...), custom_call_target="tpu_custom_call" | custom-call | flops 10066329600 | bytes 4194304 | tf_op jit(solution)/shard_map/attention_backward/pallas_call | solution.py:154
  35.4 3.8 %attention_backward.3 = (bf16[128,2048]{1,0:T(8,128)(2,1)S(1)}, bf16[1024,512]{1,0:T(8,128)(2,1)S(1)}) custom-call(s32[160]{0:T(256)S(1)} %reshape.102.table_ref, bf16[128,4096]{1,0:T(8,128)(2,1)S(1)} %bitcast.46, bf16[128,4096]{1,0:T(8,128)(2,1)S(1)} %bitcast.48, bf16[128,512]{1,0:T(8,128)(2,1)S(1)} %pad_maximum_fusion.refs_0_, ...), custom_call_target="tpu_custom_call" | custom-call | flops 10066329600 | bytes 4194304 | tf_op jit(solution)/shard_map/attention_backward/pallas_call | solution.py:154
  39.7 1.3 %collective-permute-start.17 = (bf16[512,256]{1,0:T(8,128)(2,1)S(1)}, bf16[512,256]{1,0:T(8,128)(2,1)S(1)}, u32[]{:S(2)}, u32[]{:S(2)}) collective-permute-start(bf16[512,256]{1,0:T(8,128)(2,1)S(1)} %project.3), channel_id=1, source_target_pairs={{0,1},{1,0},{2,3},{3,2},{4,5},{5,4},{6,7},{7,6},{8,9},{9,8},{10,11... | collective-permute-start | bytes 786440 | tf_op jit(solution)/shard_map/ppermute | solution.py:346
  42.2 2.0 %collective-permute-start.18 = (bf16[128,256]{1,0:T(8,128)(2,1)S(1)}, bf16[128,256]{1,0:T(8,128)(2,1)S(1)}, u32[]{:S(2)}, u32[]{:S(2)}) collective-permute-start(bf16[128,256]{1,0:T(8,128)(2,1)S(1)} %get-tuple-element.39), channel_id=1, source_target_pairs={{0,4},{1,5},{2,6},{3,7},{4,0},{5,1},{6,2},{7,3},{8,12},{9,13},{10,... | collective-permute-start | bytes 196616 | tf_op jit(solution)/shard_map/ppermute | solution.py:350
  44.2 1.7 %collective-permute-start.19 = (bf16[128,256]{1,0:T(8,128)(2,1)S(1)}, bf16[128,256]{1,0:T(8,128)(2,1)S(1)}, u32[]{:S(2)}, u32[]{:S(2)}) collective-permute-start(bf16[128,256]{1,0:T(8,128)(2,1)S(1)} %get-tuple-element.40), channel_id=1, source_target_pairs={{0,6},{1,7},{2,0},{3,1},{4,2},{5,3},{6,4},{7,5},{8,14},{9,15},{10,... | collective-permute-start | bytes 196616 | tf_op jit(solution)/shard_map/ppermute | solution.py:350
  46.4 2.8 %collective-permute-done.18 = bf16[128,256]{1,0:T(8,128)(2,1)S(1)} collective-permute-done((bf16[128,256]{1,0:T(8,128)(2,1)S(1)}, bf16[128,256]{1,0:T(8,128)(2,1)S(1)}, u32[]{:S(2)}, u32[]{:S(2)}) %collective-permute-start.18) | collective-permute-done | bytes 65568 | tf_op jit(solution)/shard_map/ppermute | solution.py:350
  49.2 2.8 %collective-permute-done.20 = bf16[128,256]{1,0:T(8,128)(2,1)S(1)} collective-permute-done((bf16[128,256]{1,0:T(8,128)(2,1)S(1)}, bf16[128,256]{1,0:T(8,128)(2,1)S(1)}, u32[]{:S(2)}, u32[]{:S(2)}) %collective-permute-start.20) | collective-permute-done | bytes 65568 | tf_op jit(solution)/shard_map/ppermute | solution.py:350
  52.0 2.0 %collective-permute-start.21 = (bf16[128,256]{1,0:T(8,128)(2,1)S(1)}, bf16[128,256]{1,0:T(8,128)(2,1)S(1)}, u32[]{:S(2)}, u32[]{:S(2)}) collective-permute-start(bf16[128,256]{1,0:T(8,128)(2,1)S(1)} %add_convert_fusion.1.refs_0_), channel_id=1, source_target_pairs={{0,8},{8,0},{16,24},{24,16},{1,9},{9,1},{17,25},{25,17},{2,10},{10... | collective-permute-start | bytes 196616 | tf_op jit(solution)/shard_map/ppermute | solution.py:359
  54.0 1.0 %collective-permute-start.22 = (bf16[128,256]{1,0:T(8,128)(2,1)S(1)}, bf16[128,256]{1,0:T(8,128)(2,1)S(1)}, u32[]{:S(2)}, u32[]{:S(2)}) collective-permute-start(bf16[128,256]{1,0:T(8,128)(2,1)S(1)} %add_convert_fusion.1.refs_0_), channel_id=1, source_target_pairs={{0,16},{8,24},{16,0},{24,8},{1,17},{9,25},{17,1},{25,9},{2,18},{10... | collective-permute-start | bytes 196616 | tf_op jit(solution)/shard_map/ppermute | solution.py:359
  56.3 2.3 %collective-permute-done.22.refs_2_ = bf16[128,256]{1,0:T(8,128)(2,1)S(1)} collective-permute-done((bf16[128,256]{1,0:T(8,128)(2,1)S(1)}, bf16[128,256]{1,0:T(8,128)(2,1)S(1)}, u32[]{:S(2)}, u32[]{:S(2)}) %collective-permute-start.22) | collective-permute-done | bytes 65568 | tf_op jit(solution)/shard_map/ppermute | solution.py:359
  58.6 1.7 %collective-permute-done.23.refs_3_ = bf16[128,256]{1,0:T(8,128)(2,1)S(1)} collective-permute-done((bf16[128,256]{1,0:T(8,128)(2,1)S(1)}, bf16[128,256]{1,0:T(8,128)(2,1)S(1)}, u32[]{:S(2)}, u32[]{:S(2)}) %collective-permute-start.23) | collective-permute-done | bytes 65568 | tf_op jit(solution)/shard_map/ppermute | solution.py:359
  60.8 1.5 %collective-permute-done.24.came_ref = bf16[512,256]{1,0:T(8,128)(2,1)S(1)} collective-permute-done((bf16[512,256]{1,0:T(8,128)(2,1)S(1)}, bf16[512,256]{1,0:T(8,128)(2,1)S(1)}, u32[]{:S(2)}, u32[]{:S(2)}) %collective-permute-start.24) | collective-permute-done | bytes 262176 | tf_op jit(solution)/shard_map/ppermute | solution.py:346
  62.4 0.9 %collective-permute-start.25 = (bf16[128,256]{1,0:T(8,128)(2,1)S(1)}, bf16[128,256]{1,0:T(8,128)(2,1)S(1)}, u32[]{:S(2)}, u32[]{:S(2)}) collective-permute-start(bf16[128,256]{1,0:T(8,128)(2,1)S(1)} %get-tuple-element.45), channel_id=1, source_target_pairs={{0,4},{1,5},{2,6},{3,7},{4,0},{5,1},{6,2},{7,3},{8,12},{9,13},{10,... | collective-permute-start | bytes 196616 | tf_op jit(solution)/shard_map/ppermute | solution.py:350
  63.3 1.5 %collective-permute-start.26 = (bf16[128,256]{1,0:T(8,128)(2,1)S(1)}, bf16[128,256]{1,0:T(8,128)(2,1)S(1)}, u32[]{:S(2)}, u32[]{:S(2)}) collective-permute-start(bf16[128,256]{1,0:T(8,128)(2,1)S(1)} %get-tuple-element.46), channel_id=1, source_target_pairs={{0,2},{1,3},{2,4},{3,5},{4,6},{5,7},{6,0},{7,1},{8,10},{9,11},{10,... | collective-permute-start | bytes 196616 | tf_op jit(solution)/shard_map/ppermute | solution.py:350
  64.8 2.4 %collective-permute-start.27 = (bf16[128,256]{1,0:T(8,128)(2,1)S(1)}, bf16[128,256]{1,0:T(8,128)(2,1)S(1)}, u32[]{:S(2)}, u32[]{:S(2)}) collective-permute-start(bf16[128,256]{1,0:T(8,128)(2,1)S(1)} %get-tuple-element.47), channel_id=1, source_target_pairs={{0,6},{1,7},{2,0},{3,1},{4,2},{5,3},{6,4},{7,5},{8,14},{9,15},{10,... | collective-permute-start | bytes 196616 | tf_op jit(solution)/shard_map/ppermute | solution.py:350
  67.1 2.7 %collective-permute-done.25 = bf16[128,256]{1,0:T(8,128)(2,1)S(1)} collective-permute-done((bf16[128,256]{1,0:T(8,128)(2,1)S(1)}, bf16[128,256]{1,0:T(8,128)(2,1)S(1)}, u32[]{:S(2)}, u32[]{:S(2)}) %collective-permute-start.25) | collective-permute-done | bytes 65568 | tf_op jit(solution)/shard_map/ppermute | solution.py:350
  69.8 1.2 %collective-permute-done.27 = bf16[128,256]{1,0:T(8,128)(2,1)S(1)} collective-permute-done((bf16[128,256]{1,0:T(8,128)(2,1)S(1)}, bf16[128,256]{1,0:T(8,128)(2,1)S(1)}, u32[]{:S(2)}, u32[]{:S(2)}) %collective-permute-start.27) | collective-permute-done | bytes 65568 | tf_op jit(solution)/shard_map/ppermute | solution.py:350
  72.4 2.1 %collective-permute-start.30 = (bf16[128,256]{1,0:T(8,128)(2,1)S(1)}, bf16[128,256]{1,0:T(8,128)(2,1)S(1)}, u32[]{:S(2)}, u32[]{:S(2)}) collective-permute-start(bf16[128,256]{1,0:T(8,128)(2,1)S(1)} %add_convert_fusion.refs_0_), channel_id=1, source_target_pairs={{0,24},{8,16},{16,8},{24,0},{1,25},{9,17},{17,9},{25,1},{2,26},{10... | collective-permute-start | bytes 196616 | tf_op jit(solution)/shard_map/ppermute | solution.py:359
  74.5 1.0 %maximum_bitcast_fusion = bf16[1,128,4096]{2,1,0:T(8,128)(2,1)} fusion(bf16[128,2048]{1,0:T(8,128)(2,1)S(1)} %get-tuple-element.35, bf16[128,2048]{1,0:T(8,128)(2,1)S(1)} %get-tuple-element.29), kind=kLoop, calls=%fused_computation | loop fusion | flops 2097152 | bytes 2097152 | tf_op jit(solution)/shard_map/broadcast_in_dim | solution.py:424
  76.2 1.4 %collective-permute-done.30.refs_3_ = bf16[128,256]{1,0:T(8,128)(2,1)S(1)} collective-permute-done((bf16[128,256]{1,0:T(8,128)(2,1)S(1)}, bf16[128,256]{1,0:T(8,128)(2,1)S(1)}, u32[]{:S(2)}, u32[]{:S(2)}) %collective-permute-start.30) | collective-permute-done | bytes 65568 | tf_op jit(solution)/shard_map/ppermute | solution.py:359
  (78 shorter events, 14.4 us)
Async XLA Ops:
  1.7 17.4 %collective-permute-start = (bf16[128,512]{1,0:T(8,128)(2,1)S(1)}, bf16[128,512]{1,0:T(8,128)(2,1)S(1)}, u32[]{:S(2)}, u32[]{:S(2)}) collective-permute-start(bf16[128,512]{1,0:T(8,128)(2,1)S(1)} %pad_maximum_fusion.1.refs_0_), channel_id=1, source_target_pairs={{0,2},{1,3},{2,4},{3,5},{4,6},{5,7},{6,0},{7,1},{8,10},{9,11},{10,... | collective-permute-start | bytes 393224 | tf_op jit(solution)/shard_map/ppermute | solution.py:350
  4.8 14.4 %collective-permute-start.1 = (bf16[128,512]{1,0:T(8,128)(2,1)S(1)}, bf16[128,512]{1,0:T(8,128)(2,1)S(1)}, u32[]{:S(2)}, u32[]{:S(2)}) collective-permute-start(bf16[128,512]{1,0:T(8,128)(2,1)S(1)} %pad_maximum_fusion.1.refs_0_), channel_id=1, source_target_pairs={{0,4},{1,5},{2,6},{3,7},{4,0},{5,1},{6,2},{7,3},{8,12},{9,13},{10,... | collective-permute-start | bytes 393224 | tf_op jit(solution)/shard_map/ppermute | solution.py:350
  7.4 11.8 %collective-permute-start.2 = (bf16[128,512]{1,0:T(8,128)(2,1)S(1)}, bf16[128,512]{1,0:T(8,128)(2,1)S(1)}, u32[]{:S(2)}, u32[]{:S(2)}) collective-permute-start(bf16[128,512]{1,0:T(8,128)(2,1)S(1)} %pad_maximum_fusion.1.refs_0_), channel_id=1, source_target_pairs={{0,6},{1,7},{2,0},{3,1},{4,2},{5,3},{6,4},{7,5},{8,14},{9,15},{10,... | collective-permute-start | bytes 393224 | tf_op jit(solution)/shard_map/ppermute | solution.py:350
  8.8 24.4 %collective-permute-start.7 = (bf16[128,512]{1,0:T(8,128)(2,1)S(1)}, bf16[128,512]{1,0:T(8,128)(2,1)S(1)}, u32[]{:S(2)}, u32[]{:S(2)}) collective-permute-start(bf16[128,512]{1,0:T(8,128)(2,1)S(1)} %pad_maximum_fusion.refs_0_), channel_id=1, source_target_pairs={{0,2},{1,3},{2,4},{3,5},{4,6},{5,7},{6,0},{7,1},{8,10},{9,11},{10,... | collective-permute-start | bytes 393224 | tf_op jit(solution)/shard_map/ppermute | solution.py:350
  10.2 9.6 %collective-permute-start.14 = (bf16[512,256]{1,0:T(8,128)(2,1)}, bf16[512,256]{1,0:T(8,128)(2,1)}, u32[]{:S(2)}, u32[]{:S(2)}) collective-permute-start(bf16[512,256]{1,0:T(8,128)(2,1)} %dynamic-slice_bitcast_fusion), channel_id=1, source_target_pairs={{0,8},{8,0},{16,24},{24,16},{1,9},{9,1},{17,25},{25,17},{2,10},{10... | collective-permute-start | bytes 786440 | tf_op jit(solution)/shard_map/ppermute | solution.py:359
  13.0 42.6 %all-to-all-start = ((bf16[4,128,1024]{2,1,0:T(8,128)(2,1)}), bf16[4,128,1024]{2,1,0:T(8,128)(2,1)S(1)}, u32[]{:S(2)}, u32[]{:S(2)}) async-start(bf16[4,128,1024]{2,1,0:T(8,128)(2,1)} %split_input.1), calls=%async_computation | async-start | bytes 2097152 | tf_op jit(solution)/shard_map/all_to_all | solution.py:394
  19.2 2.2 %collective-permute-start.3 = (bf16[128,512]{1,0:T(8,128)(2,1)S(1)}, bf16[128,512]{1,0:T(8,128)(2,1)S(1)}, u32[]{:S(2)}, u32[]{:S(2)}) collective-permute-start(bf16[128,512]{1,0:T(8,128)(2,1)S(1)} %pad_maximum_fusion.1.refs_0_), channel_id=1, source_target_pairs={{0,1},{1,0},{2,3},{3,2},{4,5},{5,4},{6,7},{7,6},{8,9},{9,8},{10,11... | collective-permute-start | bytes 393224 | tf_op jit(solution)/shard_map/ppermute | solution.py:346
  19.3 4.0 %collective-permute-start.4 = (bf16[128,512]{1,0:T(8,128)(2,1)S(1)}, bf16[128,512]{1,0:T(8,128)(2,1)S(1)}, u32[]{:S(2)}, u32[]{:S(2)}) collective-permute-start(bf16[128,512]{1,0:T(8,128)(2,1)S(1)} %collective-permute-done.refs_1_), channel_id=1, source_target_pairs={{0,1},{1,0},{2,3},{3,2},{4,5},{5,4},{6,7},{7,6},{8,9},{9,8},{10,11... | collective-permute-start | bytes 393224 | tf_op jit(solution)/shard_map/ppermute | solution.py:346
  19.8 3.6 %collective-permute-start.5 = (bf16[128,512]{1,0:T(8,128)(2,1)S(1)}, bf16[128,512]{1,0:T(8,128)(2,1)S(1)}, u32[]{:S(2)}, u32[]{:S(2)}) collective-permute-start(bf16[128,512]{1,0:T(8,128)(2,1)S(1)} %collective-permute-done.1.refs_2_), channel_id=1, source_target_pairs={{0,1},{1,0},{2,3},{3,2},{4,5},{5,4},{6,7},{7,6},{8,9},{9,8},{10,11... | collective-permute-start | bytes 393224 | tf_op jit(solution)/shard_map/ppermute | solution.py:346
  19.8 6.9 %collective-permute-start.6 = (bf16[128,512]{1,0:T(8,128)(2,1)S(1)}, bf16[128,512]{1,0:T(8,128)(2,1)S(1)}, u32[]{:S(2)}, u32[]{:S(2)}) collective-permute-start(bf16[128,512]{1,0:T(8,128)(2,1)S(1)} %collective-permute-done.2.refs_3_), channel_id=1, source_target_pairs={{0,1},{1,0},{2,3},{3,2},{4,5},{5,4},{6,7},{7,6},{8,9},{9,8},{10,11... | collective-permute-start | bytes 393224 | tf_op jit(solution)/shard_map/ppermute | solution.py:346
  21.4 11.8 %collective-permute-start.8 = (bf16[128,512]{1,0:T(8,128)(2,1)S(1)}, bf16[128,512]{1,0:T(8,128)(2,1)S(1)}, u32[]{:S(2)}, u32[]{:S(2)}) collective-permute-start(bf16[128,512]{1,0:T(8,128)(2,1)S(1)} %pad_maximum_fusion.refs_0_), channel_id=1, source_target_pairs={{0,4},{1,5},{2,6},{3,7},{4,0},{5,1},{6,2},{7,3},{8,12},{9,13},{10,... | collective-permute-start | bytes 393224 | tf_op jit(solution)/shard_map/ppermute | solution.py:350
  23.3 12.1 %collective-permute-start.10 = (bf16[128,512]{1,0:T(8,128)(2,1)S(1)}, bf16[128,512]{1,0:T(8,128)(2,1)S(1)}, u32[]{:S(2)}, u32[]{:S(2)}) collective-permute-start(bf16[128,512]{1,0:T(8,128)(2,1)S(1)} %pad_maximum_fusion.refs_0_), channel_id=1, source_target_pairs={{0,1},{1,0},{2,3},{3,2},{4,5},{5,4},{6,7},{7,6},{8,9},{9,8},{10,11... | collective-permute-start | bytes 393224 | tf_op jit(solution)/shard_map/ppermute | solution.py:346
  23.3 9.8 %collective-permute-start.9 = (bf16[128,512]{1,0:T(8,128)(2,1)S(1)}, bf16[128,512]{1,0:T(8,128)(2,1)S(1)}, u32[]{:S(2)}, u32[]{:S(2)}) collective-permute-start(bf16[128,512]{1,0:T(8,128)(2,1)S(1)} %pad_maximum_fusion.refs_0_), channel_id=1, source_target_pairs={{0,6},{1,7},{2,0},{3,1},{4,2},{5,3},{6,4},{7,5},{8,14},{9,15},{10,... | collective-permute-start | bytes 393224 | tf_op jit(solution)/shard_map/ppermute | solution.py:350
  26.8 8.4 %collective-permute-start.15 = (bf16[512,256]{1,0:T(8,128)(2,1)S(1)}, bf16[512,256]{1,0:T(8,128)(2,1)S(1)}, u32[]{:S(2)}, u32[]{:S(2)}) collective-permute-start(bf16[512,256]{1,0:T(8,128)(2,1)S(1)} %broadcast_select_fusion), channel_id=1, source_target_pairs={{0,16},{8,24},{16,0},{24,8},{1,17},{9,25},{17,1},{25,9},{2,18},{10... | collective-permute-start | bytes 786440 | tf_op jit(solution)/shard_map/ppermute | solution.py:359
  33.2 2.2 %collective-permute-start.11 = (bf16[128,512]{1,0:T(8,128)(2,1)S(1)}, bf16[128,512]{1,0:T(8,128)(2,1)S(1)}, u32[]{:S(2)}, u32[]{:S(2)}) collective-permute-start(bf16[128,512]{1,0:T(8,128)(2,1)S(1)} %collective-permute-done.7.refs_1_), channel_id=1, source_target_pairs={{0,1},{1,0},{2,3},{3,2},{4,5},{5,4},{6,7},{7,6},{8,9},{9,8},{10,11... | collective-permute-start | bytes 393224 | tf_op jit(solution)/shard_map/ppermute | solution.py:346
  33.8 1.6 %collective-permute-start.12 = (bf16[128,512]{1,0:T(8,128)(2,1)S(1)}, bf16[128,512]{1,0:T(8,128)(2,1)S(1)}, u32[]{:S(2)}, u32[]{:S(2)}) collective-permute-start(bf16[128,512]{1,0:T(8,128)(2,1)S(1)} %collective-permute-done.8.refs_2_), channel_id=1, source_target_pairs={{0,1},{1,0},{2,3},{3,2},{4,5},{5,4},{6,7},{7,6},{8,9},{9,8},{10,11... | collective-permute-start | bytes 393224 | tf_op jit(solution)/shard_map/ppermute | solution.py:346
  33.9 1.5 %collective-permute-start.13 = (bf16[128,512]{1,0:T(8,128)(2,1)S(1)}, bf16[128,512]{1,0:T(8,128)(2,1)S(1)}, u32[]{:S(2)}, u32[]{:S(2)}) collective-permute-start(bf16[128,512]{1,0:T(8,128)(2,1)S(1)} %collective-permute-done.9.refs_3_), channel_id=1, source_target_pairs={{0,1},{1,0},{2,3},{3,2},{4,5},{5,4},{6,7},{7,6},{8,9},{9,8},{10,11... | collective-permute-start | bytes 393224 | tf_op jit(solution)/shard_map/ppermute | solution.py:346
  35.3 3.9 %collective-permute-start.16 = (bf16[512,256]{1,0:T(8,128)(2,1)S(1)}, bf16[512,256]{1,0:T(8,128)(2,1)S(1)}, u32[]{:S(2)}, u32[]{:S(2)}) collective-permute-start(bf16[512,256]{1,0:T(8,128)(2,1)S(1)} %broadcast_select_fusion.1.mine_ref), channel_id=1, source_target_pairs={{0,1},{1,0},{2,3},{3,2},{4,5},{5,4},{6,7},{7,6},{8,9},{9,8},{10,11... | collective-permute-start | bytes 786440 | tf_op jit(solution)/shard_map/ppermute | solution.py:346
  39.7 2.4 %collective-permute-start.17 = (bf16[512,256]{1,0:T(8,128)(2,1)S(1)}, bf16[512,256]{1,0:T(8,128)(2,1)S(1)}, u32[]{:S(2)}, u32[]{:S(2)}) collective-permute-start(bf16[512,256]{1,0:T(8,128)(2,1)S(1)} %project.3), channel_id=1, source_target_pairs={{0,1},{1,0},{2,3},{3,2},{4,5},{5,4},{6,7},{7,6},{8,9},{9,8},{10,11... | collective-permute-start | bytes 786440 | tf_op jit(solution)/shard_map/ppermute | solution.py:346
  42.2 7.0 %collective-permute-start.18 = (bf16[128,256]{1,0:T(8,128)(2,1)S(1)}, bf16[128,256]{1,0:T(8,128)(2,1)S(1)}, u32[]{:S(2)}, u32[]{:S(2)}) collective-permute-start(bf16[128,256]{1,0:T(8,128)(2,1)S(1)} %get-tuple-element.39), channel_id=1, source_target_pairs={{0,4},{1,5},{2,6},{3,7},{4,0},{5,1},{6,2},{7,3},{8,12},{9,13},{10,... | collective-permute-start | bytes 196616 | tf_op jit(solution)/shard_map/ppermute | solution.py:350
  44.2 5.0 %collective-permute-start.19 = (bf16[128,256]{1,0:T(8,128)(2,1)S(1)}, bf16[128,256]{1,0:T(8,128)(2,1)S(1)}, u32[]{:S(2)}, u32[]{:S(2)}) collective-permute-start(bf16[128,256]{1,0:T(8,128)(2,1)S(1)} %get-tuple-element.40), channel_id=1, source_target_pairs={{0,6},{1,7},{2,0},{3,1},{4,2},{5,3},{6,4},{7,5},{8,14},{9,15},{10,... | collective-permute-start | bytes 196616 | tf_op jit(solution)/shard_map/ppermute | solution.py:350
  45.9 6.1 %collective-permute-start.20 = (bf16[128,256]{1,0:T(8,128)(2,1)S(1)}, bf16[128,256]{1,0:T(8,128)(2,1)S(1)}, u32[]{:S(2)}, u32[]{:S(2)}) collective-permute-start(bf16[128,256]{1,0:T(8,128)(2,1)S(1)} %get-tuple-element.41), channel_id=1, source_target_pairs={{0,2},{1,3},{2,4},{3,5},{4,6},{5,7},{6,0},{7,1},{8,10},{9,11},{10,... | collective-permute-start | bytes 196616 | tf_op jit(solution)/shard_map/ppermute | solution.py:350
  52.0 4.3 %collective-permute-start.21 = (bf16[128,256]{1,0:T(8,128)(2,1)S(1)}, bf16[128,256]{1,0:T(8,128)(2,1)S(1)}, u32[]{:S(2)}, u32[]{:S(2)}) collective-permute-start(bf16[128,256]{1,0:T(8,128)(2,1)S(1)} %add_convert_fusion.1.refs_0_), channel_id=1, source_target_pairs={{0,8},{8,0},{16,24},{24,16},{1,9},{9,1},{17,25},{25,17},{2,10},{10... | collective-permute-start | bytes 196616 | tf_op jit(solution)/shard_map/ppermute | solution.py:359
  54.0 4.6 %collective-permute-start.22 = (bf16[128,256]{1,0:T(8,128)(2,1)S(1)}, bf16[128,256]{1,0:T(8,128)(2,1)S(1)}, u32[]{:S(2)}, u32[]{:S(2)}) collective-permute-start(bf16[128,256]{1,0:T(8,128)(2,1)S(1)} %add_convert_fusion.1.refs_0_), channel_id=1, source_target_pairs={{0,16},{8,24},{16,0},{24,8},{1,17},{9,25},{17,1},{25,9},{2,18},{10... | collective-permute-start | bytes 196616 | tf_op jit(solution)/shard_map/ppermute | solution.py:359
  55.1 5.2 %collective-permute-start.23 = (bf16[128,256]{1,0:T(8,128)(2,1)S(1)}, bf16[128,256]{1,0:T(8,128)(2,1)S(1)}, u32[]{:S(2)}, u32[]{:S(2)}) collective-permute-start(bf16[128,256]{1,0:T(8,128)(2,1)S(1)} %add_convert_fusion.1.refs_0_), channel_id=1, source_target_pairs={{0,24},{8,16},{16,8},{24,0},{1,25},{9,17},{17,9},{25,1},{2,26},{10... | collective-permute-start | bytes 196616 | tf_op jit(solution)/shard_map/ppermute | solution.py:359
  60.7 1.6 %collective-permute-start.24 = (bf16[512,256]{1,0:T(8,128)(2,1)S(1)}, bf16[512,256]{1,0:T(8,128)(2,1)S(1)}, u32[]{:S(2)}, u32[]{:S(2)}) collective-permute-start(bf16[512,256]{1,0:T(8,128)(2,1)S(1)} %get-tuple-element.43), channel_id=1, source_target_pairs={{0,1},{1,0},{2,3},{3,2},{4,5},{5,4},{6,7},{7,6},{8,9},{9,8},{10,11... | collective-permute-start | bytes 786440 | tf_op jit(solution)/shard_map/ppermute | solution.py:346
  62.4 7.4 %collective-permute-start.25 = (bf16[128,256]{1,0:T(8,128)(2,1)S(1)}, bf16[128,256]{1,0:T(8,128)(2,1)S(1)}, u32[]{:S(2)}, u32[]{:S(2)}) collective-permute-start(bf16[128,256]{1,0:T(8,128)(2,1)S(1)} %get-tuple-element.45), channel_id=1, source_target_pairs={{0,4},{1,5},{2,6},{3,7},{4,0},{5,1},{6,2},{7,3},{8,12},{9,13},{10,... | collective-permute-start | bytes 196616 | tf_op jit(solution)/shard_map/ppermute | solution.py:350
  63.3 6.5 %collective-permute-start.26 = (bf16[128,256]{1,0:T(8,128)(2,1)S(1)}, bf16[128,256]{1,0:T(8,128)(2,1)S(1)}, u32[]{:S(2)}, u32[]{:S(2)}) collective-permute-start(bf16[128,256]{1,0:T(8,128)(2,1)S(1)} %get-tuple-element.46), channel_id=1, source_target_pairs={{0,2},{1,3},{2,4},{3,5},{4,6},{5,7},{6,0},{7,1},{8,10},{9,11},{10,... | collective-permute-start | bytes 196616 | tf_op jit(solution)/shard_map/ppermute | solution.py:350
  64.8 6.2 %collective-permute-start.27 = (bf16[128,256]{1,0:T(8,128)(2,1)S(1)}, bf16[128,256]{1,0:T(8,128)(2,1)S(1)}, u32[]{:S(2)}, u32[]{:S(2)}) collective-permute-start(bf16[128,256]{1,0:T(8,128)(2,1)S(1)} %get-tuple-element.47), channel_id=1, source_target_pairs={{0,6},{1,7},{2,0},{3,1},{4,2},{5,3},{6,4},{7,5},{8,14},{9,15},{10,... | collective-permute-start | bytes 196616 | tf_op jit(solution)/shard_map/ppermute | solution.py:350
  71.0 4.6 %collective-permute-start.28 = (bf16[128,256]{1,0:T(8,128)(2,1)S(1)}, bf16[128,256]{1,0:T(8,128)(2,1)S(1)}, u32[]{:S(2)}, u32[]{:S(2)}) collective-permute-start(bf16[128,256]{1,0:T(8,128)(2,1)S(1)} %add_convert_fusion.refs_0_), channel_id=1, source_target_pairs={{0,8},{8,0},{16,24},{24,16},{1,9},{9,1},{17,25},{25,17},{2,10},{10... | collective-permute-start | bytes 196616 | tf_op jit(solution)/shard_map/ppermute | solution.py:359
  71.6 4.6 %collective-permute-start.29 = (bf16[128,256]{1,0:T(8,128)(2,1)S(1)}, bf16[128,256]{1,0:T(8,128)(2,1)S(1)}, u32[]{:S(2)}, u32[]{:S(2)}) collective-permute-start(bf16[128,256]{1,0:T(8,128)(2,1)S(1)} %add_convert_fusion.refs_0_), channel_id=1, source_target_pairs={{0,16},{8,24},{16,0},{24,8},{1,17},{9,25},{17,1},{25,9},{2,18},{10... | collective-permute-start | bytes 196616 | tf_op jit(solution)/shard_map/ppermute | solution.py:359
  72.4 5.2 %collective-permute-start.30 = (bf16[128,256]{1,0:T(8,128)(2,1)S(1)}, bf16[128,256]{1,0:T(8,128)(2,1)S(1)}, u32[]{:S(2)}, u32[]{:S(2)}) collective-permute-start(bf16[128,256]{1,0:T(8,128)(2,1)S(1)} %add_convert_fusion.refs_0_), channel_id=1, source_target_pairs={{0,24},{8,16},{16,8},{24,0},{1,25},{9,17},{17,9},{25,1},{2,26},{10... | collective-permute-start | bytes 196616 | tf_op jit(solution)/shard_map/ppermute | solution.py:359
  (5 other events, 42.1 us)

commit v7 on v6

--- a/solution.py
+++ b/solution.py
@@ -413,14 +413,16 @@
     for step in order:
         total = total + down(sends[step - 1], step).astype(f32)
     projected = total.astype(bf16)
-    p_parts = [projected] + [across(projected, step) for step in range(1, dp_count)]
+    moved = {step: across(projected, step) for step in reversed(range(1, dp_count))}
+    p_parts = [projected] + [moved[step] for step in range(1, dp_count)]
     kept, sent = outer(x_all, p_parts)
     own, *sends = deal(kept, pair(sent), chips)
     total = own
     for step in order:
         total = total + around(sends[step - 1], step).astype(f32)
     rows = total.astype(bf16)
-    lowrank_grad = lay([rows] + [across(rows, step) for step in range(1, dp_count)])
+    moved = {step: across(rows, step) for step in reversed(range(1, dp_count))}
+    lowrank_grad = lay([rows] + [moved[step] for step in range(1, dp_count)])
     return (grad_query[None], lowrank_grad)
 
 

time: 78.9 us -> 79.1 us (level)
  transfers between devices with their start and end apart: 32 -> 32, of which waited for: 12 -> 14; matrix products, arithmetic and copies ran while one was open for 7% -> 7% of each run, Pallas kernels for 12% -> 12%
where the time goes in v7:
time: 79.1 us; the launch traced here: 78.7 us
  starting transfers between devices  39.9 us (50%)
  waiting for transfers between devices  18.9 us (24%)
  Pallas kernels  11.1 us (14%)
  other arithmetic  4.25 us (5%)
  local copies, waits for them, and re-layouts  3.64 us (5%)
  between operations  0.89 us (1%)
    ppermute x12, starting transfers between devices, around(): return lax.ppermute(x, 'seq', moves)  22.5 us
    ppermute x8, starting transfers between devices, across(): return lax.ppermute(x, 'dp', [(i, i ^ step) for i in range(dp_count)])  10.1 us
    ppermute x12, waiting for transfers between devices, around(): return lax.ppermute(x, 'seq', moves)  9.26 us
    pallas_call x2, Pallas kernels, attention(): pl.pallas_call(body, in_specs=[pl.BlockSpec(memory_space=pltpu.SMEM)] + [...  7.42 us
    ppermute x8, waiting for transfers between devices, across(): return lax.ppermute(x, 'dp', [(i, i ^ step) for i in range(dp_count)])  7.4 us
    ppermute x11, starting transfers between devices, pair(): return lax.ppermute(x, 'seq', [(i, i ^ 1) for i in range(seq_count)])  3.66 us
    all_to_all x1, starting transfers between devices, local(): x_all = lax.all_to_all(x_pieces, 'dp', 0, 0, tiled=True)  3.65 us
    ppermute x11, waiting for transfers between devices, pair(): return lax.ppermute(x, 'seq', [(i, i ^ 1) for i in range(seq_count)])  2.23 us
  transfers between devices with their start and end apart: 32, of which 14 were waited for; matrix products, arithmetic and copies ran while one was open for 7% of the time, Pallas kernels for 12%

profile of v7, /device:TPU:0, one launch (start us, length us, event | category | flops | bytes accessed | tf_op | source)
XLA Modules:
  0.0 78.7 jit_solution(6485965084708365663)
XLA Ops:
  0.7 1.1 %fusion.9 = (bf16[128,256]{1,0:T(8,128)(2,1)S(1)}, bf16[128,256]{1,0:T(8,128)(2,1)S(1)}, bf16[128,256]{1,0:T(8,128)(2,1)S(1)}, bf16[128,256]{1,0:T(8,128)(2,1)S(1)}) fusion(bf16[128,512]{1,0:T(8,128)(2,1)} %bitcast.49, bf16[128,512]{1,0:T(8,128)(2,1)} %bitcast.50), kind=kLoop, calls=%fused_computation.44 | loop fusion | bytes 524288 | tf_op jit(solution)/shard_map/slice | solution.py:366
  1.7 3.1 %collective-permute-start = (bf16[128,512]{1,0:T(8,128)(2,1)S(1)}, bf16[128,512]{1,0:T(8,128)(2,1)S(1)}, u32[]{:S(2)}, u32[]{:S(2)}) collective-permute-start(bf16[128,512]{1,0:T(8,128)(2,1)S(1)} %pad_maximum_fusion.1.refs_0_), channel_id=1, source_target_pairs={{0,2},{1,3},{2,4},{3,5},{4,6},{5,7},{6,0},{7,1},{8,10},{9,11},{10,... | collective-permute-start | bytes 393224 | tf_op jit(solution)/shard_map/ppermute | solution.py:350
  4.8 2.6 %collective-permute-start.1 = (bf16[128,512]{1,0:T(8,128)(2,1)S(1)}, bf16[128,512]{1,0:T(8,128)(2,1)S(1)}, u32[]{:S(2)}, u32[]{:S(2)}) collective-permute-start(bf16[128,512]{1,0:T(8,128)(2,1)S(1)} %pad_maximum_fusion.1.refs_0_), channel_id=1, source_target_pairs={{0,4},{1,5},{2,6},{3,7},{4,0},{5,1},{6,2},{7,3},{8,12},{9,13},{10,... | collective-permute-start | bytes 393224 | tf_op jit(solution)/shard_map/ppermute | solution.py:350
  7.4 1.3 %collective-permute-start.2 = (bf16[128,512]{1,0:T(8,128)(2,1)S(1)}, bf16[128,512]{1,0:T(8,128)(2,1)S(1)}, u32[]{:S(2)}, u32[]{:S(2)}) collective-permute-start(bf16[128,512]{1,0:T(8,128)(2,1)S(1)} %pad_maximum_fusion.1.refs_0_), channel_id=1, source_target_pairs={{0,6},{1,7},{2,0},{3,1},{4,2},{5,3},{6,4},{7,5},{8,14},{9,15},{10,... | collective-permute-start | bytes 393224 | tf_op jit(solution)/shard_map/ppermute | solution.py:350
  10.2 1.5 %collective-permute-start.14 = (bf16[512,256]{1,0:T(8,128)(2,1)}, bf16[512,256]{1,0:T(8,128)(2,1)}, u32[]{:S(2)}, u32[]{:S(2)}) collective-permute-start(bf16[512,256]{1,0:T(8,128)(2,1)} %dynamic-slice_bitcast_fusion), channel_id=1, source_target_pairs={{0,8},{8,0},{16,24},{24,16},{1,9},{9,1},{17,25},{25,17},{2,10},{10... | collective-permute-start | bytes 786440 | tf_op jit(solution)/shard_map/ppermute | solution.py:359
  11.7 1.3 %split_input.1 = bf16[4,128,1024]{2,1,0:T(8,128)(2,1)} custom-call(bf16[128,4096]{1,0:T(8,128)(2,1)S(1)} %bitcast.44), custom_call_target="tpu_custom_call" | custom-call | tf_op jit(solution)/shard_map/split_input/pallas_call | solution.py:327
  13.0 3.6 %all-to-all-start = ((bf16[4,128,1024]{2,1,0:T(8,128)(2,1)}), bf16[4,128,1024]{2,1,0:T(8,128)(2,1)S(1)}, u32[]{:S(2)}, u32[]{:S(2)}) async-start(bf16[4,128,1024]{2,1,0:T(8,128)(2,1)} %split_input.1), calls=%async_computation | async-start | bytes 2097152 | tf_op jit(solution)/shard_map/all_to_all | solution.py:394
  20.3 1.1 %broadcast_select_fusion = bf16[512,256]{1,0:T(8,128)(2,1)S(1)} fusion(bf16[512,256]{1,0:T(8,128)(2,1)} %collective-permute-done.14, pred[512]{0:T(512)(128)(4,1)S(1)} %broadcast_bitcast_fusion, bf16[1,1024,256]{2,1,0:T(8,128)(2,1)S(1)} %copy-done.3, s32[]{:T(128)S(6)} %select_n.65), kind=kLoop, calls=%fused_computation.2 | loop fusion | flops 131072 | bytes 786948 | tf_op jit(solution)/shard_map/jit(_where)/select_n | solution.py:388
  21.4 1.9 %collective-permute-start.8 = (bf16[128,512]{1,0:T(8,128)(2,1)S(1)}, bf16[128,512]{1,0:T(8,128)(2,1)S(1)}, u32[]{:S(2)}, u32[]{:S(2)}) collective-permute-start(bf16[128,512]{1,0:T(8,128)(2,1)S(1)} %pad_maximum_fusion.refs_0_), channel_id=1, source_target_pairs={{0,4},{1,5},{2,6},{3,7},{4,0},{5,1},{6,2},{7,3},{8,12},{9,13},{10,... | collective-permute-start | bytes 393224 | tf_op jit(solution)/shard_map/ppermute | solution.py:350
  23.3 3.4 %collective-permute-start.9 = (bf16[128,512]{1,0:T(8,128)(2,1)S(1)}, bf16[128,512]{1,0:T(8,128)(2,1)S(1)}, u32[]{:S(2)}, u32[]{:S(2)}) collective-permute-start(bf16[128,512]{1,0:T(8,128)(2,1)S(1)} %pad_maximum_fusion.refs_0_), channel_id=1, source_target_pairs={{0,6},{1,7},{2,0},{3,1},{4,2},{5,3},{6,4},{7,5},{8,14},{9,15},{10,... | collective-permute-start | bytes 393224 | tf_op jit(solution)/shard_map/ppermute | solution.py:350
  26.8 1.5 %collective-permute-start.15 = (bf16[512,256]{1,0:T(8,128)(2,1)S(1)}, bf16[512,256]{1,0:T(8,128)(2,1)S(1)}, u32[]{:S(2)}, u32[]{:S(2)}) collective-permute-start(bf16[512,256]{1,0:T(8,128)(2,1)S(1)} %broadcast_select_fusion), channel_id=1, source_target_pairs={{0,16},{8,24},{16,0},{24,8},{1,17},{9,25},{17,1},{25,9},{2,18},{10... | collective-permute-start | bytes 786440 | tf_op jit(solution)/shard_map/ppermute | solution.py:359
  28.3 1.2 %copy-done.2 = bf16[1,128,4096]{2,1,0:T(8,128)(2,1)S(1)} copy-done((bf16[1,128,4096]{2,1,0:T(8,128)(2,1)S(1)}, bf16[1,128,4096]{2,1,0:T(8,128)(2,1)}, u32[]{:S(2)}) %copy-start.2) | copy-done | bytes 1048600
  29.5 3.6 %attention_backward.2 = (bf16[128,2048]{1,0:T(8,128)(2,1)S(1)}, bf16[1024,512]{1,0:T(8,128)(2,1)S(1)}) custom-call(s32[160]{0:T(256)S(1)} %reshape.102.table_ref, bf16[128,4096]{1,0:T(8,128)(2,1)S(1)} %bitcast.45, bf16[128,4096]{1,0:T(8,128)(2,1)S(1)} %bitcast.47, bf16[128,512]{1,0:T(8,128)(2,1)S(1)} %pad_maximum_fusion.1.refs_0_, ...), custom_call_target="tpu_custom_call" | custom-call | flops 10066329600 | bytes 4194304 | tf_op jit(solution)/shard_map/attention_backward/pallas_call | solution.py:154
  35.4 3.8 %attention_backward.3 = (bf16[128,2048]{1,0:T(8,128)(2,1)S(1)}, bf16[1024,512]{1,0:T(8,128)(2,1)S(1)}) custom-call(s32[160]{0:T(256)S(1)} %reshape.102.table_ref, bf16[128,4096]{1,0:T(8,128)(2,1)S(1)} %bitcast.46, bf16[128,4096]{1,0:T(8,128)(2,1)S(1)} %bitcast.48, bf16[128,512]{1,0:T(8,128)(2,1)S(1)} %pad_maximum_fusion.refs_0_, ...), custom_call_target="tpu_custom_call" | custom-call | flops 10066329600 | bytes 4194304 | tf_op jit(solution)/shard_map/attention_backward/pallas_call | solution.py:154
  39.7 1.3 %collective-permute-start.17 = (bf16[512,256]{1,0:T(8,128)(2,1)S(1)}, bf16[512,256]{1,0:T(8,128)(2,1)S(1)}, u32[]{:S(2)}, u32[]{:S(2)}) collective-permute-start(bf16[512,256]{1,0:T(8,128)(2,1)S(1)} %project.3), channel_id=1, source_target_pairs={{0,1},{1,0},{2,3},{3,2},{4,5},{5,4},{6,7},{7,6},{8,9},{9,8},{10,11... | collective-permute-start | bytes 786440 | tf_op jit(solution)/shard_map/ppermute | solution.py:346
  42.2 2.3 %collective-permute-start.18 = (bf16[128,256]{1,0:T(8,128)(2,1)S(1)}, bf16[128,256]{1,0:T(8,128)(2,1)S(1)}, u32[]{:S(2)}, u32[]{:S(2)}) collective-permute-start(bf16[128,256]{1,0:T(8,128)(2,1)S(1)} %get-tuple-element.39), channel_id=1, source_target_pairs={{0,4},{1,5},{2,6},{3,7},{4,0},{5,1},{6,2},{7,3},{8,12},{9,13},{10,... | collective-permute-start | bytes 196616 | tf_op jit(solution)/shard_map/ppermute | solution.py:350
  44.5 1.6 %collective-permute-start.19 = (bf16[128,256]{1,0:T(8,128)(2,1)S(1)}, bf16[128,256]{1,0:T(8,128)(2,1)S(1)}, u32[]{:S(2)}, u32[]{:S(2)}) collective-permute-start(bf16[128,256]{1,0:T(8,128)(2,1)S(1)} %get-tuple-element.40), channel_id=1, source_target_pairs={{0,6},{1,7},{2,0},{3,1},{4,2},{5,3},{6,4},{7,5},{8,14},{9,15},{10,... | collective-permute-start | bytes 196616 | tf_op jit(solution)/shard_map/ppermute | solution.py:350
  46.6 2.2 %collective-permute-done.18 = bf16[128,256]{1,0:T(8,128)(2,1)S(1)} collective-permute-done((bf16[128,256]{1,0:T(8,128)(2,1)S(1)}, bf16[128,256]{1,0:T(8,128)(2,1)S(1)}, u32[]{:S(2)}, u32[]{:S(2)}) %collective-permute-start.18) | collective-permute-done | bytes 65568 | tf_op jit(solution)/shard_map/ppermute | solution.py:350
  49.1 3.1 %collective-permute-done.20 = bf16[128,256]{1,0:T(8,128)(2,1)S(1)} collective-permute-done((bf16[128,256]{1,0:T(8,128)(2,1)S(1)}, bf16[128,256]{1,0:T(8,128)(2,1)S(1)}, u32[]{:S(2)}, u32[]{:S(2)}) %collective-permute-start.20) | collective-permute-done | bytes 65568 | tf_op jit(solution)/shard_map/ppermute | solution.py:350
  52.2 2.0 %collective-permute-start.21 = (bf16[128,256]{1,0:T(8,128)(2,1)S(1)}, bf16[128,256]{1,0:T(8,128)(2,1)S(1)}, u32[]{:S(2)}, u32[]{:S(2)}) collective-permute-start(bf16[128,256]{1,0:T(8,128)(2,1)S(1)} %add_convert_fusion.1.refs_0_), channel_id=1, source_target_pairs={{0,8},{8,0},{16,24},{24,16},{1,9},{9,1},{17,25},{25,17},{2,10},{10... | collective-permute-start | bytes 196616 | tf_op jit(solution)/shard_map/ppermute | solution.py:359
  56.6 2.1 %collective-permute-done.22.refs_2_ = bf16[128,256]{1,0:T(8,128)(2,1)S(1)} collective-permute-done((bf16[128,256]{1,0:T(8,128)(2,1)S(1)}, bf16[128,256]{1,0:T(8,128)(2,1)S(1)}, u32[]{:S(2)}, u32[]{:S(2)}) %collective-permute-start.22) | collective-permute-done | bytes 65568 | tf_op jit(solution)/shard_map/ppermute | solution.py:359
  58.7 1.6 %collective-permute-done.23.refs_3_ = bf16[128,256]{1,0:T(8,128)(2,1)S(1)} collective-permute-done((bf16[128,256]{1,0:T(8,128)(2,1)S(1)}, bf16[128,256]{1,0:T(8,128)(2,1)S(1)}, u32[]{:S(2)}, u32[]{:S(2)}) %collective-permute-start.23) | collective-permute-done | bytes 65568 | tf_op jit(solution)/shard_map/ppermute | solution.py:359
  60.8 1.5 %collective-permute-done.24.came_ref = bf16[512,256]{1,0:T(8,128)(2,1)S(1)} collective-permute-done((bf16[512,256]{1,0:T(8,128)(2,1)S(1)}, bf16[512,256]{1,0:T(8,128)(2,1)S(1)}, u32[]{:S(2)}, u32[]{:S(2)}) %collective-permute-start.24) | collective-permute-done | bytes 262176 | tf_op jit(solution)/shard_map/ppermute | solution.py:346
  62.5 1.1 %collective-permute-start.25 = (bf16[128,256]{1,0:T(8,128)(2,1)S(1)}, bf16[128,256]{1,0:T(8,128)(2,1)S(1)}, u32[]{:S(2)}, u32[]{:S(2)}) collective-permute-start(bf16[128,256]{1,0:T(8,128)(2,1)S(1)} %get-tuple-element.45), channel_id=1, source_target_pairs={{0,4},{1,5},{2,6},{3,7},{4,0},{5,1},{6,2},{7,3},{8,12},{9,13},{10,... | collective-permute-start | bytes 196616 | tf_op jit(solution)/shard_map/ppermute | solution.py:350
  63.6 1.5 %collective-permute-start.26 = (bf16[128,256]{1,0:T(8,128)(2,1)S(1)}, bf16[128,256]{1,0:T(8,128)(2,1)S(1)}, u32[]{:S(2)}, u32[]{:S(2)}) collective-permute-start(bf16[128,256]{1,0:T(8,128)(2,1)S(1)} %get-tuple-element.46), channel_id=1, source_target_pairs={{0,2},{1,3},{2,4},{3,5},{4,6},{5,7},{6,0},{7,1},{8,10},{9,11},{10,... | collective-permute-start | bytes 196616 | tf_op jit(solution)/shard_map/ppermute | solution.py:350
  65.0 2.4 %collective-permute-start.27 = (bf16[128,256]{1,0:T(8,128)(2,1)S(1)}, bf16[128,256]{1,0:T(8,128)(2,1)S(1)}, u32[]{:S(2)}, u32[]{:S(2)}) collective-permute-start(bf16[128,256]{1,0:T(8,128)(2,1)S(1)} %get-tuple-element.47), channel_id=1, source_target_pairs={{0,6},{1,7},{2,0},{3,1},{4,2},{5,3},{6,4},{7,5},{8,14},{9,15},{10,... | collective-permute-start | bytes 196616 | tf_op jit(solution)/shard_map/ppermute | solution.py:350
  67.4 1.9 %collective-permute-done.25 = bf16[128,256]{1,0:T(8,128)(2,1)S(1)} collective-permute-done((bf16[128,256]{1,0:T(8,128)(2,1)S(1)}, bf16[128,256]{1,0:T(8,128)(2,1)S(1)}, u32[]{:S(2)}, u32[]{:S(2)}) %collective-permute-start.25) | collective-permute-done | bytes 65568 | tf_op jit(solution)/shard_map/ppermute | solution.py:350
  70.0 1.1 %collective-permute-done.27 = bf16[128,256]{1,0:T(8,128)(2,1)S(1)} collective-permute-done((bf16[128,256]{1,0:T(8,128)(2,1)S(1)}, bf16[128,256]{1,0:T(8,128)(2,1)S(1)}, u32[]{:S(2)}, u32[]{:S(2)}) %collective-permute-start.27) | collective-permute-done | bytes 65568 | tf_op jit(solution)/shard_map/ppermute | solution.py:350
  71.7 0.9 %collective-permute-start.29 = (bf16[128,256]{1,0:T(8,128)(2,1)S(1)}, bf16[128,256]{1,0:T(8,128)(2,1)S(1)}, u32[]{:S(2)}, u32[]{:S(2)}) collective-permute-start(bf16[128,256]{1,0:T(8,128)(2,1)S(1)} %add_convert_fusion.refs_0_), channel_id=1, source_target_pairs={{0,16},{8,24},{16,0},{24,8},{1,17},{9,25},{17,1},{25,9},{2,18},{10... | collective-permute-start | bytes 196616 | tf_op jit(solution)/shard_map/ppermute | solution.py:359
  72.7 2.0 %collective-permute-start.30 = (bf16[128,256]{1,0:T(8,128)(2,1)S(1)}, bf16[128,256]{1,0:T(8,128)(2,1)S(1)}, u32[]{:S(2)}, u32[]{:S(2)}) collective-permute-start(bf16[128,256]{1,0:T(8,128)(2,1)S(1)} %add_convert_fusion.refs_0_), channel_id=1, source_target_pairs={{0,24},{8,16},{16,8},{24,0},{1,25},{9,17},{17,9},{25,1},{2,26},{10... | collective-permute-start | bytes 196616 | tf_op jit(solution)/shard_map/ppermute | solution.py:359
  74.7 1.0 %maximum_bitcast_fusion = bf16[1,128,4096]{2,1,0:T(8,128)(2,1)} fusion(bf16[128,2048]{1,0:T(8,128)(2,1)S(1)} %get-tuple-element.35, bf16[128,2048]{1,0:T(8,128)(2,1)S(1)} %get-tuple-element.29), kind=kLoop, calls=%fused_computation | loop fusion | flops 2097152 | bytes 2097152 | tf_op jit(solution)/shard_map/broadcast_in_dim | solution.py:426
  76.1 1.8 %collective-permute-done.30.refs_3_ = bf16[128,256]{1,0:T(8,128)(2,1)S(1)} collective-permute-done((bf16[128,256]{1,0:T(8,128)(2,1)S(1)}, bf16[128,256]{1,0:T(8,128)(2,1)S(1)}, u32[]{:S(2)}, u32[]{:S(2)}) %collective-permute-start.30) | collective-permute-done | bytes 65568 | tf_op jit(solution)/shard_map/ppermute | solution.py:359
  (78 shorter events, 15.3 us)
Async XLA Ops:
  1.7 17.4 %collective-permute-start = (bf16[128,512]{1,0:T(8,128)(2,1)S(1)}, bf16[128,512]{1,0:T(8,128)(2,1)S(1)}, u32[]{:S(2)}, u32[]{:S(2)}) collective-permute-start(bf16[128,512]{1,0:T(8,128)(2,1)S(1)} %pad_maximum_fusion.1.refs_0_), channel_id=1, source_target_pairs={{0,2},{1,3},{2,4},{3,5},{4,6},{5,7},{6,0},{7,1},{8,10},{9,11},{10,... | collective-permute-start | bytes 393224 | tf_op jit(solution)/shard_map/ppermute | solution.py:350
  4.8 14.4 %collective-permute-start.1 = (bf16[128,512]{1,0:T(8,128)(2,1)S(1)}, bf16[128,512]{1,0:T(8,128)(2,1)S(1)}, u32[]{:S(2)}, u32[]{:S(2)}) collective-permute-start(bf16[128,512]{1,0:T(8,128)(2,1)S(1)} %pad_maximum_fusion.1.refs_0_), channel_id=1, source_target_pairs={{0,4},{1,5},{2,6},{3,7},{4,0},{5,1},{6,2},{7,3},{8,12},{9,13},{10,... | collective-permute-start | bytes 393224 | tf_op jit(solution)/shard_map/ppermute | solution.py:350
  7.4 11.8 %collective-permute-start.2 = (bf16[128,512]{1,0:T(8,128)(2,1)S(1)}, bf16[128,512]{1,0:T(8,128)(2,1)S(1)}, u32[]{:S(2)}, u32[]{:S(2)}) collective-permute-start(bf16[128,512]{1,0:T(8,128)(2,1)S(1)} %pad_maximum_fusion.1.refs_0_), channel_id=1, source_target_pairs={{0,6},{1,7},{2,0},{3,1},{4,2},{5,3},{6,4},{7,5},{8,14},{9,15},{10,... | collective-permute-start | bytes 393224 | tf_op jit(solution)/shard_map/ppermute | solution.py:350
  8.8 24.4 %collective-permute-start.7 = (bf16[128,512]{1,0:T(8,128)(2,1)S(1)}, bf16[128,512]{1,0:T(8,128)(2,1)S(1)}, u32[]{:S(2)}, u32[]{:S(2)}) collective-permute-start(bf16[128,512]{1,0:T(8,128)(2,1)S(1)} %pad_maximum_fusion.refs_0_), channel_id=1, source_target_pairs={{0,2},{1,3},{2,4},{3,5},{4,6},{5,7},{6,0},{7,1},{8,10},{9,11},{10,... | collective-permute-start | bytes 393224 | tf_op jit(solution)/shard_map/ppermute | solution.py:350
  10.2 9.6 %collective-permute-start.14 = (bf16[512,256]{1,0:T(8,128)(2,1)}, bf16[512,256]{1,0:T(8,128)(2,1)}, u32[]{:S(2)}, u32[]{:S(2)}) collective-permute-start(bf16[512,256]{1,0:T(8,128)(2,1)} %dynamic-slice_bitcast_fusion), channel_id=1, source_target_pairs={{0,8},{8,0},{16,24},{24,16},{1,9},{9,1},{17,25},{25,17},{2,10},{10... | collective-permute-start | bytes 786440 | tf_op jit(solution)/shard_map/ppermute | solution.py:359
  13.0 42.8 %all-to-all-start = ((bf16[4,128,1024]{2,1,0:T(8,128)(2,1)}), bf16[4,128,1024]{2,1,0:T(8,128)(2,1)S(1)}, u32[]{:S(2)}, u32[]{:S(2)}) async-start(bf16[4,128,1024]{2,1,0:T(8,128)(2,1)} %split_input.1), calls=%async_computation | async-start | bytes 2097152 | tf_op jit(solution)/shard_map/all_to_all | solution.py:394
  19.2 2.2 %collective-permute-start.3 = (bf16[128,512]{1,0:T(8,128)(2,1)S(1)}, bf16[128,512]{1,0:T(8,128)(2,1)S(1)}, u32[]{:S(2)}, u32[]{:S(2)}) collective-permute-start(bf16[128,512]{1,0:T(8,128)(2,1)S(1)} %pad_maximum_fusion.1.refs_0_), channel_id=1, source_target_pairs={{0,1},{1,0},{2,3},{3,2},{4,5},{5,4},{6,7},{7,6},{8,9},{9,8},{10,11... | collective-permute-start | bytes 393224 | tf_op jit(solution)/shard_map/ppermute | solution.py:346
  19.3 4.0 %collective-permute-start.4 = (bf16[128,512]{1,0:T(8,128)(2,1)S(1)}, bf16[128,512]{1,0:T(8,128)(2,1)S(1)}, u32[]{:S(2)}, u32[]{:S(2)}) collective-permute-start(bf16[128,512]{1,0:T(8,128)(2,1)S(1)} %collective-permute-done.refs_1_), channel_id=1, source_target_pairs={{0,1},{1,0},{2,3},{3,2},{4,5},{5,4},{6,7},{7,6},{8,9},{9,8},{10,11... | collective-permute-start | bytes 393224 | tf_op jit(solution)/shard_map/ppermute | solution.py:346
  19.8 3.6 %collective-permute-start.5 = (bf16[128,512]{1,0:T(8,128)(2,1)S(1)}, bf16[128,512]{1,0:T(8,128)(2,1)S(1)}, u32[]{:S(2)}, u32[]{:S(2)}) collective-permute-start(bf16[128,512]{1,0:T(8,128)(2,1)S(1)} %collective-permute-done.1.refs_2_), channel_id=1, source_target_pairs={{0,1},{1,0},{2,3},{3,2},{4,5},{5,4},{6,7},{7,6},{8,9},{9,8},{10,11... | collective-permute-start | bytes 393224 | tf_op jit(solution)/shard_map/ppermute | solution.py:346
  19.8 6.9 %collective-permute-start.6 = (bf16[128,512]{1,0:T(8,128)(2,1)S(1)}, bf16[128,512]{1,0:T(8,128)(2,1)S(1)}, u32[]{:S(2)}, u32[]{:S(2)}) collective-permute-start(bf16[128,512]{1,0:T(8,128)(2,1)S(1)} %collective-permute-done.2.refs_3_), channel_id=1, source_target_pairs={{0,1},{1,0},{2,3},{3,2},{4,5},{5,4},{6,7},{7,6},{8,9},{9,8},{10,11... | collective-permute-start | bytes 393224 | tf_op jit(solution)/shard_map/ppermute | solution.py:346
  21.4 11.8 %collective-permute-start.8 = (bf16[128,512]{1,0:T(8,128)(2,1)S(1)}, bf16[128,512]{1,0:T(8,128)(2,1)S(1)}, u32[]{:S(2)}, u32[]{:S(2)}) collective-permute-start(bf16[128,512]{1,0:T(8,128)(2,1)S(1)} %pad_maximum_fusion.refs_0_), channel_id=1, source_target_pairs={{0,4},{1,5},{2,6},{3,7},{4,0},{5,1},{6,2},{7,3},{8,12},{9,13},{10,... | collective-permute-start | bytes 393224 | tf_op jit(solution)/shard_map/ppermute | solution.py:350
  23.3 12.1 %collective-permute-start.10 = (bf16[128,512]{1,0:T(8,128)(2,1)S(1)}, bf16[128,512]{1,0:T(8,128)(2,1)S(1)}, u32[]{:S(2)}, u32[]{:S(2)}) collective-permute-start(bf16[128,512]{1,0:T(8,128)(2,1)S(1)} %pad_maximum_fusion.refs_0_), channel_id=1, source_target_pairs={{0,1},{1,0},{2,3},{3,2},{4,5},{5,4},{6,7},{7,6},{8,9},{9,8},{10,11... | collective-permute-start | bytes 393224 | tf_op jit(solution)/shard_map/ppermute | solution.py:346
  23.3 9.8 %collective-permute-start.9 = (bf16[128,512]{1,0:T(8,128)(2,1)S(1)}, bf16[128,512]{1,0:T(8,128)(2,1)S(1)}, u32[]{:S(2)}, u32[]{:S(2)}) collective-permute-start(bf16[128,512]{1,0:T(8,128)(2,1)S(1)} %pad_maximum_fusion.refs_0_), channel_id=1, source_target_pairs={{0,6},{1,7},{2,0},{3,1},{4,2},{5,3},{6,4},{7,5},{8,14},{9,15},{10,... | collective-permute-start | bytes 393224 | tf_op jit(solution)/shard_map/ppermute | solution.py:350
  26.8 8.4 %collective-permute-start.15 = (bf16[512,256]{1,0:T(8,128)(2,1)S(1)}, bf16[512,256]{1,0:T(8,128)(2,1)S(1)}, u32[]{:S(2)}, u32[]{:S(2)}) collective-permute-start(bf16[512,256]{1,0:T(8,128)(2,1)S(1)} %broadcast_select_fusion), channel_id=1, source_target_pairs={{0,16},{8,24},{16,0},{24,8},{1,17},{9,25},{17,1},{25,9},{2,18},{10... | collective-permute-start | bytes 786440 | tf_op jit(solution)/shard_map/ppermute | solution.py:359
  33.2 2.2 %collective-permute-start.11 = (bf16[128,512]{1,0:T(8,128)(2,1)S(1)}, bf16[128,512]{1,0:T(8,128)(2,1)S(1)}, u32[]{:S(2)}, u32[]{:S(2)}) collective-permute-start(bf16[128,512]{1,0:T(8,128)(2,1)S(1)} %collective-permute-done.7.refs_1_), channel_id=1, source_target_pairs={{0,1},{1,0},{2,3},{3,2},{4,5},{5,4},{6,7},{7,6},{8,9},{9,8},{10,11... | collective-permute-start | bytes 393224 | tf_op jit(solution)/shard_map/ppermute | solution.py:346
  33.8 1.6 %collective-permute-start.12 = (bf16[128,512]{1,0:T(8,128)(2,1)S(1)}, bf16[128,512]{1,0:T(8,128)(2,1)S(1)}, u32[]{:S(2)}, u32[]{:S(2)}) collective-permute-start(bf16[128,512]{1,0:T(8,128)(2,1)S(1)} %collective-permute-done.8.refs_2_), channel_id=1, source_target_pairs={{0,1},{1,0},{2,3},{3,2},{4,5},{5,4},{6,7},{7,6},{8,9},{9,8},{10,11... | collective-permute-start | bytes 393224 | tf_op jit(solution)/shard_map/ppermute | solution.py:346
  33.9 1.5 %collective-permute-start.13 = (bf16[128,512]{1,0:T(8,128)(2,1)S(1)}, bf16[128,512]{1,0:T(8,128)(2,1)S(1)}, u32[]{:S(2)}, u32[]{:S(2)}) collective-permute-start(bf16[128,512]{1,0:T(8,128)(2,1)S(1)} %collective-permute-done.9.refs_3_), channel_id=1, source_target_pairs={{0,1},{1,0},{2,3},{3,2},{4,5},{5,4},{6,7},{7,6},{8,9},{9,8},{10,11... | collective-permute-start | bytes 393224 | tf_op jit(solution)/shard_map/ppermute | solution.py:346
  35.3 3.9 %collective-permute-start.16 = (bf16[512,256]{1,0:T(8,128)(2,1)S(1)}, bf16[512,256]{1,0:T(8,128)(2,1)S(1)}, u32[]{:S(2)}, u32[]{:S(2)}) collective-permute-start(bf16[512,256]{1,0:T(8,128)(2,1)S(1)} %broadcast_select_fusion.1.mine_ref), channel_id=1, source_target_pairs={{0,1},{1,0},{2,3},{3,2},{4,5},{5,4},{6,7},{7,6},{8,9},{9,8},{10,11... | collective-permute-start | bytes 786440 | tf_op jit(solution)/shard_map/ppermute | solution.py:346
  39.7 2.4 %collective-permute-start.17 = (bf16[512,256]{1,0:T(8,128)(2,1)S(1)}, bf16[512,256]{1,0:T(8,128)(2,1)S(1)}, u32[]{:S(2)}, u32[]{:S(2)}) collective-permute-start(bf16[512,256]{1,0:T(8,128)(2,1)S(1)} %project.3), channel_id=1, source_target_pairs={{0,1},{1,0},{2,3},{3,2},{4,5},{5,4},{6,7},{7,6},{8,9},{9,8},{10,11... | collective-permute-start | bytes 786440 | tf_op jit(solution)/shard_map/ppermute | solution.py:346
  42.2 6.6 %collective-permute-start.18 = (bf16[128,256]{1,0:T(8,128)(2,1)S(1)}, bf16[128,256]{1,0:T(8,128)(2,1)S(1)}, u32[]{:S(2)}, u32[]{:S(2)}) collective-permute-start(bf16[128,256]{1,0:T(8,128)(2,1)S(1)} %get-tuple-element.39), channel_id=1, source_target_pairs={{0,4},{1,5},{2,6},{3,7},{4,0},{5,1},{6,2},{7,3},{8,12},{9,13},{10,... | collective-permute-start | bytes 196616 | tf_op jit(solution)/shard_map/ppermute | solution.py:350
  44.5 4.6 %collective-permute-start.19 = (bf16[128,256]{1,0:T(8,128)(2,1)S(1)}, bf16[128,256]{1,0:T(8,128)(2,1)S(1)}, u32[]{:S(2)}, u32[]{:S(2)}) collective-permute-start(bf16[128,256]{1,0:T(8,128)(2,1)S(1)} %get-tuple-element.40), channel_id=1, source_target_pairs={{0,6},{1,7},{2,0},{3,1},{4,2},{5,3},{6,4},{7,5},{8,14},{9,15},{10,... | collective-permute-start | bytes 196616 | tf_op jit(solution)/shard_map/ppermute | solution.py:350
  46.1 6.1 %collective-permute-start.20 = (bf16[128,256]{1,0:T(8,128)(2,1)S(1)}, bf16[128,256]{1,0:T(8,128)(2,1)S(1)}, u32[]{:S(2)}, u32[]{:S(2)}) collective-permute-start(bf16[128,256]{1,0:T(8,128)(2,1)S(1)} %get-tuple-element.41), channel_id=1, source_target_pairs={{0,2},{1,3},{2,4},{3,5},{4,6},{5,7},{6,0},{7,1},{8,10},{9,11},{10,... | collective-permute-start | bytes 196616 | tf_op jit(solution)/shard_map/ppermute | solution.py:350
  52.2 4.3 %collective-permute-start.21 = (bf16[128,256]{1,0:T(8,128)(2,1)S(1)}, bf16[128,256]{1,0:T(8,128)(2,1)S(1)}, u32[]{:S(2)}, u32[]{:S(2)}) collective-permute-start(bf16[128,256]{1,0:T(8,128)(2,1)S(1)} %add_convert_fusion.1.refs_0_), channel_id=1, source_target_pairs={{0,8},{8,0},{16,24},{24,16},{1,9},{9,1},{17,25},{25,17},{2,10},{10... | collective-permute-start | bytes 196616 | tf_op jit(solution)/shard_map/ppermute | solution.py:359
  54.3 4.4 %collective-permute-start.22 = (bf16[128,256]{1,0:T(8,128)(2,1)S(1)}, bf16[128,256]{1,0:T(8,128)(2,1)S(1)}, u32[]{:S(2)}, u32[]{:S(2)}) collective-permute-start(bf16[128,256]{1,0:T(8,128)(2,1)S(1)} %add_convert_fusion.1.refs_0_), channel_id=1, source_target_pairs={{0,16},{8,24},{16,0},{24,8},{1,17},{9,25},{17,1},{25,9},{2,18},{10... | collective-permute-start | bytes 196616 | tf_op jit(solution)/shard_map/ppermute | solution.py:359
  55.1 5.2 %collective-permute-start.23 = (bf16[128,256]{1,0:T(8,128)(2,1)S(1)}, bf16[128,256]{1,0:T(8,128)(2,1)S(1)}, u32[]{:S(2)}, u32[]{:S(2)}) collective-permute-start(bf16[128,256]{1,0:T(8,128)(2,1)S(1)} %add_convert_fusion.1.refs_0_), channel_id=1, source_target_pairs={{0,24},{8,16},{16,8},{24,0},{1,25},{9,17},{17,9},{25,1},{2,26},{10... | collective-permute-start | bytes 196616 | tf_op jit(solution)/shard_map/ppermute | solution.py:359
  60.8 1.6 %collective-permute-start.24 = (bf16[512,256]{1,0:T(8,128)(2,1)S(1)}, bf16[512,256]{1,0:T(8,128)(2,1)S(1)}, u32[]{:S(2)}, u32[]{:S(2)}) collective-permute-start(bf16[512,256]{1,0:T(8,128)(2,1)S(1)} %get-tuple-element.43), channel_id=1, source_target_pairs={{0,1},{1,0},{2,3},{3,2},{4,5},{5,4},{6,7},{7,6},{8,9},{9,8},{10,11... | collective-permute-start | bytes 786440 | tf_op jit(solution)/shard_map/ppermute | solution.py:346
  62.5 6.8 %collective-permute-start.25 = (bf16[128,256]{1,0:T(8,128)(2,1)S(1)}, bf16[128,256]{1,0:T(8,128)(2,1)S(1)}, u32[]{:S(2)}, u32[]{:S(2)}) collective-permute-start(bf16[128,256]{1,0:T(8,128)(2,1)S(1)} %get-tuple-element.45), channel_id=1, source_target_pairs={{0,4},{1,5},{2,6},{3,7},{4,0},{5,1},{6,2},{7,3},{8,12},{9,13},{10,... | collective-permute-start | bytes 196616 | tf_op jit(solution)/shard_map/ppermute | solution.py:350
  63.6 6.4 %collective-permute-start.26 = (bf16[128,256]{1,0:T(8,128)(2,1)S(1)}, bf16[128,256]{1,0:T(8,128)(2,1)S(1)}, u32[]{:S(2)}, u32[]{:S(2)}) collective-permute-start(bf16[128,256]{1,0:T(8,128)(2,1)S(1)} %get-tuple-element.46), channel_id=1, source_target_pairs={{0,2},{1,3},{2,4},{3,5},{4,6},{5,7},{6,0},{7,1},{8,10},{9,11},{10,... | collective-permute-start | bytes 196616 | tf_op jit(solution)/shard_map/ppermute | solution.py:350
  65.0 6.0 %collective-permute-start.27 = (bf16[128,256]{1,0:T(8,128)(2,1)S(1)}, bf16[128,256]{1,0:T(8,128)(2,1)S(1)}, u32[]{:S(2)}, u32[]{:S(2)}) collective-permute-start(bf16[128,256]{1,0:T(8,128)(2,1)S(1)} %get-tuple-element.47), channel_id=1, source_target_pairs={{0,6},{1,7},{2,0},{3,1},{4,2},{5,3},{6,4},{7,5},{8,14},{9,15},{10,... | collective-permute-start | bytes 196616 | tf_op jit(solution)/shard_map/ppermute | solution.py:350
  71.1 4.6 %collective-permute-start.28 = (bf16[128,256]{1,0:T(8,128)(2,1)S(1)}, bf16[128,256]{1,0:T(8,128)(2,1)S(1)}, u32[]{:S(2)}, u32[]{:S(2)}) collective-permute-start(bf16[128,256]{1,0:T(8,128)(2,1)S(1)} %add_convert_fusion.refs_0_), channel_id=1, source_target_pairs={{0,8},{8,0},{16,24},{24,16},{1,9},{9,1},{17,25},{25,17},{2,10},{10... | collective-permute-start | bytes 196616 | tf_op jit(solution)/shard_map/ppermute | solution.py:359
  71.7 4.4 %collective-permute-start.29 = (bf16[128,256]{1,0:T(8,128)(2,1)S(1)}, bf16[128,256]{1,0:T(8,128)(2,1)S(1)}, u32[]{:S(2)}, u32[]{:S(2)}) collective-permute-start(bf16[128,256]{1,0:T(8,128)(2,1)S(1)} %add_convert_fusion.refs_0_), channel_id=1, source_target_pairs={{0,16},{8,24},{16,0},{24,8},{1,17},{9,25},{17,1},{25,9},{2,18},{10... | collective-permute-start | bytes 196616 | tf_op jit(solution)/shard_map/ppermute | solution.py:359
  72.7 5.2 %collective-permute-start.30 = (bf16[128,256]{1,0:T(8,128)(2,1)S(1)}, bf16[128,256]{1,0:T(8,128)(2,1)S(1)}, u32[]{:S(2)}, u32[]{:S(2)}) collective-permute-start(bf16[128,256]{1,0:T(8,128)(2,1)S(1)} %add_convert_fusion.refs_0_), channel_id=1, source_target_pairs={{0,24},{8,16},{16,8},{24,0},{1,25},{9,17},{17,9},{25,1},{2,26},{10... | collective-permute-start | bytes 196616 | tf_op jit(solution)/shard_map/ppermute | solution.py:359
  (5 other events, 42.1 us)
